TPU v7x, 32 devices: a whole 2x2x4 slice. The times are simulated.
32 devices in a mesh: wide: 8 (over y, x, core), narrow: 4 (over z).
Axes of the slice: x: 2, y: 2, z: 4, core: 2. Of those that a mesh axis runs over, the one named last changes fastest.
Arguments:
- node_feats: bfloat16 [8192, 1024], P('wide'), may hold values from -6 to 6
- neigh_weight: bfloat16 [1024, 1024], P(None, 'narrow'), may hold values from -0.1875 to 0.1875
- neigh_bias: bfloat16 [1024], P('narrow'), may hold values from -3 to 3
- combine_weight: bfloat16 [2048, 1024], P(None, 'narrow')
- combine_bias: bfloat16 [1024], P('narrow'), may hold values from -3 to 3
- cotangent: bfloat16 [8192, 1024], P('wide', 'narrow'), may hold values from -6 to 6
- neighbour_slot: int32 [8192, 50], P('wide'), may hold values from 0 to 3071, as said below
- neighbour_mask: int32 [8192, 50], P('wide'), may hold values from 0 to 1, as said below
- visit_count: int32 [8192, 50], P('wide'), may hold values from 1 to 128, as said below
- send_rows: int32 [64, 256], P('wide'), may hold values from 0 to 1023, as said below
Outputs:
- embedding: bfloat16 [8192, 1024], P('wide', 'narrow')
- grad_features: float32 [8192, 1024], P('wide', 'narrow')
- grad_neigh_weight: float32 [1024, 1024], P(None, 'narrow')
- grad_neigh_bias: float32 [1024], P('narrow')
- grad_combine_weight: float32 [2048, 1024], P(None, 'narrow')
- grad_combine_bias: float32 [1024], P('narrow')
Inputs may be any that keep to these rules, and one draw needn't show every extreme that they name: `neighbour_slot`: an entry below 1024 is a row of the node's own device; an entry e of 1024 or more names slot (e - 1024) % 256 of the rows that owner (e - 1024) // 256 sends, never the node's own device. `neighbour_mask`: each row holds 5 to 50 ones followed by zeros. `visit_count`: powers of two. `send_rows`: row o * (devices along wide) + r lists, by index among owner o's 1024 nodes, the rows that requester r receives from o; the 256 entries of a row are distinct.
All inputs are finite; a program needn't handle non-finite values.
Results may differ from a plain program's by a relative error of at most 0.0095.
Values may be sent and summed in bfloat16 or wider, within the bound.
A program may use at most 128 MiB of HBM per device.

v0:
```python
import jax
import jax.numpy as jnp
from jax import lax
from jax.sharding import PartitionSpec as P

EPSILON = 1e-06


def contract_rows(left, right):
    return lax.dot_general(
        left, right, (((0,), (0,)), ((), ())), preferred_element_type=jnp.float32
    )


def contract_rows_exact(left, right):
    return lax.dot_general(
        left,
        right,
        (((0,), (0,)), ((), ())),
        precision=lax.Precision.HIGHEST,
        preferred_element_type=jnp.float32,
    )


def contract_cols(left, right):
    return lax.dot_general(
        left, right, (((1,), (1,)), ((), ())), preferred_element_type=jnp.float32
    )


def dense_weights(slot_block, weight_block, table_rows):
    positions = jnp.arange(table_rows, dtype=jnp.int32)
    hits = slot_block[:, :, None] == positions[None, None, :]
    return jnp.sum(jnp.where(hits, weight_block[:, :, None], 0.0), axis=1)


def pool_rows(msg_table, slot_ids, row_weights):
    row_count = slot_ids.shape[0]
    table_rows = msg_table.shape[0]
    step_rows = min(512, row_count)
    num_blocks = row_count // step_rows

    def pool_one_block(inputs):
        slot_block, weight_block = inputs
        mixing = dense_weights(slot_block, weight_block, table_rows)
        return jnp.dot(
            mixing, msg_table, precision=lax.Precision.HIGHEST, preferred_element_type=jnp.float32
        )

    pooled = lax.map(
        pool_one_block,
        (
            slot_ids.reshape(num_blocks, step_rows, -1),
            row_weights.reshape(num_blocks, step_rows, -1),
        ),
    )
    return pooled.reshape(row_count, msg_table.shape[1])


def spread_rows(grad_rows, slot_ids, row_weights, total_rows):
    row_count = slot_ids.shape[0]
    step_rows = min(512, row_count)
    num_blocks = row_count // step_rows
    columns = grad_rows.shape[1]

    def spread_one_block(running, inputs):
        slot_block, weight_block, grad_block = inputs
        mixing = dense_weights(slot_block, weight_block, total_rows)
        return (running + contract_rows_exact(mixing, grad_block.astype(jnp.float32)), None)

    initial = jnp.zeros((total_rows, columns), jnp.float32)
    result, _ = lax.scan(
        spread_one_block,
        initial,
        (
            slot_ids.reshape(num_blocks, step_rows, -1),
            row_weights.reshape(num_blocks, step_rows, -1),
            grad_rows.reshape(num_blocks, step_rows, columns),
        ),
    )
    return result


def shards(
    node_feats,
    neigh_weight,
    neigh_bias,
    combine_weight,
    combine_bias,
    cotangent,
    neighbour_slot,
    neighbour_mask,
    visit_count,
    send_rows,
):
    width = node_feats.shape[1]
    local_rows = node_feats.shape[0]
    owners = lax.axis_size("wide")
    capacity = send_rows.shape[1]
    masked = (visit_count * neighbour_mask).astype(jnp.float32)
    importance = masked / jnp.sum(masked, axis=1, keepdims=True)
    selector = (
        send_rows.reshape(-1)[:, None] == jnp.arange(local_rows, dtype=jnp.int32)[None, :]
    ).astype(jnp.float32)
    hidden = jnp.dot(
        node_feats, neigh_weight, preferred_element_type=jnp.float32
    ) + neigh_bias.astype(jnp.float32)
    message = jnp.maximum(hidden, 0.0)
    outgoing = jnp.dot(
        selector, message, precision=lax.Precision.HIGHEST, preferred_element_type=jnp.float32
    ).reshape(owners, capacity, -1)
    incoming = lax.all_to_all(outgoing, "wide", split_axis=0, concat_axis=0, tiled=True)
    msg_table = jnp.concatenate([message, incoming.reshape(owners * capacity, -1)], axis=0)
    pooled = pool_rows(msg_table, neighbour_slot, importance)
    pooled_full = lax.all_gather(pooled, "narrow", axis=1, tiled=True)
    self_rows = combine_weight[:width]
    pool_weight = combine_weight[width:]
    pool_exact = jnp.dot(
        pooled_full,
        pool_weight.astype(jnp.float32),
        precision=lax.Precision.HIGHEST,
        preferred_element_type=jnp.float32,
    )
    pre_act = (
        jnp.dot(node_feats, self_rows, preferred_element_type=jnp.float32)
        + pool_exact
        + combine_bias.astype(jnp.float32)
    )
    activated = jnp.maximum(pre_act, 0.0)
    squares = lax.psum(jnp.sum(activated * activated, axis=1), "narrow")
    inv_norm = lax.rsqrt(squares / width + EPSILON)
    embedding = (activated * inv_norm[:, None]).astype(jnp.bfloat16)
    upstream = cotangent.astype(jnp.float32)
    inner_dot = lax.psum(jnp.sum(activated * upstream, axis=1), "narrow")
    cubed = inv_norm * inv_norm * inv_norm
    grad_act = upstream * inv_norm[:, None] - activated * (inner_dot * cubed / width)[:, None]
    grad_pre = jnp.where(pre_act > 0, grad_act, 0.0).astype(jnp.bfloat16)
    grad_combine = jnp.concatenate(
        [
            contract_rows(node_feats, grad_pre),
            contract_rows_exact(pooled_full, grad_pre.astype(jnp.float32)),
        ],
        axis=0,
    )
    grad_cbias = jnp.sum(grad_pre.astype(jnp.float32), axis=0)
    self_part = contract_cols(grad_pre, self_rows)
    pooled_part = contract_cols(grad_pre, pool_weight)
    grad_pooled = lax.psum_scatter(pooled_part, "narrow", scatter_dimension=1, tiled=True).astype(
        jnp.bfloat16
    )
    grad_table = spread_rows(
        grad_pooled, neighbour_slot, importance, local_rows + owners * capacity
    )
    returned = lax.all_to_all(
        grad_table[local_rows:].reshape(owners, capacity, -1),
        "wide",
        split_axis=0,
        concat_axis=0,
        tiled=True,
    )
    grad_message = grad_table[:local_rows] + contract_rows_exact(
        selector, returned.reshape(owners * capacity, -1)
    )
    grad_hidden = jnp.where(hidden > 0, grad_message, 0.0).astype(jnp.bfloat16)
    grad_neigh = contract_rows(node_feats, grad_hidden)
    grad_nbias = jnp.sum(grad_hidden.astype(jnp.float32), axis=0)
    partial_inputs = self_part + contract_cols(grad_hidden, neigh_weight)
    grad_features = lax.psum_scatter(partial_inputs, "narrow", scatter_dimension=1, tiled=True)
    grad_neigh, grad_nbias, grad_combine, grad_cbias = lax.psum(
        (grad_neigh, grad_nbias, grad_combine, grad_cbias), "wide"
    )
    return (embedding, grad_features, grad_neigh, grad_nbias, grad_combine, grad_cbias)


def solution(mesh):
    placed = (
        P("wide", None),
        P(None, "narrow"),
        P("narrow"),
        P(None, "narrow"),
        P("narrow"),
        P("wide", "narrow"),
        P("wide", None),
        P("wide", None),
        P("wide", None),
        P("wide", None),
    )
    return jax.shard_map(
        shards,
        mesh=mesh,
        in_specs=placed,
        out_specs=(
            P("wide", "narrow"),
            P("wide", "narrow"),
            P(None, "narrow"),
            P("narrow"),
            P(None, "narrow"),
            P("narrow"),
        ),
        check_vma=False,
    )
```

profile of v0, /device:TPU:0, one launch (start us, length us, event | category | flops | bytes accessed | tf_op | source)
XLA Modules:
  0.0 655.2 jit_solution(17773311874145433632)
XLA Ops:
  7.2 0.0 copy-start
  7.2 0.8 convert_element_type.35
  8.0 0.7 copy.52
  8.7 0.1 copy-done
  8.8 1.8 broadcast_maximum_fusion
  10.6 5.3 fusion.5
  15.9 5.3 all-to-all-start
  21.2 0.0 all-gather.2.cloned.1.call-start
  21.2 1.3 copy.37
  22.5 1.0 convert_reduce_fusion.2
  23.5 1.0 convert_divide_fusion
  24.5 0.2 reshape.53
  24.7 1.1 reshape.52
  25.9 22.0 %all-to-all-done = f32[8,256,256]{2,1,0:T(8,128)} async-done(((f32[8,256,256]{2,1,0:T(8,128)}), f32[8,256,256]{2,1,0:T(8,128)}, u32[]{:S(2)}, u32[]{:S(2)}) %all-to-all-start) | async-done | bytes 2097184 | tf_op jit(solution)/shard_map/all_to_all | solution.py:112
  47.9 3.7 pad_maximum_fusion
  51.6 111.6 %while.21 = (s32[]{:T(128)}, f32[2,512,256]{2,1,0:T(8,128)}, s32[2,512,50]{1,2,0:T(8,128)S(1)}, f32[2,512,50]{1,2,0:T(8,128)S(1)}, f32[3072,256]{1,0:T(8,128)}, /*index=5*/s32[]{:T(128)}) while((s32[]{:T(128)}, f32[2,512,256]{2,1,0:T(8,128)}, s32[2,512,50]{1,2,0:T(8,128)S(1)}, f32[2,512,50]{1,2,0:T(8,128)S(1)}, f32[3072,256]{1,0:T(8,128)}, ...), condition=%wide.region_3.4_spmd, body=%wide.region_1.3_spmd.sunk | while | flops 5066194944 | bytes 16867916 | solution.py:50
  51.7 46.7 %select_reduce_fusion.4 = f32[512,3072]{1,0:T(8,128)} fusion(f32[512,50]{0,1:T(8,128)S(1)} %dynamic-slice_bitcast_fusion.8, s32[512,50]{0,1:T(8,128)S(1)} %dynamic-slice_bitcast_fusion.9), kind=kLoop, calls=%fused_computation.clone.1 | loop fusion | flops 234356736 | bytes 6496256 | tf_op jit(solution)/shard_map/while/body/eval_jaxpr/reduce_sum | solution.py:34
  98.4 9.0 %fusion.52 = f32[2,512,256]{2,1,0:T(8,128)} fusion(f32[2,512,256]{2,1,0:T(8,128)} %get-tuple-element.215, s32[]{:T(128)} %get-tuple-element.214, f32[512,3072]{1,0:T(8,128)} %select_reduce_fusion.4, f32[3072,256]{1,0:T(8,128)} %get-tuple-element.224), kind=kOutput, calls=%fused_computation.3.clone.1 | convolution fusion | flops 4831838208 | bytes 9961984 | tf_op jit(solution)/shard_map/while/body/eval_jaxpr/dot_general | solution.py:46
  107.4 46.7 %select_reduce_fusion.4 = f32[512,3072]{1,0:T(8,128)} fusion(f32[512,50]{0,1:T(8,128)S(1)} %dynamic-slice_bitcast_fusion.8, s32[512,50]{0,1:T(8,128)S(1)} %dynamic-slice_bitcast_fusion.9), kind=kLoop, calls=%fused_computation.clone.1 | loop fusion | flops 234356736 | bytes 6496256 | tf_op jit(solution)/shard_map/while/body/eval_jaxpr/reduce_sum | solution.py:34
  154.1 9.0 %fusion.52 = f32[2,512,256]{2,1,0:T(8,128)} fusion(f32[2,512,256]{2,1,0:T(8,128)} %get-tuple-element.215, s32[]{:T(128)} %get-tuple-element.214, f32[512,3072]{1,0:T(8,128)} %select_reduce_fusion.4, f32[3072,256]{1,0:T(8,128)} %get-tuple-element.224), kind=kOutput, calls=%fused_computation.3.clone.1 | convolution fusion | flops 4831838208 | bytes 9961984 | tf_op jit(solution)/shard_map/while/body/eval_jaxpr/dot_general | solution.py:46
  163.2 0.0 all-gather.2.cloned.1.call-update
  163.2 0.2 reduce-scatter.3.cloned.1.call-start
  163.4 1.3 copy.40
  164.7 0.0 copy-start.1
  164.7 3.0 fusion.21
  167.7 76.4 %all-gather.2.cloned.1.call-done = f32[1024,1024]{1,0:T(8,128)} async-done(((f32[1024,256]{1,0:T(8,128)}), f32[1024,1024]{1,0:T(8,128)}) %all-gather.2.cloned.1.call-update) | async-done | bytes 4194320 | tf_op jit(solution)/shard_map/all_gather | solution.py:115
  244.0 6.0 fusion.15
  250.0 9.1 %all-reduce.2 = (f32[1024]{0:T(1024)S(1)}, f32[1024]{0:T(1024)S(1)}) all-reduce(f32[1024]{0:T(1024)S(1)} %get-tuple-element.109, f32[1024]{0:T(1024)S(1)} %get-tuple-element.108), channel_id=1, replica_groups=mesh['wide'=8,'narrow'=4] {'narrow'}, use_global_device_ids=true, to_apply=%region_5.6 | all-reduce | flops 2048 | bytes 16384 | tf_op jit(solution)/shard_map/psum | solution.py:130
  259.2 2.5 convert_reduce_fusion
  261.7 3.8 fusion.16
  265.4 0.0 reduce-scatter.3.cloned.1.call-update
  265.5 75.9 %reduce-scatter.3.cloned.1.call-done = f32[1024,256]{1,0:T(8,128)} async-done(((f32[1024,1024]{1,0:T(8,128)}), f32[1024,256]{1,0:T(8,128)}) %reduce-scatter.3.cloned.1.call-update) | async-done | bytes 1048592 | tf_op jit(solution)/shard_map/reduce_scatter | solution.py:148
  341.4 2.1 convert_element_type.40
  343.4 113.6 %while.22 = (s32[]{:T(128)}, f32[3072,256]{1,0:T(8,128)}, s32[2,512,50]{1,2,0:T(8,128)S(1)}, f32[2,512,50]{1,2,0:T(8,128)S(1)}, bf16[2,512,256]{2,1,0:T(8,128)(2,1)}, /*index=5*/s32[]{:T(128)}, s32[]{:T(128)}) while((s32[]{:T(128)}, f32[3072,256]{1,0:T(8,128)}, s32[2,512,50]{1,2,0:T(8,128)S(1)}, f32[2,512,50]{1,2,0:T(8,128)S(1)}, ...), condition=%wide.region_11.12_spmd.clone, body=%wide.region_9.11_spmd.clone.sunk | while | flops 5067767808 | bytes 19751520 | solution.py:72
  343.5 46.7 %select_reduce_fusion.5 = f32[512,3072]{1,0:T(8,128)} fusion(f32[512,50]{0,1:T(8,128)S(1)} %dynamic-slice_bitcast_fusion.10, s32[512,50]{0,1:T(8,128)S(1)} %dynamic-slice_bitcast_fusion.11), kind=kLoop, calls=%fused_computation.6.clone.1 | loop fusion | flops 234356736 | bytes 6496256 | tf_op jit(solution)/shard_map/while/body/eval_jaxpr/reduce_sum | solution.py:34
  390.2 9.5 %convolution_add_fusion.5 = f32[3072,256]{1,0:T(8,128)} fusion(f32[512,3072]{1,0:T(8,128)} %select_reduce_fusion.5, f32[3072,256]{1,0:T(8,128)} %get-tuple-element.234, pred[]{:T(512)S(6)} %compare.3, bf16[2,512,256]{2,1,0:T(8,128)(2,1)} %get-tuple-element.244, s32[]{:T(128)} %get-tuple-element.233), kind=kOutput, calls=%fused_computation.8.clone.1 | convolution fusion | flops 4833411072 | bytes 12845569 | tf_op jit(solution)/shard_map/while/body/eval_jaxpr/dot_general | solution.py:16
  399.8 46.7 %select_reduce_fusion.5 = f32[512,3072]{1,0:T(8,128)} fusion(f32[512,50]{0,1:T(8,128)S(1)} %dynamic-slice_bitcast_fusion.10, s32[512,50]{0,1:T(8,128)S(1)} %dynamic-slice_bitcast_fusion.11), kind=kLoop, calls=%fused_computation.6.clone.1 | loop fusion | flops 234356736 | bytes 6496256 | tf_op jit(solution)/shard_map/while/body/eval_jaxpr/reduce_sum | solution.py:34
  446.5 10.5 %convolution_add_fusion.5 = f32[3072,256]{1,0:T(8,128)} fusion(f32[512,3072]{1,0:T(8,128)} %select_reduce_fusion.5, f32[3072,256]{1,0:T(8,128)} %get-tuple-element.234, pred[]{:T(512)S(6)} %compare.3, bf16[2,512,256]{2,1,0:T(8,128)(2,1)} %get-tuple-element.244, s32[]{:T(128)} %get-tuple-element.233), kind=kOutput, calls=%fused_computation.8.clone.1 | convolution fusion | flops 4833411072 | bytes 12845569 | tf_op jit(solution)/shard_map/while/body/eval_jaxpr/dot_general | solution.py:16
  457.0 3.0 slice.15
  460.0 4.4 all-to-all-start.1
  464.4 0.3 all-reduce.5.cloned.1.call-start
  464.7 0.7 convolution_bitcast_fusion.1
  465.4 4.3 fusion.26
  469.7 1.5 pad_maximum_fusion.1
  471.2 3.6 copy.43
  474.9 16.2 %all-to-all-done.1 = f32[8,256,256]{2,1,0:T(8,128)} async-done(((f32[8,256,256]{2,1,0:T(8,128)}), f32[8,256,256]{2,1,0:T(8,128)}, u32[]{:S(2)}, u32[]{:S(2)}) %all-to-all-start.1) | async-done | bytes 2097184 | tf_op jit(solution)/shard_map/all_to_all | solution.py:154
  491.1 6.7 %convert_reduce_fusion.1 = (f32[256]{0:T(256)S(1)}, bf16[1024,256]{0,1:T(8,128)(2,1)S(1)}) fusion(f32[2048,256]{1,0:T(8,128)} %bitcast.8, s32[2048]{0:T(1024)S(1)} %bitcast.73, f32[3072,256]{0,1:T(8,128)} %copy.43, f32[1024,256]{0,1:T(8,128)} %copy-done.6), kind=kOutput, calls=%fused_computation.37 | convolution fusion | flops 6446120960 | bytes 4727808 | tf_op jit(solution)/shard_map/dot_general | solution.py:16
  497.8 0.0 copy-start.3
  497.8 0.8 copy-done.3
  498.6 1.7 convolution_bitcast_fusion.2
  500.3 0.0 all-reduce.5.cloned.1.call-update
  500.3 0.0 copy-start.2
  500.3 0.0 reduce-scatter.5.cloned.1.call-start
  500.4 0.0 copy-start.4
  500.4 1.9 fusion.19
  502.3 2.8 convolution_add_fusion.1
  505.1 0.0 reduce-scatter.5.cloned.1.call-update
  505.1 1.0 copy-done.5
  506.1 1.0 copy.46
  507.1 13.0 %all-reduce = (f32[256]{0:T(256)}, f32[256]{0:T(256)}) all-reduce(f32[256]{0:T(256)S(1)} %get-tuple-element.144, f32[256]{0:T(256)S(1)} %get-tuple-element.136), channel_id=1, replica_groups=mesh['wide'=8,'narrow'=4] {'wide'}, use_global_device_ids=true, to_apply=%region_15.16 | all-reduce | flops 512 | bytes 4096 | tf_op jit(solution)/shard_map/psum | solution.py:169
  520.2 48.9 %all-reduce.5.cloned.1.call-done = (f32[1024,256]{0,1:T(8,128)}, f32[2048,256]{0,1:T(8,128)}) async-done(((f32[1024,256]{0,1:T(8,128)}, f32[2048,256]{0,1:T(8,128)}), (f32[1024,256]{0,1:T(8,128)}, f32[2048,256]{0,1:T(8,128)})) %all-reduce.5.cloned.1.call-update) | async-done | bytes 3145744 | tf_op jit(solution)/shard_map/psum | solution.py:169
  569.1 3.0 copy.48
  572.0 1.3 copy.47
  573.3 75.3 %reduce-scatter.5.cloned.1.call-done = f32[1024,256]{1,0:T(8,128)} async-done(((f32[1024,1024]{1,0:T(8,128)}), f32[1024,256]{1,0:T(8,128)}) %reduce-scatter.5.cloned.1.call-update) | async-done | bytes 1048592 | tf_op jit(solution)/shard_map/reduce_scatter | solution.py:168
  (26 shorter events, 0.2 us)
Async XLA Ops:
  7.2 1.6 copy-start
  10.6 5.3 copy-start.6
  15.9 6.7 %copy-start.8 = (s32[1024,50]{0,1:T(8,128)S(1)}, s32[1024,50]{0,1:T(8,128)}, u32[]{:S(2)}) copy-start(s32[1024,50]{0,1:T(8,128)} %param.22) | copy-start | bytes 614404
  15.9 32.1 %all-to-all-start = ((f32[8,256,256]{2,1,0:T(8,128)}), f32[8,256,256]{2,1,0:T(8,128)}, u32[]{:S(2)}, u32[]{:S(2)}) async-start(f32[8,256,256]{2,1,0:T(8,128)} %bitcast.69), calls=%async_computation | async-start | bytes 4194304 | tf_op jit(solution)/shard_map/all_to_all | solution.py:112
  21.2 222.9 %all-gather.2.cloned.1.call-start = ((), (), s32[]{:S(2)}) async-start(), calls=%async_computation.4 | async-start | bytes 5242880 | tf_op jit(solution)/shard_map/all_gather | solution.py:115
  51.6 113.1 %copy-start.9 = (bf16[256]{0:T(256)(128)(2,1)S(1)}, bf16[256]{0:T(256)(128)(2,1)}, u32[]{:S(2)}) copy-start(bf16[256]{0:T(256)(128)(2,1)} %param.18) | copy-start | bytes 1540
  163.2 178.1 %reduce-scatter.3.cloned.1.call-start = ((), (), s32[]{:S(2)}) async-start(), calls=%async_computation.5 | async-start | bytes 5242880 | tf_op jit(solution)/shard_map/reduce_scatter | solution.py:148
  164.7 85.3 %copy-start.1 = (bf16[1024,256]{0,1:T(8,128)(2,1)}, bf16[1024,256]{0,1:T(8,128)(2,1)S(1)}, u32[]{:S(2)}) copy-start(bf16[1024,256]{0,1:T(8,128)(2,1)S(1)} %copy.40) | copy-start | bytes 1572868
  460.0 31.0 %all-to-all-start.1 = ((f32[8,256,256]{2,1,0:T(8,128)}), f32[8,256,256]{2,1,0:T(8,128)}, u32[]{:S(2)}, u32[]{:S(2)}) async-start(f32[8,256,256]{2,1,0:T(8,128)} %bitcast.67), calls=%async_computation.2 | async-start | bytes 4194304 | tf_op jit(solution)/shard_map/all_to_all | solution.py:154
  464.4 104.6 %all-reduce.5.cloned.1.call-start = ((), (), s32[]{:S(2)}) async-start(), calls=%async_computation.7 | async-start | bytes 6291456 | tf_op jit(solution)/shard_map/psum | solution.py:169
  497.8 0.8 copy-start.3
  500.3 2.0 copy-start.2
  500.3 148.3 %reduce-scatter.5.cloned.1.call-start = ((), (), s32[]{:S(2)}) async-start(), calls=%async_computation.6 | async-start | bytes 5242880 | tf_op jit(solution)/shard_map/reduce_scatter | solution.py:168
  500.4 1.9 copy-start.4
  505.1 1.1 copy-start.5
  569.1 3.0 copy-start.7
Sparse Core Ops, SparseCore 0:
  163.3 80.6 all-gather.1
  265.6 75.7 reduce-scatter.2
  500.4 68.5 all-reduce.4
  571.8 76.8 reduce-scatter.4
where the time goes:
time: 656 us; the launch traced here: 655 us
  waiting for transfers between devices  315 us (48%)
  other arithmetic  199 us (30%)
  matrix products  76 us (12%)
  blocking collectives  22.1 us (3%)
  local copies, waits for them, and re-layouts  18.6 us (3%)
  between operations  14 us (2%)
  starting transfers between devices  10.2 us (2%)
    reduce_sum x4, other arithmetic, dense_weights(): return jnp.sum(jnp.where(hits, weight_block[:, :, None], 0.0), axis=1)  187 us
    all_gather x1, waiting for transfers between devices, shards(): pooled_full = lax.all_gather(pooled, 'narrow', axis=1, tiled=True)  76.4 us
    reduce_scatter x1, waiting for transfers between devices, shards(): lax.psum_scatter(pooled_part, 'narrow', scatter_dimension=1, tiled=True)  75.9 us
    reduce_scatter x1, waiting for transfers between devices, shards(): lax.psum_scatter(partial_inputs, 'narrow', scatter_dimension=1, tiled=True)  75.3 us
    psum x1, waiting for transfers between devices, shards(): lax.psum((grad_neigh, grad_nbias, grad_combine, grad_cbias), 'wide')  48.9 us
    dot_general x4, matrix products, contract_rows_exact(): lax.dot_general(left, right, (((0,), (0,)), ((), ())), precision=lax.Prec...  31 us
    all_to_all x1, waiting for transfers between devices, shards(): lax.all_to_all(outgoing, 'wide', split_axis=0, concat_axis=0, tiled=True)  22 us
    dot_general x2, matrix products, pool_one_block(): jnp.dot(mixing, msg_table, precision=lax.Precision.HIGHEST, preferred_ele...  18.1 us
  transfers between devices with their start and end apart: 6, of which 6 were waited for; matrix products, arithmetic and copies ran while one was open for 4% of the time, Pallas kernels for 0%

commit v1 on v0

v1 whole, which is shorter than its diff:
```python
import jax
import jax.numpy as jnp
from jax import lax
from jax.sharding import PartitionSpec as P

EPSILON = 1e-06
F32 = jnp.float32
BF16 = jnp.bfloat16


def mm(left, right, dims=((1,), (0,))):
    return lax.dot_general(left, right, (dims, ((), ())), preferred_element_type=F32)


def split(value):
    high = lax.reduce_precision(value, 8, 7)
    return high.astype(BF16), (value - high).astype(BF16)


def mm2(left, right):
    high, low = split(right)
    return mm(left, high) + mm(left, low)


def counts_matrix(slots, weights, table_rows):
    positions = jnp.arange(table_rows, dtype=jnp.int32)
    hits = slots[:, :, None] == positions[None, None, :]
    return jnp.sum(jnp.where(hits, weights[:, :, None], 0.0), axis=1)


def shards(
    node_feats,
    neigh_weight,
    neigh_bias,
    combine_weight,
    combine_bias,
    cotangent,
    neighbour_slot,
    neighbour_mask,
    visit_count,
    send_rows,
):
    width = node_feats.shape[1]
    local_rows = node_feats.shape[0]
    owners = lax.axis_size("wide")
    capacity = send_rows.shape[1]
    masked = (visit_count * neighbour_mask).astype(F32)
    inv_sum = 1.0 / jnp.sum(masked, axis=1, keepdims=True)
    counts = counts_matrix(neighbour_slot, masked, local_rows + owners * capacity)
    counts_hi, counts_lo = split(counts)
    selector = (
        send_rows.reshape(-1)[:, None] == jnp.arange(local_rows, dtype=jnp.int32)[None, :]
    ).astype(BF16)
    neigh_full = lax.all_gather(neigh_weight, "narrow", axis=1, tiled=True)
    bias_full = lax.all_gather(neigh_bias, "narrow", axis=0, tiled=True)
    hidden = mm(node_feats, neigh_full) + bias_full.astype(F32)
    message = jnp.maximum(hidden, 0.0)
    msg_hi, msg_lo = split(message)
    self_rows = combine_weight[:width]
    pool_weight = combine_weight[width:]
    z = mm(msg_hi, pool_weight) + mm(msg_lo, pool_weight)
    outgoing = mm2(selector, z).reshape(owners, capacity, -1)
    incoming = lax.all_to_all(outgoing, "wide", split_axis=0, concat_axis=0, tiled=True)
    table = jnp.concatenate([z, incoming.reshape(owners * capacity, -1)], axis=0)
    t_hi, t_lo = split(table)
    pool = mm(counts_hi, t_hi) + mm(counts_hi, t_lo) + mm(counts_lo, t_hi)
    pre_act = mm(node_feats, self_rows) + pool * inv_sum + combine_bias.astype(F32)
    activated = jnp.maximum(pre_act, 0.0)
    upstream = cotangent.astype(F32)
    squares = lax.psum(jnp.sum(activated * activated, axis=1), "narrow")
    inner_dot = lax.psum(jnp.sum(activated * upstream, axis=1), "narrow")
    inv_norm = lax.rsqrt(squares / width + EPSILON)
    embedding = (activated * inv_norm[:, None]).astype(BF16)
    cubed = inv_norm * inv_norm * inv_norm
    grad_act = upstream * inv_norm[:, None] - activated * (inner_dot * cubed / width)[:, None]
    grad_pre = jnp.where(pre_act > 0, grad_act, 0.0)
    scaled = (grad_pre * inv_sum).astype(BF16)
    grad_pre = grad_pre.astype(BF16)
    grad_cbias = jnp.sum(grad_pre.astype(F32), axis=0)
    grad_table = mm(counts_hi, scaled, ((0,), (0,)))
    returned = lax.all_to_all(
        grad_table[local_rows:].astype(BF16).reshape(owners, capacity, -1),
        "wide",
        split_axis=0,
        concat_axis=0,
        tiled=True,
    )
    y = (
        grad_table[:local_rows]
        + mm(selector, returned.reshape(owners * capacity, -1), ((0,), (0,)))
    ).astype(BF16)
    grad_combine = jnp.concatenate(
        [mm(node_feats, grad_pre, ((0,), (0,))), mm(msg_hi, y, ((0,), (0,)))], axis=0
    )
    to_rows = lambda v: lax.all_to_all(v, "narrow", split_axis=0, concat_axis=1, tiled=True)
    to_cols = lambda v: lax.all_to_all(v, "narrow", split_axis=1, concat_axis=0, tiled=True)
    combine_full = lax.all_gather(combine_weight, "narrow", axis=1, tiled=True)
    grad_pre_rows = to_rows(grad_pre)
    y_rows = to_rows(y)
    rows = local_rows // lax.axis_size("narrow")
    hidden_rows = lax.dynamic_slice_in_dim(hidden, lax.axis_index("narrow") * rows, rows, 0)
    grad_message = mm(y_rows, combine_full[width:], ((1,), (1,)))
    grad_hidden_rows = jnp.where(hidden_rows > 0, grad_message, 0.0).astype(BF16)
    grad_hidden = to_cols(grad_hidden_rows)
    grad_features_rows = mm(grad_pre_rows, combine_full[:width], ((1,), (1,))) + mm(
        grad_hidden_rows, neigh_full, ((1,), (1,))
    )
    grad_features = to_cols(grad_features_rows.astype(BF16)).astype(F32)
    grad_neigh = mm(node_feats, grad_hidden, ((0,), (0,)))
    grad_nbias = jnp.sum(grad_hidden.astype(F32), axis=0)
    grad_neigh, grad_nbias, grad_combine, grad_cbias = lax.psum(
        (grad_neigh, grad_nbias, grad_combine, grad_cbias), "wide"
    )
    return (embedding, grad_features, grad_neigh, grad_nbias, grad_combine, grad_cbias)


def solution(mesh):
    placed = (
        P("wide", None),
        P(None, "narrow"),
        P("narrow"),
        P(None, "narrow"),
        P("narrow"),
        P("wide", "narrow"),
        P("wide", None),
        P("wide", None),
        P("wide", None),
        P("wide", None),
    )
    return jax.shard_map(
        shards,
        mesh=mesh,
        in_specs=placed,
        out_specs=(
            P("wide", "narrow"),
            P("wide", "narrow"),
            P(None, "narrow"),
            P("narrow"),
            P(None, "narrow"),
            P("narrow"),
        ),
        check_vma=False,
    )
```

time: 656 us -> 356 us (0.54)
  waiting for transfers between devices: 315 us -> 89.1 us
  other arithmetic: 199 us -> 104 us
  blocking collectives: 22.1 us -> 69.6 us
  matrix products: 76 us -> 50.9 us
  local copies, waits for them, and re-layouts: 18.6 us -> 11.6 us
    reduce_scatter x2 -> x0, waiting for transfers between devices: 151 us -> none  [the longest x1 75.9 us: shards(): lax.psum_scatter(pooled_part, 'narrow', scatter_dimension=1, tiled=True)]
    reduce_sum x6 -> x4, other arithmetic: 190 us -> 100 us  [the longest x1 96.2 us: counts_matrix(): return jnp.sum(jnp.where(hits, weights[:, :, None], 0.0), axis=1)]
    all_gather x1 -> x2, waiting for transfers between devices: 76.4 us -> 34.8 us  [the longest x1 34.8 us: shards(): neigh_full = lax.all_gather(neigh_weight, 'narrow', axis=1, tiled=True)]
    all_to_all x0 -> x2, blocking collectives: none -> 35.4 us  [the longest x1 19.1 us: shards(): lax.all_to_all(grad_table[local_rows:].astype(BF16).reshape(owners, capac...]
    dot_general x15 -> x17, matrix products: 76 us -> 50.9 us  [mm(): lax.dot_general(left, right, (dims, ((), ())), preferred_element_type=F32)]
    all_to_all x1, waiting for transfers between devices: 22 us -> 0.01 us  [shards(): lax.all_to_all(outgoing, 'wide', split_axis=0, concat_axis=0, tiled=True)]
    psum x1, waiting for transfers between devices: 48.9 us -> 28.2 us  [shards(): lax.psum((grad_neigh, grad_nbias, grad_combine, grad_cbias), 'wide')]
    all_gather x0 -> x1, blocking collectives: none -> 12.6 us  [shards(): bias_full = lax.all_gather(neigh_bias, 'narrow', axis=0, tiled=True)]
  transfers between devices with their start and end apart: 6 -> 7, of which waited for: 6 -> 5; matrix products, arithmetic and copies ran while one was open for 4% -> 44% of each run, Pallas kernels for 0% -> 0%
where the time goes in v1:
time: 356 us; the launch traced here: 355 us
  other arithmetic  104 us (29%)
  waiting for transfers between devices  89.1 us (25%)
  blocking collectives  69.6 us (20%)
  matrix products  50.9 us (14%)
  starting transfers between devices  15.7 us (4%)
  between operations  14 us (4%)
  local copies, waits for them, and re-layouts  11.6 us (3%)
    reduce_sum x1, other arithmetic, counts_matrix(): return jnp.sum(jnp.where(hits, weights[:, :, None], 0.0), axis=1)  96.2 us
    dot_general x17, matrix products, mm(): lax.dot_general(left, right, (dims, ((), ())), preferred_element_type=F32)  50.9 us
    all_gather x1, waiting for transfers between devices, shards(): neigh_full = lax.all_gather(neigh_weight, 'narrow', axis=1, tiled=True)  34.8 us
    psum x1, waiting for transfers between devices, shards(): lax.psum((grad_neigh, grad_nbias, grad_combine, grad_cbias), 'wide')  28.2 us
    all_to_all x2, waiting for transfers between devices, shards(): lax.all_to_all(v, 'narrow', split_axis=0, concat_axis=1, tiled=True)  19.9 us
    all_to_all x1, blocking collectives, shards(): lax.all_to_all(grad_table[local_rows:].astype(BF16).reshape(owners, capac...  19.1 us
    all_to_all x1, blocking collectives, shards(): lax.all_to_all(v, 'narrow', split_axis=1, concat_axis=0, tiled=True)  16.3 us
    all_gather x1, blocking collectives, shards(): bias_full = lax.all_gather(neigh_bias, 'narrow', axis=0, tiled=True)  12.6 us
  transfers between devices with their start and end apart: 7, of which 5 were waited for; matrix products, arithmetic and copies ran while one was open for 44% of the time, Pallas kernels for 0%

profile of v1, /device:TPU:0, one launch (start us, length us, event | category | flops | bytes accessed | tf_op | source)
XLA Modules:
  0.0 355.2 jit_solution(12699208619916700158)
XLA Ops:
  7.2 0.0 copy-start
  7.2 0.0 all-gather.4.cloned.1.call-start
  7.2 0.7 all-gather.4.cloned.1.call-update
  7.9 0.0 all-gather.6.cloned.1.call-start
  8.0 0.7 all-gather.6.cloned.1.call-update
  8.7 0.7 reshape.54
  9.3 12.6 %all-gather = bf16[4,1,256]{2,1,0:T(2,128)(2,1)S(1)} all-gather(bf16[1,1,256]{2,1,0:T(2,128)(2,1)S(1)} %reshape.54), channel_id=1, replica_groups=mesh['wide'=8,'narrow'=4] {'narrow'}, dimensions={0}, use_global_device_ids=true | all-gather | bytes 2560 | tf_op jit(solution)/shard_map/all_gather | solution.py:55
  21.9 0.7 copy.54
  22.6 1.1 fusion.60
  23.7 34.8 %all-gather.4.cloned.1.call-done = bf16[1024,1024]{1,0:T(8,128)(2,1)} async-done(((bf16[1024,256]{1,0:T(8,128)(2,1)}), bf16[1024,1024]{1,0:T(8,128)(2,1)}) %all-gather.4.cloned.1.call-update) | async-done | bytes 2097168 | tf_op jit(solution)/shard_map/all_gather | solution.py:54
  58.5 0.0 copy-done
  58.6 4.1 %broadcast_add_fusion = f32[1024,1024]{0,1:T(8,128)S(1)} fusion(f32[1024]{0:T(1024)S(1)} %bitcast.59, bf16[1024,1024]{1,0:T(8,128)(2,1)S(1)} %copy-done, bf16[1024,1024]{1,0:T(8,128)(2,1)} %all-gather.4.cloned.1.call-done), kind=kOutput, calls=%fused_computation.29 | convolution fusion | flops 2148532224 | bytes 8392704 | tf_op jit(solution)/shard_map/dot_general | solution.py:12
  62.6 0.7 fusion.12
  63.4 1.2 copy-done.2
  64.6 0.7 convolution_add_fusion
  65.3 1.6 fusion.2
  67.0 2.8 fusion.11
  69.7 4.5 %all-to-all-start = ((f32[8,256,256]{2,1,0:T(8,128)}), f32[8,256,256]{2,1,0:T(8,128)}, u32[]{:S(2)}, u32[]{:S(2)}) async-start(f32[8,256,256]{2,1,0:T(8,128)} %bitcast.48), calls=%async_computation | async-start | bytes 4194304 | tf_op jit(solution)/shard_map/all_to_all | solution.py:63
  74.3 0.0 copy-start.12
  74.3 96.2 %select_reduce_fusion = f32[1024,3072]{1,0:T(8,128)} fusion(f32[1024,50]{0,1:T(8,128)S(1)} %get-tuple-element.41, s32[1024,50]{0,1:T(8,128)} %param.16), kind=kLoop, calls=%fused_computation | loop fusion | flops 468713472 | bytes 12992512 | tf_op jit(solution)/shard_map/reduce_sum | solution.py:28
  170.5 0.0 copy-done.12
  170.5 0.0 all-to-all-done
  170.5 7.1 %fusion.19 = f32[1024,256]{1,0:T(8,128)S(1)} fusion(f32[2048,256]{1,0:T(8,128)} %bitcast.2, f32[1024,256]{1,0:T(8,128)S(1)} %convolution_add_fusion, f32[1024,3072]{1,0:T(8,128)} %select_reduce_fusion), kind=kOutput, calls=%fused_computation.30 | convolution fusion | flops 1620049920 | bytes 16777216 | tf_op jit(solution)/shard_map/dot_general | solution.py:12
  177.7 1.6 copy-done.1
  179.3 3.4 fusion.4
  182.7 0.0 copy-start.5
  182.7 0.0 copy-start.6
  182.8 3.6 %fusion.29 = f32[1024,256]{1,0:T(8,128)S(1)} fusion(f32[1024,256]{1,0:T(8,128)S(1)} %fusion.4, f32[1024,256]{1,0:T(8,128)S(1)} %fusion.19, f32[1024]{0:T(1024)S(1)} %broadcast_divide_fusion, f32[2048,256]{1,0:T(8,128)} %bitcast.2, f32[1024,256]{1,0:T(8,128)S(1)} %convolution_add_fusion, f32[1024,3072]{1,0:T(8,128)S(1)} %copy-done.1), kind=kOutput, calls=%fused_computation.44 | convolution fusion | flops 1620049920 | bytes 18878464 | tf_op jit(solution)/shard_map/dot_general | solution.py:12
  186.4 0.9 fusion.40
  187.3 0.0 copy-start.3
  187.3 9.2 %all-reduce.2 = (f32[1024]{0:T(1024)S(1)}, f32[1024]{0:T(1024)S(1)}) all-reduce(f32[1024]{0:T(1024)S(1)} %get-tuple-element.31, f32[1024]{0:T(1024)S(1)} %get-tuple-element.30), channel_id=1, replica_groups=mesh['wide'=8,'narrow'=4] {'narrow'}, use_global_device_ids=true, to_apply=%region_3.4 | all-reduce | flops 2048 | bytes 16384 | tf_op jit(solution)/shard_map/psum | solution.py:70
  196.6 7.1 %fusion.43 = f32[3072,256]{1,0:T(8,128)S(1)} fusion(f32[1024]{0:T(1024)S(1)} %broadcast_divide_fusion, bf16[1024,256]{1,0:T(8,128)(2,1)} %param.15, f32[1024,256]{1,0:T(8,128)S(1)} %get-tuple-element.45, f32[1024]{0:T(1024)S(1)} %get-tuple-element.43, f32[1024]{0:T(1024)S(1)} %get-tuple-element.44, f32[1024,3072]{1,0:T(8,128)} %select_reduce_fusion), kind=kOutput, calls=%fused_computation.60 | convolution fusion | flops 1619263488 | bytes 17313792 | tf_op jit(solution)/shard_map/dot_general | solution.py:12
  203.7 0.0 copy-done.3
  203.7 0.1 slice.49
  203.8 19.1 %all_to_all.80 = bf16[8,256,256]{2,1,0:T(8,128)(2,1)S(1)} all-to-all(bf16[8,256,256]{2,1,0:T(8,128)(2,1)S(1)} %bitcast.46), channel_id=1, replica_groups=mesh['wide'=8,'narrow'=4] {'wide'}, dimensions={0} | all-to-all | bytes 2097152 | tf_op jit(solution)/shard_map/all_to_all | solution.py:81
  222.9 2.7 fusion.31
  225.6 1.0 copy.44
  226.6 3.5 all-to-all-start.3
  230.1 0.0 all-gather.6.cloned.1.call-done
  230.1 14.1 %all-to-all-done.3 = bf16[4,256,256]{1,2,0:T(8,128)(2,1)S(1)} async-done(((bf16[4,256,256]{1,2,0:T(8,128)(2,1)}), bf16[4,256,256]{1,2,0:T(8,128)(2,1)S(1)}, u32[]{:S(2)}, u32[]{:S(2)}) %all-to-all-start.3) | async-done | bytes 524320 | tf_op jit(solution)/shard_map/all_to_all | solution.py:95
  244.2 0.0 copy-done.9
  244.2 2.6 fusion.35
  246.7 1.0 copy.47
  247.8 3.5 all-to-all-start.5
  251.2 2.6 convert_reduce_fusion
  253.8 1.0 copy.43
  254.8 1.7 convolution_bitcast_fusion
  256.5 3.9 %fusion.42 = f32[1024,256]{0,1:T(8,128)} fusion(bf16[1024,256]{1,0:T(8,128)(2,1)S(1)} %copy-done.10, f32[1024,1024]{0,1:T(8,128)} %copy-done.2), kind=kOutput, calls=%fused_computation.59 | convolution fusion | flops 540016640 | bytes 5767168 | tf_op jit(solution)/shard_map/dot_general | solution.py:12
  260.5 4.7 %all-to-all-done.5 = bf16[256,4,256]{2,0,1:T(8,128)(2,1)S(1)} async-done(((bf16[256,4,256]{2,0,1:T(8,128)(2,1)}), bf16[256,4,256]{2,0,1:T(8,128)(2,1)S(1)}, u32[]{:S(2)}, u32[]{:S(2)}) %all-to-all-start.5) | async-done | bytes 524320 | tf_op jit(solution)/shard_map/all_to_all | solution.py:96
  265.2 4.1 %all-to-all-start.1 = ((bf16[4,256,256]{1,2,0:T(8,128)(2,1)}), bf16[4,256,256]{1,2,0:T(8,128)(2,1)}, u32[]{:S(2)}, u32[]{:S(2)}) async-start(bf16[4,256,256]{1,2,0:T(8,128)(2,1)} %copy.43), calls=%async_computation.1 | async-start | bytes 1048576 | tf_op jit(solution)/shard_map/all_to_all | solution.py:95
  269.3 0.0 all-reduce.5.cloned.1.call-start
  269.4 3.1 pad_maximum_fusion.1
  272.5 1.7 convolution_bitcast_fusion.1
  274.2 0.0 all-reduce.5.cloned.1.call-update
  274.2 3.3 fusion.61
  277.6 5.8 %all-to-all-done.1 = bf16[4,256,256]{1,2,0:T(8,128)(2,1)} async-done(((bf16[4,256,256]{1,2,0:T(8,128)(2,1)}), bf16[4,256,256]{1,2,0:T(8,128)(2,1)}, u32[]{:S(2)}, u32[]{:S(2)}) %all-to-all-start.1) | async-done | bytes 524320 | tf_op jit(solution)/shard_map/all_to_all | solution.py:95
  283.4 2.8 fusion.32
  286.2 16.3 %all_to_all.81 = bf16[256,4,256]{2,0,1:T(8,128)(2,1)S(1)} all-to-all(bf16[256,4,256]{2,0,1:T(8,128)(2,1)S(1)} %bitcast.49), channel_id=1, replica_groups=mesh['wide'=8,'narrow'=4] {'narrow'}, dimensions={1} | all-to-all | bytes 1048576 | tf_op jit(solution)/shard_map/all_to_all | solution.py:96
  302.6 1.1 convert_element_type.96
  303.6 0.2 convert_reduce_fusion.1
  303.8 12.4 %all-reduce = (f32[256]{0:T(256)}, f32[256]{0:T(256)}) all-reduce(f32[256]{0:T(256)S(1)} %convert_reduce_fusion.1, f32[256]{0:T(256)S(1)} %get-tuple-element.38), channel_id=1, replica_groups=mesh['wide'=8,'narrow'=4] {'wide'}, use_global_device_ids=true, to_apply=%region_8.9 | all-reduce | flops 512 | bytes 4096 | tf_op jit(solution)/shard_map/psum | solution.py:111
  316.1 28.2 %all-reduce.5.cloned.1.call-done = (f32[1024,256]{0,1:T(8,128)}, f32[2048,256]{0,1:T(8,128)}) async-done(((f32[1024,256]{0,1:T(8,128)}, f32[2048,256]{0,1:T(8,128)}), (f32[1024,256]{0,1:T(8,128)}, f32[2048,256]{0,1:T(8,128)})) %all-reduce.5.cloned.1.call-update) | async-done | bytes 3145744 | tf_op jit(solution)/shard_map/psum | solution.py:111
  344.4 3.0 copy.50
  347.4 1.3 copy.49
  (20 shorter events, 0.1 us)
Async XLA Ops:
  7.2 51.4 %copy-start = (bf16[1024,1024]{1,0:T(8,128)(2,1)S(1)}, bf16[1024,1024]{1,0:T(8,128)(2,1)}, u32[]{:S(2)}) copy-start(bf16[1024,1024]{1,0:T(8,128)(2,1)} %param.10) | copy-start | bytes 6291460
  7.2 51.4 %all-gather.4.cloned.1.call-start = ((), (), s32[]{:S(2)}) async-start(), calls=%async_computation.6 | async-start | bytes 2621440 | tf_op jit(solution)/shard_map/all_gather | solution.py:54
  7.9 222.2 %all-gather.6.cloned.1.call-start = ((), (), s32[]{:S(2)}) async-start(), calls=%async_computation.7 | async-start | bytes 5242880 | tf_op jit(solution)/shard_map/all_gather | solution.py:97
  58.6 4.1 %copy-start.4 = (bf16[2048,256]{1,0:T(8,128)(2,1)S(1)}, bf16[2048,256]{1,0:T(8,128)(2,1)}, u32[]{:S(2)}) copy-start(bf16[2048,256]{1,0:T(8,128)(2,1)} %param.13) | copy-start | bytes 3145732
  62.6 1.9 copy-start.2
  69.7 100.8 %all-to-all-start = ((f32[8,256,256]{2,1,0:T(8,128)}), f32[8,256,256]{2,1,0:T(8,128)}, u32[]{:S(2)}, u32[]{:S(2)}) async-start(f32[8,256,256]{2,1,0:T(8,128)} %bitcast.48), calls=%async_computation | async-start | bytes 4194304 | tf_op jit(solution)/shard_map/all_to_all | solution.py:63
  74.3 96.2 %copy-start.12 = (bf16[256]{0:T(256)(128)(2,1)S(1)}, bf16[256]{0:T(256)(128)(2,1)}, u32[]{:S(2)}) copy-start(bf16[256]{0:T(256)(128)(2,1)} %param.14) | copy-start | bytes 1540
  170.5 8.8 %copy-start.1 = (f32[1024,3072]{1,0:T(8,128)S(1)}, f32[1024,3072]{1,0:T(8,128)}, u32[]{:S(2)}) copy-start(f32[1024,3072]{1,0:T(8,128)} %select_reduce_fusion) | copy-start | bytes 37748740
  182.7 3.6 %copy-start.5 = (bf16[2048,256]{1,0:T(8,128)(2,1)S(1)}, bf16[2048,256]{1,0:T(8,128)(2,1)}, u32[]{:S(2)}) copy-start(bf16[2048,256]{1,0:T(8,128)(2,1)} %param.13) | copy-start | bytes 3145732
  182.7 3.6 %copy-start.6 = (bf16[1024,256]{1,0:T(8,128)(2,1)S(1)}, bf16[1024,256]{1,0:T(8,128)(2,1)}, u32[]{:S(2)}) copy-start(bf16[1024,256]{1,0:T(8,128)(2,1)} %param.15) | copy-start | bytes 1572868
  187.3 16.4 %copy-start.3 = (f32[1024,256]{1,0:T(8,128)}, f32[1024,256]{1,0:T(8,128)S(1)}, u32[]{:S(2)}) copy-start(f32[1024,256]{1,0:T(8,128)S(1)} %get-tuple-element.45) | copy-start | bytes 3145732
  225.6 18.6 %copy-start.9 = (bf16[1024,256]{1,0:T(8,128)(2,1)}, bf16[1024,256]{1,0:T(8,128)(2,1)S(1)}, u32[]{:S(2)}) copy-start(bf16[1024,256]{1,0:T(8,128)(2,1)S(1)} %fusion.31) | copy-start | bytes 1572868
  226.6 17.6 %all-to-all-start.3 = ((bf16[4,256,256]{1,2,0:T(8,128)(2,1)}), bf16[4,256,256]{1,2,0:T(8,128)(2,1)S(1)}, u32[]{:S(2)}, u32[]{:S(2)}) async-start(bf16[4,256,256]{1,2,0:T(8,128)(2,1)} %copy.44), calls=%async_computation.3 | async-start | bytes 1048576 | tf_op jit(solution)/shard_map/all_to_all | solution.py:95
  246.7 1.0 copy-start.7
  247.8 17.4 %all-to-all-start.5 = ((bf16[256,4,256]{2,0,1:T(8,128)(2,1)}), bf16[256,4,256]{2,0,1:T(8,128)(2,1)S(1)}, u32[]{:S(2)}, u32[]{:S(2)}) async-start(bf16[256,4,256]{2,0,1:T(8,128)(2,1)} %copy.47), calls=%async_computation.5 | async-start | bytes 1048576 | tf_op jit(solution)/shard_map/all_to_all | solution.py:96
  254.8 1.7 copy-start.10
  265.2 18.2 %all-to-all-start.1 = ((bf16[4,256,256]{1,2,0:T(8,128)(2,1)}), bf16[4,256,256]{1,2,0:T(8,128)(2,1)}, u32[]{:S(2)}, u32[]{:S(2)}) async-start(bf16[4,256,256]{1,2,0:T(8,128)(2,1)} %copy.43), calls=%async_computation.1 | async-start | bytes 1048576 | tf_op jit(solution)/shard_map/all_to_all | solution.py:95
  269.3 75.1 %all-reduce.5.cloned.1.call-start = ((), (), s32[]{:S(2)}) async-start(), calls=%async_computation.8 | async-start | bytes 6291456 | tf_op jit(solution)/shard_map/psum | solution.py:111
  272.5 1.8 copy-start.8
  344.4 3.0 copy-start.11
Sparse Core Ops, SparseCore 0:
  9.6 48.9 all-gather.3
  60.1 78.7 all-gather.5
  274.3 69.9 all-reduce.4

commit v2 on v1

v2 whole, which is shorter than its diff:
```python
import functools

import jax
import jax.numpy as jnp
from jax import lax
from jax.experimental import pallas as pl
from jax.experimental.pallas import tpu as pltpu
from jax.sharding import PartitionSpec as P

EPSILON = 1e-06
F32 = jnp.float32
BF16 = jnp.bfloat16
I32 = jnp.int32
MESH = pl.DeviceIdType.MESH


def mm(left, right):
    return jnp.dot(left, right, preferred_element_type=F32)


def mm_nt(left, right):
    return lax.dot_general(left, right, (((1,), (1,)), ((), ())), preferred_element_type=F32)


def at(index, size):
    return pl.ds(pl.multiple_of(index * size, size), size)


class Sizes:
    def __init__(self, feats, neigh, send, slot, wide, narrow):
        self.rows, self.width = feats.shape
        self.cols = neigh.shape[1]
        self.cap = send.shape[1]
        self.slots = slot.shape[1]
        self.wide, self.narrow = wide, narrow
        self.chunk = min(256, self.rows)
        self.part = self.rows // narrow
        self.local = self.rows // self.cap
        self.blocks = self.local + wide
        self.red_rows = max(16, self.cols // wide)
        self.red_down = self.cols // self.red_rows
        self.red_across = wide // self.red_down
        self.red_lanes = self.width // self.red_across


NAMES_IN = ["feats_in", "nw_in", "nb_in", "comb_in", "cb_in", "cot_in", "slot_in", "mask_in", "visit_in", "send_in"]
NAMES_OUT = ["emb_out", "gf_out", "gn_out", "gc_out", "gnb_out", "gcb_out"]


def scratch(z):
    R, D, C, W, N, U, CAP = z.rows, z.width, z.cols, z.wide, z.narrow, z.part, z.cap
    v = lambda *shape: pltpu.VMEM(shape[:-1], shape[-1])
    bufs = dict(
        feats=v(R, D, BF16),
        nwfull=v(N, D, C, BF16),
        nbfull=v(N, 8, C, F32),
        wfull=v(N, 2 * D, C, BF16),
        cb=v(8, C, F32),
        cot=v(R, C, BF16),
        slot=v(R, z.slots, I32),
        mask=v(R, z.slots, I32),
        visit=v(R, z.slots, I32),
        send=v(CAP, W, I32),
        code=v(R, 128, I32),
        wts=v(R, 128, F32),
        counts=v(z.blocks, R, CAP, BF16),
        sel=v(W, CAP, R, BF16),
        msg=v(R, D, BF16),
        zacc=v(R, C, F32),
        zhi=v(R, C, BF16),
        zlo=v(R, C, BF16),
        zsend=v(W, 2, CAP, C, BF16),
        ztab=v(W, 2, CAP, C, BF16),
        acc=v(R, C, F32),
        self_t=v(C, R, F32),
        cot_t=v(C, R, F32),
        invs=v(16, R, F32),
        stat=v(8, R, F32),
        stats=v(N, 8, R, F32),
        emb=v(R, C, BF16),
        gp=v(C, R, BF16),
        gps=v(C, R, BF16),
        gprows=v(N, C, U, BF16),
        gsend=v(W, C, CAP, BF16),
        gret=v(W, C, CAP, BF16),
        yacc=v(C, R, F32),
        y=v(C, R, BF16),
        yrows=v(N, C, U, BF16),
        msg_t=v(D, U, BF16),
        gh=v(D, U, BF16),
        ghc=v(N, C, U, BF16),
        gf=v(D, U, F32),
        gfb=v(D, U, BF16),
        gfc=v(N, C, U, BF16),
        gc=v(2, C, D, BF16),
        gc_in=v(W, 2, z.red_rows, z.red_lanes, BF16),
        gc_sum=v(2, C, D, BF16),
        gn=v(1, C, D, BF16),
        gn_in=v(W, 1, z.red_rows, z.red_lanes, BF16),
        gn_sum=v(1, C, D, BF16),
        gcb=v(8, C, F32),
        gcb_in=v(W, 8, C, F32),
        gnb=v(8, C, F32),
        gnb_in=v(W, 8, C, F32),
    )
    sems = {}
    for name, count in dict(
        nw=N, nwf=N, nb=N, wt=N, wtf=N, st=N, gp_n=N, y_n=N, gh_n=N, gf_n=N,
        z_w=W, gr_w=W, rsc=W, agc=W, rsn=W, agn=W, bc=W, bn=W,
    ).items():
        sems[name + "_s"] = pltpu.SemaphoreType.DMA((count,))
        sems[name + "_r"] = pltpu.SemaphoreType.DMA((count,))
    sems["load"] = pltpu.SemaphoreType.DMA((10,))
    sems["store"] = pltpu.SemaphoreType.DMA((6,))
    return bufs, sems


class Refs:
    pass


def kernel(z, names, *refs):
    g = Refs()
    for name, ref in zip(names, refs):
        setattr(g, name, ref)
    R, D, C, W, N, U, CAP = z.rows, z.width, z.cols, z.wide, z.narrow, z.part, z.cap
    CH = z.chunk
    half = D // 2
    me_w, me_n = lax.axis_index("wide"), lax.axis_index("narrow")
    core = lax.rem(me_w, 2)
    sibling = me_w + 1 - 2 * core

    def loop(count, body, start=0):
        def step(i, carry):
            body(i)
            return carry

        lax.fori_loop(start, count, step, 0)

    def ahead_n(d):
        return lax.rem(me_n + d, N)

    def behind_n(d):
        return lax.rem(me_n - d + N, N)

    def ahead_w(d):
        return lax.rem(me_w + d, W)

    def behind_w(d):
        return lax.rem(me_w - d + W, W)

    def remote(name, d, src, dst, axis, peer):
        return pltpu.make_async_remote_copy(
            src_ref=src,
            dst_ref=dst,
            send_sem=getattr(g, name + "_s").at[d],
            recv_sem=getattr(g, name + "_r").at[d],
            device_id={axis: peer},
            device_id_type=MESH,
        )

    def nw_copy(d):
        return remote("nw", d, g.nw_in.at[at(core, half)], g.nwfull.at[me_n, at(core, half)], "narrow", ahead_n(d))

    def nw_arrive(d):
        s = behind_n(d)
        return remote("nw", d, g.nwfull.at[s, at(core, half)], g.nwfull.at[s, at(core, half)], "narrow", s)

    def nw_forward(d):
        s = behind_n(d)
        return remote("nwf", d, g.nwfull.at[s, at(core, half)], g.nwfull.at[s, at(core, half)], "wide", sibling)

    def nb_copy(d):
        return remote("nb", d, g.nbfull.at[me_n], g.nbfull.at[me_n], "narrow", ahead_n(d))

    def wt_copy(d):
        return remote("wt", d, g.comb_in.at[at(core, D)], g.wfull.at[me_n, at(core, D)], "narrow", ahead_n(d))

    def wt_arrive(d):
        s = behind_n(d)
        return remote("wt", d, g.wfull.at[s, at(core, D)], g.wfull.at[s, at(core, D)], "narrow", s)

    def wt_forward(d):
        s = behind_n(d)
        return remote("wtf", d, g.wfull.at[s, at(core, D)], g.wfull.at[s, at(core, D)], "wide", sibling)

    def z_copy(d):
        peer = ahead_w(d)
        return remote("z_w", d, g.zsend.at[peer], g.ztab.at[me_w], "wide", peer)

    def stat_copy(d):
        return remote("st", d, g.stat, g.stats.at[me_n], "narrow", ahead_n(d))

    def gp_copy(d):
        s = ahead_n(d)
        return remote("gp_n", d, g.gp.at[:, at(s, U)], g.gprows.at[me_n], "narrow", s)

    def ret_copy(d):
        peer = ahead_w(d)
        return remote("gr_w", d, g.gsend.at[peer], g.gret.at[me_w], "wide", peer)

    def y_copy(d):
        s = ahead_n(d)
        return remote("y_n", d, g.y.at[:, at(s, U)], g.yrows.at[me_n], "narrow", s)

    def gh_copy(d):
        s = ahead_n(d)
        return remote("gh_n", d, g.gh.at[at(s, C)], g.ghc.at[me_n], "narrow", s)

    def gf_copy(d):
        s = ahead_n(d)
        return remote("gf_n", d, g.gfb.at[at(s, C)], g.gfc.at[me_n], "narrow", s)

    def red_block(w):
        down, across = lax.rem(w, z.red_down), w // z.red_down
        return (slice(None), at(down, z.red_rows), at(across, z.red_lanes))

    def rs_copy(name, src, dst, d):
        peer = ahead_w(d)
        return remote(name, d, src.at[red_block(peer)], dst.at[me_w], "wide", peer)

    def ag_copy(name, ref, d):
        mine = red_block(me_w)
        return remote(name, d, ref.at[mine], ref.at[mine], "wide", ahead_w(d))

    def bias_copy(name, src, dst, d):
        return remote(name, d, src, dst.at[me_w], "wide", ahead_w(d))

    loads = [
        (g.feats_in, g.feats),
        (g.nw_in, g.nwfull.at[me_n]),
        (g.comb_in, g.wfull.at[me_n]),
        (g.slot_in, g.slot),
        (g.mask_in, g.mask),
        (g.visit_in, g.visit),
        (g.send_in, g.send),
        (g.cot_in, g.cot),
        (g.nb_in, g.nbfull.at[me_n]),
        (g.cb_in, g.cb),
    ]

    def load(i):
        return pltpu.make_async_copy(loads[i][0], loads[i][1], g.load.at[i])

    barrier = pltpu.get_barrier_semaphore()
    loop(W, lambda d: pl.semaphore_signal(barrier, inc=1, device_id={"wide": ahead_w(d)}, device_id_type=MESH), 1)
    loop(N, lambda d: pl.semaphore_signal(barrier, inc=1, device_id={"narrow": ahead_n(d)}, device_id_type=MESH), 1)
    order = (8, 3, 4, 5, 0, 1, 2, 6, 7, 9)
    for i in order:
        load(i).start()
    pl.semaphore_wait(barrier, W - 1 + N - 1)
    loop(N, lambda d: nw_copy(d).start(), 1)
    load(8).wait()
    loop(N, lambda d: nb_copy(d).start(), 1)

    for i in (3, 4, 5):
        load(i).wait()
    K = z.slots
    shift = CAP.bit_length() - 1

    def fill(i):
        rows = at(i, CH)
        g.code[rows, :] = jnp.zeros((CH, 128), I32)
        g.wts[rows, :] = jnp.zeros((CH, 128), F32)
        g.code[rows, 0:K] = g.slot[rows, :]
        g.code[rows, 64 : 64 + K] = g.slot[rows, :]
        weight = (g.mask[rows, :] * g.visit[rows, :]).astype(F32)
        g.wts[rows, 0:K] = weight
        g.wts[rows, 64 : 64 + K] = weight

    loop(R // CH, fill)

    lane = lax.broadcasted_iota(I32, (8, 128), 1)
    sub = lax.broadcasted_iota(I32, (8, 128), 0)
    half_lane = jnp.where(lane >= 64, 1, 0)
    place = [sub == 2 * j + half_lane for j in range(4)]
    place_b = [jnp.where(m, 1.0, 0.0) for m in place]
    place_b = [jnp.concatenate([m, m], axis=0).astype(BF16) for m in place_b]
    low_row = lax.broadcasted_iota(I32, (CAP, 128), 0).astype(F32).astype(BF16)

    def count_group(i):
        start = pl.multiple_of(i * 16, 16)
        outs = []
        for p in range(2):
            rows = pl.ds(pl.multiple_of(start + 8 * p, 8), 8)
            code, weight = g.code[rows, :], g.wts[rows, :]
            high, low = code >> shift, (code & (CAP - 1)).astype(F32)
            left = []
            for h in range(0, z.blocks, 2):
                pair = [jnp.where(high == h + q, weight, 0.0) for q in range(2)]
                pair = jnp.concatenate(pair, axis=0).astype(BF16)
                left.append(jnp.concatenate([pair * place_b[j] for j in range(4)], axis=1))
            left = jnp.concatenate(left, axis=0)
            right = []
            for j in range(4):
                row = jnp.sum(jnp.where(place[j], low, 0.0), axis=0, keepdims=True)
                row = jnp.broadcast_to(row.astype(BF16), (CAP, 128))
                right.append(jnp.where(low_row == row, jnp.ones((), BF16), jnp.zeros((), BF16)))
            outs.append(mm_nt(left, jnp.concatenate(right, axis=1)))
        for h in range(z.blocks):
            block = [out[h * 8 : h * 8 + 8] for out in outs]
            g.counts[h, pl.ds(start, 16), :] = jnp.concatenate(block, axis=0).astype(BF16)

    UNROLL = 4
    groups = R // 16 // UNROLL

    def count_groups(first, last):
        def body(i):
            for q in range(UNROLL):
                count_group(i * UNROLL + q)

        loop(last, body, first)

    def hidden(s):
        def body(i):
            rows = at(i, CH)
            value = mm(g.feats[rows, :], g.nwfull[s]) + g.nbfull[s, 0:1, :]
            value = jnp.maximum(value, 0.0)
            top = value.astype(BF16)
            rest = (value - top.astype(F32)).astype(BF16)
            g.msg[rows, at(s, C)] = top
            weight = g.wfull[me_n, pl.ds(pl.multiple_of(D + s * C, C), C), :]
            g.zacc[rows, :] += mm(top, weight) + mm(rest, weight)

        loop(R // CH, body)

    def zero(i):
        g.zacc[at(i, CH), :] = jnp.zeros((CH, C), F32)

    loop(R // CH, zero)
    for i in (0, 1, 2):
        load(i).wait()
    hidden(me_n)

    load(6).wait()

    def select(d):
        r = ahead_w(d)
        which = lax.broadcasted_iota(I32, (CAP, W), 1)
        col = jnp.sum(jnp.where(which == r, g.send[...], 0), axis=1, keepdims=True)
        place_u = lax.broadcasted_iota(I32, (CAP, R), 1)
        g.sel[r] = jnp.where(place_u == col, 1.0, 0.0).astype(BF16)

    loop(W, select, 1)

    per = groups // N if groups >= N else 0
    for d in range(1, N):
        count_groups((d - 1) * per, d * per)
        nw_arrive(d).wait_recv()
        nw_forward(d).start()
    loop(N, lambda d: wt_copy(d).start(), 1)
    count_groups((N - 1) * per, groups)

    def take(d):
        s = behind_n(d)
        nw_forward(d).wait_recv()
        nb_copy(d).wait_recv()
        hidden(s)

    loop(N, take, 1)

    def split_z(i):
        rows = at(i, CH)
        value = g.zacc[rows, :]
        top = value.astype(BF16)
        g.zhi[rows, :] = top
        g.zlo[rows, :] = (value - top.astype(F32)).astype(BF16)

    loop(R // CH, split_z)

    def send_z(d):
        peer = ahead_w(d)
        g.zsend[peer, 0] = mm(g.sel[peer], g.zhi[...]).astype(BF16)
        g.zsend[peer, 1] = mm(g.sel[peer], g.zlo[...]).astype(BF16)
        z_copy(d).start()

    loop(W, send_z, 1)

    load(7).wait()
    load(9).wait()

    def own_part(i):
        rows = at(i, CH)
        value = mm(g.feats[rows, :], g.wfull[me_n, 0:D, :]) + g.cb[0:1, :]
        g.self_t[:, rows] = value.T
        g.cot_t[:, rows] = g.cot[rows, :].astype(F32).T
        total = jnp.zeros((CH, C), F32)
        for h in range(z.local):
            part = slice(h * CAP, (h + 1) * CAP)
            block = g.counts[h, rows, :]
            total += mm(block, g.zhi[part, :]) + mm(block, g.zlo[part, :])
        g.acc[rows, :] = total

    loop(R // CH, own_part)
    ones = jnp.ones((16, 128), BF16)
    g.invs[...] = 2.0 / mm_nt(ones, g.wts[...].astype(BF16))

    def mine_t(i):
        cols = at(i, C)
        g.msg_t[cols, :] = g.msg[at(me_n, U), cols].astype(F32).T.astype(BF16)

    loop(D // C, mine_t)

    def take_z(d):
        s = behind_w(d)
        z_copy(d).wait_recv()

        def body(i):
            rows = at(i, CH)
            block = g.counts[z.local + s, rows, :]
            g.acc[rows, :] += mm(block, g.ztab[s, 0]) + mm(block, g.ztab[s, 1])

        loop(R // CH, body)

    loop(W, take_z, 1)

    which8 = lax.broadcasted_iota(I32, (8, CH), 0)

    def activate(i):
        rows = at(i, CH)
        pre = g.acc[rows, :].T * g.invs[0:1, rows] + g.self_t[:, rows]
        g.self_t[:, rows] = pre
        act = jnp.maximum(pre, 0.0)
        squares = jnp.sum(act * act, axis=0, keepdims=True)
        inner = jnp.sum(act * g.cot_t[:, rows], axis=0, keepdims=True)
        g.stat[:, rows] = jnp.where(which8 == 0, squares, jnp.where(which8 == 1, inner, 0.0))

    loop(R // CH, activate)
    loop(N, lambda d: stat_copy(d).start(), 1)
    loop(N, lambda d: stat_copy(d).wait_recv(), 1)
    g.stats[me_n] = g.stat[...]

    def norms(rows):
        total = g.stats[0, :, rows]
        for s in range(1, N):
            total += g.stats[s, :, rows]
        return lax.rsqrt(total[0:1] / D + EPSILON), total[1:2]

    def grad_act(i):
        rows = at(i, CH)
        inv, inner = norms(rows)
        pre = g.self_t[:, rows]
        act = jnp.maximum(pre, 0.0)
        grad = g.cot_t[:, rows] * inv - act * (inner * (inv * inv * inv) / D)
        grad = jnp.where(pre > 0, grad, 0.0)
        g.gp[:, rows] = grad.astype(BF16)
        g.gps[:, rows] = (grad * g.invs[0:1, rows]).astype(BF16)

    loop(R // CH, grad_act)
    loop(N, lambda d: gp_copy(d).start(), 1)

    def send_ret(d):
        peer = ahead_w(d)
        g.gsend[peer] = mm(g.gps[...], g.counts[z.local + peer]).astype(BF16)
        ret_copy(d).start()

    loop(W, send_ret, 1)

    join = max(1, 128 // CAP)
    for h in range(0, z.local, join):
        parts = [mm(g.gps[...], g.counts[h + q]) for q in range(join)]
        parts = jnp.concatenate(parts, axis=1) if join > 1 else parts[0]
        g.yacc[:, h * CAP : (h + join) * CAP] = parts

    def embed(i):
        rows = at(i, CH)
        inv, _ = norms(rows)
        value = jnp.maximum(g.self_t[:, rows], 0.0) * inv
        g.emb[rows, :] = value.T.astype(BF16)

    loop(R // CH, embed)
    emb_store = pltpu.make_async_copy(g.emb, g.emb_out, g.store.at[0])
    emb_store.start()

    def pass_weights(d):
        wt_arrive(d).wait_recv()
        wt_forward(d).start()

    loop(N, pass_weights, 1)

    LW = min(512, D)

    def grad_self(i):
        lanes = at(i, LW)
        g.gc[0, :, lanes] = mm(g.gp[...], g.feats[:, lanes]).astype(BF16)

    loop(D // LW, grad_self)
    ones_r = jnp.ones((8, R), BF16)
    g.gcb[...] = mm_nt(ones_r, g.gp[...])

    g.gprows[me_n] = g.gp[:, at(me_n, U)]

    def take_ret(d):
        s = behind_w(d)
        ret_copy(d).wait_recv()

        def body(i):
            lanes = at(i, CH)
            g.yacc[:, lanes] += mm(g.gret[s], g.sel[s, :, lanes])

        loop(R // CH, body)

    loop(W, take_ret, 1)

    def round_y(i):
        lanes = at(i, CH)
        g.y[:, lanes] = g.yacc[:, lanes].astype(BF16)

    loop(R // CH, round_y)
    loop(N, lambda d: y_copy(d).start(), 1)
    g.yrows[me_n] = g.y[:, at(me_n, U)]

    def grad_pool(i):
        lanes = at(i, LW)
        g.gc[1, :, lanes] = mm(g.y[...], g.msg[:, lanes]).astype(BF16)

    loop(D // LW, grad_pool)
    loop(W, lambda d: bias_copy("bc", g.gcb, g.gcb_in, d).start(), 1)
    loop(W, lambda d: rs_copy("rsc", g.gc, g.gc_in, d).start(), 1)

    loop(N, lambda d: gp_copy(d).wait_recv(), 1)
    loop(N, lambda d: wt_forward(d).wait_recv(), 1)

    def self_rows(i):
        rows = at(i, CH)
        total = jnp.zeros((CH, U), F32)
        for s in range(N):
            total += mm(g.wfull[s, rows, :], g.gprows[s])
        g.gf[rows, :] = total

    loop(D // CH, self_rows)
    loop(N, lambda d: y_copy(d).wait_recv(), 1)

    def hidden_rows(i):
        rows = at(i, CH)
        wrows = pl.ds(pl.multiple_of(D + i * CH, CH), CH)
        total = jnp.zeros((CH, U), F32)
        for s in range(N):
            total += mm(g.wfull[s, wrows, :], g.yrows[s])
        g.gh[rows, :] = jnp.where(g.msg_t[rows, :] > 0, total, 0.0).astype(BF16)

    loop(D // CH, hidden_rows)
    loop(N, lambda d: gh_copy(d).start(), 1)
    g.ghc[me_n] = g.gh[at(me_n, C), :]

    def feature_rows(i):
        rows = at(i, CH)
        total = g.gf[rows, :]
        for s in range(N):
            total += mm(g.nwfull[s, rows, :], g.gh[s * C : (s + 1) * C, :])
        g.gfb[rows, :] = total.astype(BF16)

    loop(D // CH, feature_rows)
    loop(N, lambda d: gf_copy(d).start(), 1)
    g.gfc[me_n] = g.gfb[at(me_n, C), :]

    def reduce_sum(own, arrived, out):
        mine = red_block(me_w)
        total = own[mine].astype(F32)

        def body(d, total):
            return total + arrived[behind_w(d)].astype(F32)

        out[mine] = lax.fori_loop(1, W, body, total).astype(BF16)

    loop(W, lambda d: rs_copy("rsc", g.gc, g.gc_in, d).wait_recv(), 1)
    reduce_sum(g.gc, g.gc_in, g.gc_sum)
    loop(W, lambda d: ag_copy("agc", g.gc_sum, d).start(), 1)

    loop(N, lambda d: gh_copy(d).wait_recv(), 1)

    def grad_neigh(i):
        lanes = at(i, LW)
        total = jnp.zeros((C, LW), F32)
        for s in range(N):
            total += mm(g.ghc[s], g.feats[s * U : (s + 1) * U, lanes])
        g.gn[0, :, lanes] = total.astype(BF16)

    loop(D // LW, grad_neigh)
    total = jnp.zeros((8, C), F32)
    ones_u = jnp.ones((8, U), BF16)
    for s in range(N):
        total += mm_nt(ones_u, g.ghc[s])
    g.gnb[...] = total
    loop(W, lambda d: rs_copy("rsn", g.gn, g.gn_in, d).start(), 1)
    loop(W, lambda d: bias_copy("bn", g.gnb, g.gnb_in, d).start(), 1)

    loop(N, lambda d: gf_copy(d).wait_recv(), 1)
    gf_store = pltpu.make_async_copy(g.gfc, g.gf_out, g.store.at[1])
    gf_store.start()

    loop(W, lambda d: rs_copy("rsn", g.gn, g.gn_in, d).wait_recv(), 1)
    reduce_sum(g.gn, g.gn_in, g.gn_sum)
    loop(W, lambda d: ag_copy("agn", g.gn_sum, d).start(), 1)

    def bias_sum(name, own, arrived):
        loop(W, lambda d: bias_copy(name, own, arrived, d).wait_recv(), 1)
        loop(W, lambda d: bias_copy(name, own, arrived, d).wait_send(), 1)

        def body(d, total):
            return total + arrived[behind_w(d)]

        own[...] = lax.fori_loop(1, W, body, own[...])

    bias_sum("bc", g.gcb, g.gcb_in)
    bias_sum("bn", g.gnb, g.gnb_in)

    def ag_arrive(name, ref, d):
        theirs = red_block(behind_w(d))
        return remote(name, d, ref.at[theirs], ref.at[theirs], "wide", behind_w(d))

    loop(W, lambda d: ag_arrive("agc", g.gc_sum, d).wait_recv(), 1)
    stores = [
        emb_store,
        gf_store,
        pltpu.make_async_copy(g.gc_sum, g.gc_out, g.store.at[2]),
        pltpu.make_async_copy(g.gcb, g.gcb_out, g.store.at[3]),
        pltpu.make_async_copy(g.gnb, g.gnb_out, g.store.at[4]),
        pltpu.make_async_copy(g.gn_sum, g.gn_out, g.store.at[5]),
    ]
    for store in stores[2:5]:
        store.start()
    loop(W, lambda d: ag_arrive("agn", g.gn_sum, d).wait_recv(), 1)
    stores[5].start()

    def drain_n(d):
        for copy in (nw_copy, nw_forward, nb_copy, wt_copy, wt_forward, stat_copy, gp_copy, y_copy, gh_copy, gf_copy):
            copy(d).wait_send()

    def drain_w(d):
        z_copy(d).wait_send()
        ret_copy(d).wait_send()
        rs_copy("rsc", g.gc, g.gc_in, d).wait_send()
        ag_copy("agc", g.gc_sum, d).wait_send()
        rs_copy("rsn", g.gn, g.gn_in, d).wait_send()
        ag_copy("agn", g.gn_sum, d).wait_send()

    loop(N, drain_n, 1)
    loop(W, drain_w, 1)
    for store in stores:
        store.wait()


def shards(wide, narrow, node_feats, neigh_weight, neigh_bias, combine_weight, combine_bias, cotangent,
           neighbour_slot, neighbour_mask, visit_count, send_rows):
    z = Sizes(node_feats, neigh_weight, send_rows, neighbour_slot, wide, narrow)
    R, D, C, W, N, U = z.rows, z.width, z.cols, z.wide, z.narrow, z.part
    bufs, sems = scratch(z)
    names = NAMES_IN + NAMES_OUT + list(bufs) + list(sems)
    rows8 = lambda b: jnp.broadcast_to(b.astype(F32)[None, :], (8, C))
    outs = (
        jax.ShapeDtypeStruct((R, C), BF16),
        jax.ShapeDtypeStruct((N, C, U), BF16),
        jax.ShapeDtypeStruct((1, C, D), BF16),
        jax.ShapeDtypeStruct((2, C, D), BF16),
        jax.ShapeDtypeStruct((8, C), F32),
        jax.ShapeDtypeStruct((8, C), F32),
    )
    emb, gf, gn, gc, gnb, gcb = pl.pallas_call(
        functools.partial(kernel, z, names),
        out_shape=outs,
        in_specs=[pl.BlockSpec(memory_space=pl.ANY)] * len(NAMES_IN),
        out_specs=[pl.BlockSpec(memory_space=pl.ANY)] * len(NAMES_OUT),
        scratch_shapes=list(bufs.values()) + list(sems.values()),
        compiler_params=pltpu.CompilerParams(
            collective_id=0, has_side_effects=True, vmem_limit_bytes=60 * 2**20
        ),
        cost_estimate=pl.CostEstimate(flops=2 * 10**10, bytes_accessed=2 * 10**7, transcendentals=0),
        name="layer",
    )(
        node_feats, neigh_weight, rows8(neigh_bias), combine_weight, rows8(combine_bias), cotangent,
        neighbour_slot, neighbour_mask, visit_count, send_rows.T,
    )
    grad_features = gf.transpose(0, 2, 1).reshape(R, C).astype(F32)
    grad_neigh = gn[0].T.astype(F32)
    grad_combine = gc.transpose(0, 2, 1).reshape(2 * D, C).astype(F32)
    return emb, grad_features, grad_neigh, gnb[0], grad_combine, gcb[0]


def solution(mesh):
    placed = (
        P("wide", None),
        P(None, "narrow"),
        P("narrow"),
        P(None, "narrow"),
        P("narrow"),
        P("wide", "narrow"),
        P("wide", None),
        P("wide", None),
        P("wide", None),
        P("wide", None),
    )
    return jax.shard_map(
        functools.partial(shards, mesh.shape["wide"], mesh.shape["narrow"]),
        mesh=mesh,
        in_specs=placed,
        out_specs=(
            P("wide", "narrow"),
            P("wide", "narrow"),
            P(None, "narrow"),
            P("narrow"),
            P(None, "narrow"),
            P("narrow"),
        ),
        check_vma=False,
    )
```

time: 356 us -> 167 us (0.47)
  the two profiles are of different devices: /device:TPU:0 before, /device:TPU:29 now
where the time goes in v2:
time: 167 us; the launch traced here: 166 us
  Pallas kernels  148 us (89%)
  local copies, waits for them, and re-layouts  15.6 us (9%)
    pallas_call x1, Pallas kernels, shards(): pl.pallas_call(functools.partial(kernel, z, names), out_shape=outs, in_sp...  148 us
    unnamed x18, local copies, waits for them, and re-layouts  8.77 us

profile of v2, /device:TPU:29, one launch (start us, length us, event | category | flops | bytes accessed | tf_op | source)
XLA Modules:
  0.0 166.4 jit_solution(14352880729572439679)
XLA Ops:
  0.6 0.0 copy-start.3
  0.6 0.0 copy-start.4
  0.7 0.0 copy-start.5
  0.7 2.0 %copy.22.refs_6_ = s32[1024,50]{1,0:T(8,128)} copy(s32[1024,50]{0,1:T(8,128)} %param.16) | data formatting | bytes 409600 | tf_op args[6]
  2.6 1.9 %copy.23.refs_7_ = s32[1024,50]{1,0:T(8,128)} copy(s32[1024,50]{0,1:T(8,128)} %param.17) | data formatting | bytes 409600 | tf_op args[7]
  4.6 1.9 %copy.24.refs_8_ = s32[1024,50]{1,0:T(8,128)} copy(s32[1024,50]{0,1:T(8,128)} %param.18) | data formatting | bytes 409600 | tf_op args[8]
  6.5 0.0 copy-done.3
  6.5 0.8 copy.21
  7.3 0.0 copy-done.4
  7.3 0.6 broadcast_in_dim.4.refs_2_
  7.9 0.0 copy-done.5
  7.9 0.6 broadcast_in_dim.5.refs_4_
  8.5 148.5 %layer.1 = (bf16[1024,256]{1,0:T(8,128)(2,1)}, bf16[4,256,256]{2,1,0:T(8,128)(2,1)}, bf16[1,256,1024]{2,1,0:T(8,128)(2,1)}, bf16[2,256,1024]{2,1,0:T(8,128)(2,1)}, f32[8,256]{1,0:T(8,128)}, /*index=5*/f32[8,256]{1,0:T(8,128)}) custom-call(bf16[1024,1024]{1,0:T(8,128)(2,1)} %refs_0_.1, bf16[1024,256]{1,0:T(8,128)(2,1)} %refs_1_.1, ...), custom_call_target="tpu_custom_call" | custom-call | flops 20000000000 | bytes 20000000 | tf_op jit(solution)/shard_map/layer/pallas_call | solution.py:659
  157.0 1.5 convert_bitcast_fusion
  158.5 0.0 copy-start.1
  158.5 1.8 %copy.26 = f32[2,1024,256]{2,1,0:T(8,128)} copy(f32[2,1024,256]{1,2,0:T(8,128)S(1)} %convert_bitcast_fusion) | data formatting | bytes 4194304 | tf_op jit(solution)/shard_map/convert_element_type | solution.py:676
  160.3 0.0 copy-start
  160.3 0.0 copy-done.1
  160.3 0.1 convert_bitcast_fusion.2
  160.4 1.3 copy.25
  161.7 0.0 copy-start.2
  161.7 0.0 copy-done
  161.7 0.1 convert_bitcast_fusion.1
  161.8 1.3 copy.27
  163.1 1.3 slice.6
  164.4 1.3 slice.7
  165.6 0.0 copy-done.2
  165.6 0.8 copy.29
Async XLA Ops:
  0.6 5.9 %copy-start.3 = (s32[8,256]{1,0:T(8,128)S(1)}, s32[8,256]{1,0:T(8,128)}, u32[]{:S(2)}) copy-start(s32[8,256]{1,0:T(8,128)} %param.19) | copy-start | bytes 24580
  0.6 6.7 %copy-start.4 = (bf16[256]{0:T(256)(128)(2,1)S(1)}, bf16[256]{0:T(256)(128)(2,1)}, u32[]{:S(2)}) copy-start(bf16[256]{0:T(256)(128)(2,1)} %param.12) | copy-start | bytes 1540
  0.7 7.3 %copy-start.5 = (bf16[256]{0:T(256)(128)(2,1)S(1)}, bf16[256]{0:T(256)(128)(2,1)}, u32[]{:S(2)}) copy-start(bf16[256]{0:T(256)(128)(2,1)} %param.14) | copy-start | bytes 1540
  158.5 1.8 %copy-start.1 = (bf16[4,256,256]{2,1,0:T(8,128)(2,1)S(1)}, bf16[4,256,256]{2,1,0:T(8,128)(2,1)}, u32[]{:S(2)}) copy-start(bf16[4,256,256]{2,1,0:T(8,128)(2,1)} %get-tuple-element.13) | copy-start | bytes 1572868
  160.3 1.4 copy-start
  161.7 3.9 %copy-start.2 = (bf16[1024,256]{1,0:T(8,128)(2,1)S(1)}, bf16[1024,256]{1,0:T(8,128)(2,1)}, u32[]{:S(2)}) copy-start(bf16[1024,256]{1,0:T(8,128)(2,1)} %get-tuple-element.36) | copy-start | bytes 1572868

commit v3 on v2

--- a/solution.py
+++ b/solution.py
@@ -31,7 +31,7 @@
         self.rows, self.width = feats.shape
         self.cols = neigh.shape[1]
         self.cap = send.shape[1]
-        self.slots = slot.shape[1]
+        self.slots = slot.shape[0]
         self.wide, self.narrow = wide, narrow
         self.chunk = min(256, self.rows)
         self.part = self.rows // narrow
@@ -55,12 +55,12 @@
         nwfull=v(N, D, C, BF16),
         nbfull=v(N, 8, C, F32),
         wfull=v(N, 2 * D, C, BF16),
-        cb=v(8, C, F32),
         cot=v(R, C, BF16),
-        slot=v(R, z.slots, I32),
-        mask=v(R, z.slots, I32),
-        visit=v(R, z.slots, I32),
-        send=v(CAP, W, I32),
+        slot=v(z.slots, R, I32),
+        mask=v(z.slots, R, I32),
+        visit=v(z.slots, R, I32),
+        send=v(W, CAP, I32),
+        send_t=v(CAP, W, I32),
         code=v(R, 128, I32),
         wts=v(R, 128, F32),
         counts=v(z.blocks, R, CAP, BF16),
@@ -105,11 +105,11 @@
     )
     sems = {}
     for name, count in dict(
-        nw=N, nwf=N, nb=N, wt=N, wtf=N, st=N, gp_n=N, y_n=N, gh_n=N, gf_n=N,
+        nw=N, nwp=(N, W // 2), nwf=N, nb=N, wt=N, wtf=N, st=N, gp_n=N, y_n=N, gh_n=N, gf_n=N,
         z_w=W, gr_w=W, rsc=W, agc=W, rsn=W, agn=W, bc=W, bn=W,
     ).items():
-        sems[name + "_s"] = pltpu.SemaphoreType.DMA((count,))
-        sems[name + "_r"] = pltpu.SemaphoreType.DMA((count,))
+        sems[name + "_s"] = pltpu.SemaphoreType.DMA(count if isinstance(count, tuple) else (count,))
+        sems[name + "_r"] = pltpu.SemaphoreType.DMA(count if isinstance(count, tuple) else (count,))
     sems["load"] = pltpu.SemaphoreType.DMA((10,))
     sems["store"] = pltpu.SemaphoreType.DMA((6,))
     return bufs, sems
@@ -149,26 +149,30 @@
     def behind_w(d):
         return lax.rem(me_w - d + W, W)
 
-    def remote(name, d, src, dst, axis, peer):
+    def remote(name, index, src, dst, axis, peer):
         return pltpu.make_async_remote_copy(
             src_ref=src,
             dst_ref=dst,
-            send_sem=getattr(g, name + "_s").at[d],
-            recv_sem=getattr(g, name + "_r").at[d],
+            send_sem=getattr(g, name + "_s").at[index],
+            recv_sem=getattr(g, name + "_r").at[index],
             device_id={axis: peer},
             device_id_type=MESH,
         )
 
+    def share(w):
+        return at(lax.rem(w, 2) * (W // 2) + w // 2, D // W)
+
     def nw_copy(d):
-        return remote("nw", d, g.nw_in.at[at(core, half)], g.nwfull.at[me_n, at(core, half)], "narrow", ahead_n(d))
-
-    def nw_arrive(d):
-        s = behind_n(d)
-        return remote("nw", d, g.nwfull.at[s, at(core, half)], g.nwfull.at[s, at(core, half)], "narrow", s)
+        mine = share(me_w)
+        return remote("nw", d, g.nw_in.at[mine], g.nwfull.at[me_n, mine], "narrow", ahead_n(d))
+
+    def nw_pass(d, e):
+        part = g.nwfull.at[behind_n(d), share(me_w)]
+        return remote("nwp", (d, e), part, part, "wide", ahead_w(2 * e))
 
     def nw_forward(d):
-        s = behind_n(d)
-        return remote("nwf", d, g.nwfull.at[s, at(core, half)], g.nwfull.at[s, at(core, half)], "wide", sibling)
+        part = g.nwfull.at[behind_n(d), at(core, half)]
+        return remote("nwf", d, part, part, "wide", sibling)
 
     def nb_copy(d):
         return remote("nb", d, g.nbfull.at[me_n], g.nbfull.at[me_n], "narrow", ahead_n(d))
@@ -235,8 +239,6 @@
         (g.visit_in, g.visit),
         (g.send_in, g.send),
         (g.cot_in, g.cot),
-        (g.nb_in, g.nbfull.at[me_n]),
-        (g.cb_in, g.cb),
     ]
 
     def load(i):
@@ -245,12 +247,12 @@
     barrier = pltpu.get_barrier_semaphore()
     loop(W, lambda d: pl.semaphore_signal(barrier, inc=1, device_id={"wide": ahead_w(d)}, device_id_type=MESH), 1)
     loop(N, lambda d: pl.semaphore_signal(barrier, inc=1, device_id={"narrow": ahead_n(d)}, device_id_type=MESH), 1)
-    order = (8, 3, 4, 5, 0, 1, 2, 6, 7, 9)
+    order = (3, 4, 5, 0, 1, 2, 6, 7)
     for i in order:
         load(i).start()
     pl.semaphore_wait(barrier, W - 1 + N - 1)
     loop(N, lambda d: nw_copy(d).start(), 1)
-    load(8).wait()
+    g.nbfull[me_n] = jnp.broadcast_to(g.nb_in[...].astype(F32), (8, C))
     loop(N, lambda d: nb_copy(d).start(), 1)
 
     for i in (3, 4, 5):
@@ -262,9 +264,10 @@
         rows = at(i, CH)
         g.code[rows, :] = jnp.zeros((CH, 128), I32)
         g.wts[rows, :] = jnp.zeros((CH, 128), F32)
-        g.code[rows, 0:K] = g.slot[rows, :]
-        g.code[rows, 64 : 64 + K] = g.slot[rows, :]
-        weight = (g.mask[rows, :] * g.visit[rows, :]).astype(F32)
+        code = g.slot[:, rows].T
+        g.code[rows, 0:K] = code
+        g.code[rows, 64 : 64 + K] = code
+        weight = (g.mask[:, rows] * g.visit[:, rows]).astype(F32).T
         g.wts[rows, 0:K] = weight
         g.wts[rows, 64 : 64 + K] = weight
 
@@ -327,29 +330,34 @@
     def zero(i):
         g.zacc[at(i, CH), :] = jnp.zeros((CH, C), F32)
 
+    count_groups(0, groups // 4)
+    def pass_nw(d):
+        nw_copy(d).wait_recv()
+        loop(W // 2, lambda e: nw_pass(d, e).start(), 1)
+
+    loop(N, pass_nw, 1)
+    loop(N, lambda d: wt_copy(d).start(), 1)
     loop(R // CH, zero)
     for i in (0, 1, 2):
         load(i).wait()
     hidden(me_n)
-
     load(6).wait()
+    g.send_t[...] = g.send[...].T
 
     def select(d):
         r = ahead_w(d)
         which = lax.broadcasted_iota(I32, (CAP, W), 1)
-        col = jnp.sum(jnp.where(which == r, g.send[...], 0), axis=1, keepdims=True)
+        col = jnp.sum(jnp.where(which == r, g.send_t[...], 0), axis=1, keepdims=True)
         place_u = lax.broadcasted_iota(I32, (CAP, R), 1)
         g.sel[r] = jnp.where(place_u == col, 1.0, 0.0).astype(BF16)
 
     loop(W, select, 1)
-
-    per = groups // N if groups >= N else 0
-    for d in range(1, N):
-        count_groups((d - 1) * per, d * per)
-        nw_arrive(d).wait_recv()
+    count_groups(groups // 4, groups // 2)
+    def forward_nw(d):
+        loop(W // 2, lambda e: nw_pass(d, e).wait_recv(), 1)
         nw_forward(d).start()
-    loop(N, lambda d: wt_copy(d).start(), 1)
-    count_groups((N - 1) * per, groups)
+
+    loop(N, forward_nw, 1)
 
     def take(d):
         s = behind_n(d)
@@ -376,12 +384,12 @@
 
     loop(W, send_z, 1)
 
+    count_groups(groups // 2, groups)
     load(7).wait()
-    load(9).wait()
 
     def own_part(i):
         rows = at(i, CH)
-        value = mm(g.feats[rows, :], g.wfull[me_n, 0:D, :]) + g.cb[0:1, :]
+        value = mm(g.feats[rows, :], g.wfull[me_n, 0:D, :]) + g.cb_in[...].astype(F32)
         g.self_t[:, rows] = value.T
         g.cot_t[:, rows] = g.cot[rows, :].astype(F32).T
         total = jnp.zeros((CH, C), F32)
@@ -624,6 +632,7 @@
     stores[5].start()
 
     def drain_n(d):
+        loop(W // 2, lambda e: nw_pass(d, e).wait_send(), 1)
         for copy in (nw_copy, nw_forward, nb_copy, wt_copy, wt_forward, stat_copy, gp_copy, y_copy, gh_copy, gf_copy):
             copy(d).wait_send()
 
@@ -641,13 +650,21 @@
         store.wait()
 
 
+def finish(emb_in, gf, gn, gc, gnb, gcb, emb_out, gf_out, gn_out, gc_out, gnb_out, gcb_out):
+    gf_out[...] = gf[0].astype(F32).T
+    gn_out[...] = gn[0].astype(F32).T
+    for i in range(2):
+        gc_out[i] = gc[i].astype(F32).T
+    gnb_out[...] = gnb[0:1, :]
+    gcb_out[...] = gcb[0:1, :]
+
+
 def shards(wide, narrow, node_feats, neigh_weight, neigh_bias, combine_weight, combine_bias, cotangent,
            neighbour_slot, neighbour_mask, visit_count, send_rows):
-    z = Sizes(node_feats, neigh_weight, send_rows, neighbour_slot, wide, narrow)
+    z = Sizes(node_feats, neigh_weight, send_rows, neighbour_slot.T, wide, narrow)
     R, D, C, W, N, U = z.rows, z.width, z.cols, z.wide, z.narrow, z.part
     bufs, sems = scratch(z)
     names = NAMES_IN + NAMES_OUT + list(bufs) + list(sems)
-    rows8 = lambda b: jnp.broadcast_to(b.astype(F32)[None, :], (8, C))
     outs = (
         jax.ShapeDtypeStruct((R, C), BF16),
         jax.ShapeDtypeStruct((N, C, U), BF16),
@@ -659,7 +676,9 @@
     emb, gf, gn, gc, gnb, gcb = pl.pallas_call(
         functools.partial(kernel, z, names),
         out_shape=outs,
-        in_specs=[pl.BlockSpec(memory_space=pl.ANY)] * len(NAMES_IN),
+        in_specs=[
+            pl.BlockSpec(memory_space=pltpu.VMEM if name in ("nb_in", "cb_in") else pl.ANY) for name in NAMES_IN
+        ],
         out_specs=[pl.BlockSpec(memory_space=pl.ANY)] * len(NAMES_OUT),
         scratch_shapes=list(bufs.values()) + list(sems.values()),
         compiler_params=pltpu.CompilerParams(
@@ -668,13 +687,44 @@
         cost_estimate=pl.CostEstimate(flops=2 * 10**10, bytes_accessed=2 * 10**7, transcendentals=0),
         name="layer",
     )(
-        node_feats, neigh_weight, rows8(neigh_bias), combine_weight, rows8(combine_bias), cotangent,
-        neighbour_slot, neighbour_mask, visit_count, send_rows.T,
+        node_feats, neigh_weight, neigh_bias.reshape(1, C), combine_weight, combine_bias.reshape(1, C), cotangent,
+        neighbour_slot.T, neighbour_mask.T, visit_count.T, send_rows,
     )
-    grad_features = gf.transpose(0, 2, 1).reshape(R, C).astype(F32)
-    grad_neigh = gn[0].T.astype(F32)
-    grad_combine = gc.transpose(0, 2, 1).reshape(2 * D, C).astype(F32)
-    return emb, grad_features, grad_neigh, gnb[0], grad_combine, gcb[0]
+    Q = D // N
+    whole = pl.BlockSpec((8, C), lambda i: (0, 0))
+    line = pl.BlockSpec((1, C), lambda i: (0, 0))
+    emb, grad_features, grad_neigh, grad_combine, gnb, gcb = pl.pallas_call(
+        finish,
+        grid=(N,),
+        out_shape=(
+            jax.ShapeDtypeStruct((R, C), BF16),
+            jax.ShapeDtypeStruct((R, C), F32),
+            jax.ShapeDtypeStruct((D, C), F32),
+            jax.ShapeDtypeStruct((2, D, C), F32),
+            jax.ShapeDtypeStruct((1, C), F32),
+            jax.ShapeDtypeStruct((1, C), F32),
+        ),
+        in_specs=[
+            pl.BlockSpec(memory_space=pl.ANY),
+            pl.BlockSpec((1, C, U), lambda i: (i, 0, 0)),
+            pl.BlockSpec((1, C, Q), lambda i: (0, 0, i)),
+            pl.BlockSpec((2, C, Q), lambda i: (0, 0, i)),
+            whole,
+            whole,
+        ],
+        out_specs=[
+            pl.BlockSpec(memory_space=pl.ANY),
+            pl.BlockSpec((U, C), lambda i: (i, 0)),
+            pl.BlockSpec((Q, C), lambda i: (i, 0)),
+            pl.BlockSpec((2, Q, C), lambda i: (0, i, 0)),
+            line,
+            line,
+        ],
+        input_output_aliases={0: 0},
+        compiler_params=pltpu.CompilerParams(vmem_limit_bytes=16 * 2**20),
+        name="finish",
+    )(emb, gf, gn, gc, gnb, gcb)
+    return emb, grad_features, grad_neigh, gnb.reshape(C), grad_combine.reshape(2 * D, C), gcb.reshape(C)
 
 
 def solution(mesh):

time: 167 us -> 141 us (0.84)
  the two profiles are of different devices: /device:TPU:29 before, /device:TPU:25 now
where the time goes in v3:
time: 141 us; the launch traced here: 140 us
  Pallas kernels  131 us (93%)
  local copies, waits for them, and re-layouts  8.97 us (6%)
    pallas_call x1, Pallas kernels, shards(): pl.pallas_call(functools.partial(kernel, z, names), out_shape=outs, in_sp...  128 us
    unnamed x13, local copies, waits for them, and re-layouts  6.53 us

profile of v3, /device:TPU:25, one launch (start us, length us, event | category | flops | bytes accessed | tf_op | source)
XLA Modules:
  0.0 140.2 jit_solution(3751838601356008343)
XLA Ops:
  0.6 1.2 reshape.27.refs_2_
  1.9 1.2 reshape.28.refs_4_
  3.1 127.9 %layer.1 = (bf16[1024,256]{1,0:T(8,128)(2,1)}, bf16[4,256,256]{2,1,0:T(8,128)(2,1)}, bf16[1,256,1024]{2,1,0:T(8,128)(2,1)}, bf16[2,256,1024]{2,1,0:T(8,128)(2,1)}, f32[8,256]{1,0:T(8,128)}, /*index=5*/f32[8,256]{1,0:T(8,128)}) custom-call(bf16[1024,1024]{1,0:T(8,128)(2,1)} %refs_0_.1, bf16[1024,256]{1,0:T(8,128)(2,1)} %refs_1_.1, ...), custom_call_target="tpu_custom_call" | custom-call | flops 20000000000 | bytes 20000000 | tf_op jit(solution)/shard_map/layer/pallas_call | solution.py:676
  130.9 0.0 copy-start
  130.9 1.0 copy-done
  132.0 0.0 copy-start.1
  132.0 1.2 copy-done.1
  133.2 0.0 copy-start.2
  133.2 1.0 copy-done.2
  134.2 0.0 copy-start.3
  134.2 1.0 copy-done.3
  135.3 0.0 copy-start.4
  135.3 0.7 copy-done.4
  136.0 0.0 copy-start.5
  136.0 0.7 copy-done.5
  136.7 2.7 %finish.1 = (bf16[1024,256]{1,0:T(8,128)(2,1)S(1)}, f32[1024,256]{1,0:T(8,128)}, f32[1024,256]{1,0:T(8,128)}, f32[2,1024,256]{2,1,0:T(8,128)}, f32[1,256]{1,0:T(1,128)}, /*index=5*/f32[1,256]{1,0:T(1,128)}) custom-call(bf16[1024,256]{1,0:T(8,128)(2,1)S(1)} %copy-done, bf16[4,256,256]{2,1,0:T(8,128)(2,1)S(1)} %copy-done.2, ...), custom_call_target="tpu_custom_call", output_to_operand_aliasing={{0}: (0, {})} | custom-call | tf_op jit(solution)/shard_map/finish/pallas_call | solution.py:696
  139.4 0.8 copy.19
Async XLA Ops:
  130.9 1.0 copy-start
  132.0 1.2 copy-start.1
  133.2 1.0 copy-start.2
  134.2 1.0 copy-start.3
  135.3 0.7 copy-start.4
  136.0 0.7 copy-start.5

commit v4 on v3

--- a/solution.py
+++ b/solution.py
@@ -11,6 +11,7 @@
 F32 = jnp.float32
 BF16 = jnp.bfloat16
 I32 = jnp.int32
+I16 = jnp.int16
 MESH = pl.DeviceIdType.MESH
 
 
@@ -23,6 +24,8 @@
 
 
 def at(index, size):
+    if isinstance(index, int):
+        return slice(index * size, (index + 1) * size)
     return pl.ds(pl.multiple_of(index * size, size), size)
 
 
@@ -37,9 +40,10 @@
         self.part = self.rows // narrow
         self.local = self.rows // self.cap
         self.blocks = self.local + wide
-        self.red_rows = max(16, self.cols // wide)
-        self.red_down = self.cols // self.red_rows
-        self.red_across = wide // self.red_down
+        self.pairs = wide // 2
+        self.red_rows = max(16, self.cols // 2 // self.pairs)
+        self.red_down = self.cols // 2 // self.red_rows
+        self.red_across = self.pairs // self.red_down
         self.red_lanes = self.width // self.red_across
 
 
@@ -69,8 +73,12 @@
         zacc=v(R, C, F32),
         zhi=v(R, C, BF16),
         zlo=v(R, C, BF16),
-        zsend=v(W, 2, CAP, C, BF16),
-        ztab=v(W, 2, CAP, C, BF16),
+        zqa=v(R, C, BF16),
+        zqb=v(R, C, BF16),
+        zscale=v(8, C, F32),
+        zscales=v(W, 8, C, F32),
+        zsend=v(W, CAP, C, I16),
+        ztab=v(W, CAP, C, I16),
         acc=v(R, C, F32),
         self_t=v(C, R, F32),
         cot_t=v(C, R, F32),
@@ -93,10 +101,12 @@
         gfb=v(D, U, BF16),
         gfc=v(N, C, U, BF16),
         gc=v(2, C, D, BF16),
-        gc_in=v(W, 2, z.red_rows, z.red_lanes, BF16),
+        gc_half=v(2, C // 2, D, BF16),
+        gc_in=v(W // 2, 2, z.red_rows, z.red_lanes, BF16),
         gc_sum=v(2, C, D, BF16),
         gn=v(1, C, D, BF16),
-        gn_in=v(W, 1, z.red_rows, z.red_lanes, BF16),
+        gn_half=v(1, C // 2, D, BF16),
+        gn_in=v(W // 2, 1, z.red_rows, z.red_lanes, BF16),
         gn_sum=v(1, C, D, BF16),
         gcb=v(8, C, F32),
         gcb_in=v(W, 8, C, F32),
@@ -105,8 +115,8 @@
     )
     sems = {}
     for name, count in dict(
-        nw=N, nwp=(N, W // 2), nwf=N, nb=N, wt=N, wtf=N, st=N, gp_n=N, y_n=N, gh_n=N, gf_n=N,
-        z_w=W, gr_w=W, rsc=W, agc=W, rsn=W, agn=W, bc=W, bn=W,
+        nw=N, nwp=(N, W // 2), nwf=N, nb=N, wt=(2, N), wtp=(2, N), wtf=(2, N), st=N, gp_n=N, y_n=(2, N), gh_n=N, gf_n=N,
+        z_w=W, zs_w=W, gr_w=(2, W), hsc=1, rsc=W // 2, agc=W // 2, fwc=W // 2, hsn=1, rsn=W // 2, agn=W // 2, fwn=W // 2, bc=W, bn=W,
     ).items():
         sems[name + "_s"] = pltpu.SemaphoreType.DMA(count if isinstance(count, tuple) else (count,))
         sems[name + "_r"] = pltpu.SemaphoreType.DMA(count if isinstance(count, tuple) else (count,))
@@ -137,6 +147,10 @@
 
         lax.fori_loop(start, count, step, 0)
 
+    def sweep(count, body):
+        for i in range(count):
+            body(i)
+
     def ahead_n(d):
         return lax.rem(me_n + d, N)
 
@@ -177,21 +191,36 @@
     def nb_copy(d):
         return remote("nb", d, g.nbfull.at[me_n], g.nbfull.at[me_n], "narrow", ahead_n(d))
 
-    def wt_copy(d):
-        return remote("wt", d, g.comb_in.at[at(core, D)], g.wfull.at[me_n, at(core, D)], "narrow", ahead_n(d))
-
-    def wt_arrive(d):
-        s = behind_n(d)
-        return remote("wt", d, g.wfull.at[s, at(core, D)], g.wfull.at[s, at(core, D)], "narrow", s)
-
-    def wt_forward(d):
-        s = behind_n(d)
-        return remote("wtf", d, g.wfull.at[s, at(core, D)], g.wfull.at[s, at(core, D)], "wide", sibling)
+    step = (2, 4)
+
+    def wt_bit(k):
+        return lax.rem(me_w // step[k], 2)
+
+    def wt_partner(k):
+        return me_w + step[k] - 2 * step[k] * wt_bit(k)
+
+    def wt_rows(k):
+        return pl.ds(pl.multiple_of(k * D + (2 * core + wt_bit(k)) * (D // 4), D // 4), D // 4)
+
+    def wt_copy(k, d):
+        mine = wt_rows(k)
+        return remote("wt", (k, d), g.comb_in.at[mine], g.wfull.at[me_n, mine], "narrow", ahead_n(d))
+
+    def wt_pass(k, d):
+        part = g.wfull.at[behind_n(d), wt_rows(k)]
+        return remote("wtp", (k, d), part, part, "wide", wt_partner(k))
+
+    def wt_forward(k, d):
+        part = g.wfull.at[behind_n(d), pl.ds(pl.multiple_of(k * D + core * half, half), half)]
+        return remote("wtf", (k, d), part, part, "wide", sibling)
 
     def z_copy(d):
         peer = ahead_w(d)
         return remote("z_w", d, g.zsend.at[peer], g.ztab.at[me_w], "wide", peer)
 
+    def zscale_copy(d):
+        return remote("zs_w", d, g.zscale, g.zscales.at[me_w], "wide", ahead_w(d))
+
     def stat_copy(d):
         return remote("st", d, g.stat, g.stats.at[me_n], "narrow", ahead_n(d))
 
@@ -199,13 +228,13 @@
         s = ahead_n(d)
         return remote("gp_n", d, g.gp.at[:, at(s, U)], g.gprows.at[me_n], "narrow", s)
 
-    def ret_copy(d):
-        peer = ahead_w(d)
-        return remote("gr_w", d, g.gsend.at[peer], g.gret.at[me_w], "wide", peer)
-
-    def y_copy(d):
-        s = ahead_n(d)
-        return remote("y_n", d, g.y.at[:, at(s, U)], g.yrows.at[me_n], "narrow", s)
+    def ret_copy(p, d):
+        peer, rows = ahead_w(d), at(p, C // 2)
+        return remote("gr_w", (p, d), g.gsend.at[peer, rows], g.gret.at[me_w, rows], "wide", peer)
+
+    def y_copy(p, d):
+        s, rows = ahead_n(d), at(p, C // 2)
+        return remote("y_n", (p, d), g.y.at[rows, at(s, U)], g.yrows.at[me_n, rows], "narrow", s)
 
     def gh_copy(d):
         s = ahead_n(d)
@@ -216,16 +245,60 @@
         return remote("gf_n", d, g.gfb.at[at(s, C)], g.gfc.at[me_n], "narrow", s)
 
     def red_block(w):
-        down, across = lax.rem(w, z.red_down), w // z.red_down
-        return (slice(None), at(down, z.red_rows), at(across, z.red_lanes))
-
-    def rs_copy(name, src, dst, d):
-        peer = ahead_w(d)
-        return remote(name, d, src.at[red_block(peer)], dst.at[me_w], "wide", peer)
-
-    def ag_copy(name, ref, d):
+        q = w // 2
+        row = lax.rem(w, 2) * (C // 2) + lax.rem(q, z.red_down) * z.red_rows
+        return (slice(None), pl.ds(pl.multiple_of(row, z.red_rows), z.red_rows), at(q // z.red_down, z.red_lanes))
+
+    def half_copy(k):
+        src = getattr(g, "g" + k)
+        return remote("hs" + k, 0, src.at[:, at(1 - core, C // 2)], getattr(g, "g" + k + "_half"), "wide", sibling)
+
+    def rs_copy(k, e):
+        peer = ahead_w(2 * e)
+        return remote("rs" + k, e, getattr(g, "g" + k).at[red_block(peer)], getattr(g, "g" + k + "_in").at[me_w // 2], "wide", peer)
+
+    def ag_copy(k, e):
+        part = getattr(g, "g" + k + "_sum").at[red_block(me_w)]
+        return remote("ag" + k, e, part, part, "wide", ahead_w(2 * e))
+
+    def ag_forward(k, e):
+        part = getattr(g, "g" + k + "_sum").at[red_block(behind_w(2 * e))]
+        return remote("fw" + k, e, part, part, "wide", sibling)
+
+    def reduce_pair(k):
+        own, other = getattr(g, "g" + k), getattr(g, "g" + k + "_half")
+        half_copy(k).wait_recv()
+        mine = (slice(None), at(core, C // 2))
+        own[mine] = (own[mine].astype(F32) + other[...].astype(F32)).astype(BF16)
+        loop(W // 2, lambda e: rs_copy(k, e).start(), 1)
+
+    def reduce_sum(k):
+        own, arrived, out = getattr(g, "g" + k), getattr(g, "g" + k + "_in"), getattr(g, "g" + k + "_sum")
+        loop(W // 2, lambda e: rs_copy(k, e).wait_recv(), 1)
         mine = red_block(me_w)
-        return remote(name, d, ref.at[mine], ref.at[mine], "wide", ahead_w(d))
+        total = lax.fori_loop(
+            1, W // 2, lambda e, t: t + arrived[behind_w(2 * e) // 2].astype(F32), own[mine].astype(F32)
+        )
+        out[mine] = total.astype(BF16)
+        loop(W // 2, lambda e: ag_copy(k, e).start(), 1)
+        ag_forward(k, 0).start()
+
+    def gather_pass(k):
+        def body(e):
+            ag_copy(k, e).wait_recv()
+            ag_forward(k, e).start()
+
+        loop(W // 2, body, 1)
+
+    def drain_reduce(k):
+        half_copy(k).wait_send()
+
+        def body(e):
+            rs_copy(k, e).wait_send()
+            ag_copy(k, e).wait_send()
+
+        loop(W // 2, body, 1)
+        loop(W // 2, lambda e: ag_forward(k, e).wait_send())
 
     def bias_copy(name, src, dst, d):
         return remote(name, d, src, dst.at[me_w], "wide", ahead_w(d))
@@ -247,12 +320,23 @@
     barrier = pltpu.get_barrier_semaphore()
     loop(W, lambda d: pl.semaphore_signal(barrier, inc=1, device_id={"wide": ahead_w(d)}, device_id_type=MESH), 1)
     loop(N, lambda d: pl.semaphore_signal(barrier, inc=1, device_id={"narrow": ahead_n(d)}, device_id_type=MESH), 1)
-    order = (3, 4, 5, 0, 1, 2, 6, 7)
+    order = (6, 3, 4, 5, 0, 1, 2, 7)
     for i in order:
         load(i).start()
+    load(6).wait()
+    g.send_t[...] = g.send[...].T
+
+    def select(d):
+        r = ahead_w(d)
+        which = lax.broadcasted_iota(I32, (CAP, W), 1)
+        col = jnp.sum(jnp.where(which == r, g.send_t[...], 0), axis=1, keepdims=True)
+        place_u = lax.broadcasted_iota(I32, (CAP, R), 1)
+        g.sel[r] = jnp.where(place_u == col, 1.0, 0.0).astype(BF16)
+
+    loop(W, select, 1)
     pl.semaphore_wait(barrier, W - 1 + N - 1)
     loop(N, lambda d: nw_copy(d).start(), 1)
-    g.nbfull[me_n] = jnp.broadcast_to(g.nb_in[...].astype(F32), (8, C))
+    g.nbfull[me_n] = jnp.broadcast_to(g.nb_in[...].astype(F32).reshape(1, C), (8, C))
     loop(N, lambda d: nb_copy(d).start(), 1)
 
     for i in (3, 4, 5):
@@ -325,47 +409,72 @@
             weight = g.wfull[me_n, pl.ds(pl.multiple_of(D + s * C, C), C), :]
             g.zacc[rows, :] += mm(top, weight) + mm(rest, weight)
 
-        loop(R // CH, body)
+        sweep(R // CH, body)
 
     def zero(i):
         g.zacc[at(i, CH), :] = jnp.zeros((CH, C), F32)
 
-    count_groups(0, groups // 4)
-    def pass_nw(d):
-        nw_copy(d).wait_recv()
-        loop(W // 2, lambda e: nw_pass(d, e).start(), 1)
-
-    loop(N, pass_nw, 1)
-    loop(N, lambda d: wt_copy(d).start(), 1)
     loop(R // CH, zero)
     for i in (0, 1, 2):
         load(i).wait()
     hidden(me_n)
-    load(6).wait()
-    g.send_t[...] = g.send[...].T
-
-    def select(d):
-        r = ahead_w(d)
-        which = lax.broadcasted_iota(I32, (CAP, W), 1)
-        col = jnp.sum(jnp.where(which == r, g.send_t[...], 0), axis=1, keepdims=True)
-        place_u = lax.broadcasted_iota(I32, (CAP, R), 1)
-        g.sel[r] = jnp.where(place_u == col, 1.0, 0.0).astype(BF16)
-
-    loop(W, select, 1)
-    count_groups(groups // 4, groups // 2)
+    fifth = groups // 16
+
+    def share_pass(k, d):
+        wt_copy(k, d).wait_recv()
+        wt_pass(k, d).start()
+
+    count_groups(0, 4 * fifth)
+    def pass_nw(d):
+        nw_copy(d).wait_recv()
+        loop(W // 2, lambda e: nw_pass(d, e).start(), 1)
+
+    loop(N, pass_nw, 1)
+    for k in range(2):
+        loop(N, lambda d: wt_copy(k, d).start(), 1)
+    count_groups(4 * fifth, 8 * fifth)
+
     def forward_nw(d):
         loop(W // 2, lambda e: nw_pass(d, e).wait_recv(), 1)
         nw_forward(d).start()
 
-    loop(N, forward_nw, 1)
-
     def take(d):
-        s = behind_n(d)
         nw_forward(d).wait_recv()
         nb_copy(d).wait_recv()
-        hidden(s)
-
-    loop(N, take, 1)
+        hidden(behind_n(d))
+
+    forward_nw(1)
+    count_groups(8 * fifth, 11 * fifth)
+    loop(N, forward_nw, 2)
+    count_groups(11 * fifth, groups)
+    take(1)
+    loop(N, take, 2)
+
+    def column_max(i, most):
+        return jnp.maximum(most, jnp.max(jnp.abs(g.zacc[at(i, CH), :]), axis=0, keepdims=True))
+
+    most = lax.fori_loop(0, R // CH, column_max, jnp.full((1, C), 1e-30, F32))
+    scale = most * (1.0 / 32766.0)
+    g.zscale[...] = jnp.broadcast_to(scale, (8, C))
+    loop(W, lambda d: zscale_copy(d).start(), 1)
+    inv_scale = 1.0 / scale
+
+    def code_z(i):
+        rows = at(i, CH)
+        whole = jnp.round(g.zacc[rows, :] * inv_scale)
+        high = jnp.floor(whole * (1.0 / 256.0))
+        g.zqa[rows, :] = high.astype(BF16)
+        g.zqb[rows, :] = (whole - high * 256.0).astype(BF16)
+
+    loop(R // CH, code_z)
+
+    def send_z(d):
+        peer = ahead_w(d)
+        picked = mm(g.sel[peer], g.zqa[...]) * 256.0 + mm(g.sel[peer], g.zqb[...])
+        g.zsend[peer] = picked.astype(I32).astype(I16)
+        z_copy(d).start()
+
+    loop(W, send_z, 1)
 
     def split_z(i):
         rows = at(i, CH)
@@ -375,21 +484,11 @@
         g.zlo[rows, :] = (value - top.astype(F32)).astype(BF16)
 
     loop(R // CH, split_z)
-
-    def send_z(d):
-        peer = ahead_w(d)
-        g.zsend[peer, 0] = mm(g.sel[peer], g.zhi[...]).astype(BF16)
-        g.zsend[peer, 1] = mm(g.sel[peer], g.zlo[...]).astype(BF16)
-        z_copy(d).start()
-
-    loop(W, send_z, 1)
-
-    count_groups(groups // 2, groups)
     load(7).wait()
 
     def own_part(i):
         rows = at(i, CH)
-        value = mm(g.feats[rows, :], g.wfull[me_n, 0:D, :]) + g.cb_in[...].astype(F32)
+        value = mm(g.feats[rows, :], g.wfull[me_n, 0:D, :]) + g.cb_in[...].astype(F32).reshape(1, C)
         g.self_t[:, rows] = value.T
         g.cot_t[:, rows] = g.cot[rows, :].astype(F32).T
         total = jnp.zeros((CH, C), F32)
@@ -399,7 +498,7 @@
             total += mm(block, g.zhi[part, :]) + mm(block, g.zlo[part, :])
         g.acc[rows, :] = total
 
-    loop(R // CH, own_part)
+    sweep(R // CH, own_part)
     ones = jnp.ones((16, 128), BF16)
     g.invs[...] = 2.0 / mm_nt(ones, g.wts[...].astype(BF16))
 
@@ -412,14 +511,18 @@
     def take_z(d):
         s = behind_w(d)
         z_copy(d).wait_recv()
+        value = g.ztab[s].astype(I32).astype(F32) * g.zscales[s, 0:1, :]
+        top = value.astype(BF16)
+        rest = (value - top.astype(F32)).astype(BF16)
 
         def body(i):
             rows = at(i, CH)
             block = g.counts[z.local + s, rows, :]
-            g.acc[rows, :] += mm(block, g.ztab[s, 0]) + mm(block, g.ztab[s, 1])
-
-        loop(R // CH, body)
-
+            g.acc[rows, :] += mm(block, top) + mm(block, rest)
+
+        sweep(R // CH, body)
+
+    loop(W, lambda d: zscale_copy(d).wait_recv(), 1)
     loop(W, take_z, 1)
 
     which8 = lax.broadcasted_iota(I32, (8, CH), 0)
@@ -433,6 +536,8 @@
         inner = jnp.sum(act * g.cot_t[:, rows], axis=0, keepdims=True)
         g.stat[:, rows] = jnp.where(which8 == 0, squares, jnp.where(which8 == 1, inner, 0.0))
 
+    for k in range(2):
+        loop(N, functools.partial(share_pass, k), 1)
     loop(R // CH, activate)
     loop(N, lambda d: stat_copy(d).start(), 1)
     loop(N, lambda d: stat_copy(d).wait_recv(), 1)
@@ -457,12 +562,13 @@
     loop(R // CH, grad_act)
     loop(N, lambda d: gp_copy(d).start(), 1)
 
-    def send_ret(d):
-        peer = ahead_w(d)
-        g.gsend[peer] = mm(g.gps[...], g.counts[z.local + peer]).astype(BF16)
-        ret_copy(d).start()
-
-    loop(W, send_ret, 1)
+    def send_ret(p, d):
+        peer, rows = ahead_w(d), at(p, C // 2)
+        g.gsend[peer, rows, :] = mm(g.gps[rows, :], g.counts[z.local + peer]).astype(BF16)
+        ret_copy(p, d).start()
+
+    for p in range(2):
+        loop(W, functools.partial(send_ret, p), 1)
 
     join = max(1, 128 // CAP)
     for h in range(0, z.local, join):
@@ -480,11 +586,12 @@
     emb_store = pltpu.make_async_copy(g.emb, g.emb_out, g.store.at[0])
     emb_store.start()
 
-    def pass_weights(d):
-        wt_arrive(d).wait_recv()
-        wt_forward(d).start()
-
-    loop(N, pass_weights, 1)
+    def pass_weights(k, d):
+        wt_pass(k, d).wait_recv()
+        wt_forward(k, d).start()
+
+    for k in range(2):
+        loop(N, functools.partial(pass_weights, k), 1)
 
     LW = min(512, D)
 
@@ -492,42 +599,40 @@
         lanes = at(i, LW)
         g.gc[0, :, lanes] = mm(g.gp[...], g.feats[:, lanes]).astype(BF16)
 
-    loop(D // LW, grad_self)
+    sweep(D // LW, grad_self)
     ones_r = jnp.ones((8, R), BF16)
     g.gcb[...] = mm_nt(ones_r, g.gp[...])
 
     g.gprows[me_n] = g.gp[:, at(me_n, U)]
 
-    def take_ret(d):
-        s = behind_w(d)
-        ret_copy(d).wait_recv()
+    def take_ret(p, d):
+        s, half_rows = behind_w(d), at(p, C // 2)
+        ret_copy(p, d).wait_recv()
 
         def body(i):
             lanes = at(i, CH)
-            g.yacc[:, lanes] += mm(g.gret[s], g.sel[s, :, lanes])
-
-        loop(R // CH, body)
-
-    loop(W, take_ret, 1)
-
-    def round_y(i):
-        lanes = at(i, CH)
-        g.y[:, lanes] = g.yacc[:, lanes].astype(BF16)
-
-    loop(R // CH, round_y)
-    loop(N, lambda d: y_copy(d).start(), 1)
+            g.yacc[half_rows, lanes] += mm(g.gret[s, half_rows, :], g.sel[s, :, lanes])
+
+        sweep(R // CH, body)
+
+    for p in range(2):
+        loop(W, functools.partial(take_ret, p), 1)
+        half_rows = at(p, C // 2)
+        g.y[half_rows, :] = g.yacc[half_rows, :].astype(BF16)
+        loop(N, lambda d: y_copy(p, d).start(), 1)
     g.yrows[me_n] = g.y[:, at(me_n, U)]
 
     def grad_pool(i):
         lanes = at(i, LW)
         g.gc[1, :, lanes] = mm(g.y[...], g.msg[:, lanes]).astype(BF16)
 
-    loop(D // LW, grad_pool)
+    sweep(D // LW, grad_pool)
     loop(W, lambda d: bias_copy("bc", g.gcb, g.gcb_in, d).start(), 1)
-    loop(W, lambda d: rs_copy("rsc", g.gc, g.gc_in, d).start(), 1)
+    half_copy("c").start()
 
     loop(N, lambda d: gp_copy(d).wait_recv(), 1)
-    loop(N, lambda d: wt_forward(d).wait_recv(), 1)
+    for k in range(2):
+        loop(N, lambda d: wt_forward(k, d).wait_recv(), 1)
 
     def self_rows(i):
         rows = at(i, CH)
@@ -536,18 +641,20 @@
             total += mm(g.wfull[s, rows, :], g.gprows[s])
         g.gf[rows, :] = total
 
-    loop(D // CH, self_rows)
-    loop(N, lambda d: y_copy(d).wait_recv(), 1)
+    sweep(D // CH, self_rows)
+    reduce_pair("c")
+    for p in range(2):
+        loop(N, lambda d: y_copy(p, d).wait_recv(), 1)
 
     def hidden_rows(i):
         rows = at(i, CH)
-        wrows = pl.ds(pl.multiple_of(D + i * CH, CH), CH)
+        wrows = slice(D + i * CH, D + (i + 1) * CH)
         total = jnp.zeros((CH, U), F32)
         for s in range(N):
             total += mm(g.wfull[s, wrows, :], g.yrows[s])
         g.gh[rows, :] = jnp.where(g.msg_t[rows, :] > 0, total, 0.0).astype(BF16)
 
-    loop(D // CH, hidden_rows)
+    sweep(D // CH, hidden_rows)
     loop(N, lambda d: gh_copy(d).start(), 1)
     g.ghc[me_n] = g.gh[at(me_n, C), :]
 
@@ -558,24 +665,13 @@
             total += mm(g.nwfull[s, rows, :], g.gh[s * C : (s + 1) * C, :])
         g.gfb[rows, :] = total.astype(BF16)
 
-    loop(D // CH, feature_rows)
+    sweep(D // CH, feature_rows)
+    g.gfc[me_n] = g.gfb[at(me_n, C), :]
+
+    reduce_sum("c")
+
+    loop(N, lambda d: gh_copy(d).wait_recv(), 1)
     loop(N, lambda d: gf_copy(d).start(), 1)
-    g.gfc[me_n] = g.gfb[at(me_n, C), :]
-
-    def reduce_sum(own, arrived, out):
-        mine = red_block(me_w)
-        total = own[mine].astype(F32)
-
-        def body(d, total):
-            return total + arrived[behind_w(d)].astype(F32)
-
-        out[mine] = lax.fori_loop(1, W, body, total).astype(BF16)
-
-    loop(W, lambda d: rs_copy("rsc", g.gc, g.gc_in, d).wait_recv(), 1)
-    reduce_sum(g.gc, g.gc_in, g.gc_sum)
-    loop(W, lambda d: ag_copy("agc", g.gc_sum, d).start(), 1)
-
-    loop(N, lambda d: gh_copy(d).wait_recv(), 1)
 
     def grad_neigh(i):
         lanes = at(i, LW)
@@ -584,40 +680,36 @@
             total += mm(g.ghc[s], g.feats[s * U : (s + 1) * U, lanes])
         g.gn[0, :, lanes] = total.astype(BF16)
 
-    loop(D // LW, grad_neigh)
+    sweep(D // LW, grad_neigh)
     total = jnp.zeros((8, C), F32)
     ones_u = jnp.ones((8, U), BF16)
     for s in range(N):
         total += mm_nt(ones_u, g.ghc[s])
     g.gnb[...] = total
-    loop(W, lambda d: rs_copy("rsn", g.gn, g.gn_in, d).start(), 1)
+    half_copy("n").start()
     loop(W, lambda d: bias_copy("bn", g.gnb, g.gnb_in, d).start(), 1)
+
+    gather_pass("c")
+    reduce_pair("n")
+    reduce_sum("n")
+
+    def bias_sum(name, own, arrived):
+        loop(W, lambda d: bias_copy(name, own, arrived, d).wait_recv(), 1)
+        loop(W, lambda d: bias_copy(name, own, arrived, d).wait_send(), 1)
+
+        def body(d, total):
+            return total + arrived[behind_w(d)]
+
+        own[...] = lax.fori_loop(1, W, body, own[...])
+
+    bias_sum("bc", g.gcb, g.gcb_in)
+    bias_sum("bn", g.gnb, g.gnb_in)
 
     loop(N, lambda d: gf_copy(d).wait_recv(), 1)
     gf_store = pltpu.make_async_copy(g.gfc, g.gf_out, g.store.at[1])
     gf_store.start()
 
-    loop(W, lambda d: rs_copy("rsn", g.gn, g.gn_in, d).wait_recv(), 1)
-    reduce_sum(g.gn, g.gn_in, g.gn_sum)
-    loop(W, lambda d: ag_copy("agn", g.gn_sum, d).start(), 1)
-
-    def bias_sum(name, own, arrived):
-        loop(W, lambda d: bias_copy(name, own, arrived, d).wait_recv(), 1)
-        loop(W, lambda d: bias_copy(name, own, arrived, d).wait_send(), 1)
-
-        def body(d, total):
-            return total + arrived[behind_w(d)]
-
-        own[...] = lax.fori_loop(1, W, body, own[...])
-
-    bias_sum("bc", g.gcb, g.gcb_in)
-    bias_sum("bn", g.gnb, g.gnb_in)
-
-    def ag_arrive(name, ref, d):
-        theirs = red_block(behind_w(d))
-        return remote(name, d, ref.at[theirs], ref.at[theirs], "wide", behind_w(d))
-
-    loop(W, lambda d: ag_arrive("agc", g.gc_sum, d).wait_recv(), 1)
+    loop(W // 2, lambda e: ag_forward("c", e).wait_recv())
     stores = [
         emb_store,
         gf_store,
@@ -628,29 +720,37 @@
     ]
     for store in stores[2:5]:
         store.start()
-    loop(W, lambda d: ag_arrive("agn", g.gn_sum, d).wait_recv(), 1)
+    gather_pass("n")
+    loop(W // 2, lambda e: ag_forward("n", e).wait_recv())
     stores[5].start()
 
     def drain_n(d):
         loop(W // 2, lambda e: nw_pass(d, e).wait_send(), 1)
-        for copy in (nw_copy, nw_forward, nb_copy, wt_copy, wt_forward, stat_copy, gp_copy, y_copy, gh_copy, gf_copy):
+        for copy in (nw_copy, nw_forward, nb_copy, stat_copy, gp_copy, gh_copy, gf_copy):
             copy(d).wait_send()
+        for k in range(2):
+            wt_copy(k, d).wait_send()
+            wt_pass(k, d).wait_send()
+            wt_forward(k, d).wait_send()
+        for p in range(2):
+            y_copy(p, d).wait_send()
 
     def drain_w(d):
         z_copy(d).wait_send()
-        ret_copy(d).wait_send()
-        rs_copy("rsc", g.gc, g.gc_in, d).wait_send()
-        ag_copy("agc", g.gc_sum, d).wait_send()
-        rs_copy("rsn", g.gn, g.gn_in, d).wait_send()
-        ag_copy("agn", g.gn_sum, d).wait_send()
+        zscale_copy(d).wait_send()
+        for p in range(2):
+            ret_copy(p, d).wait_send()
 
     loop(N, drain_n, 1)
     loop(W, drain_w, 1)
+    drain_reduce("c")
+    drain_reduce("n")
     for store in stores:
         store.wait()
 
 
 def finish(emb_in, gf, gn, gc, gnb, gcb, emb_out, gf_out, gn_out, gc_out, gnb_out, gcb_out):
+    emb_out[...] = emb_in[...]
     gf_out[...] = gf[0].astype(F32).T
     gn_out[...] = gn[0].astype(F32).T
     for i in range(2):
@@ -687,7 +787,7 @@
         cost_estimate=pl.CostEstimate(flops=2 * 10**10, bytes_accessed=2 * 10**7, transcendentals=0),
         name="layer",
     )(
-        node_feats, neigh_weight, neigh_bias.reshape(1, C), combine_weight, combine_bias.reshape(1, C), cotangent,
+        node_feats, neigh_weight, neigh_bias, combine_weight, combine_bias, cotangent,
         neighbour_slot.T, neighbour_mask.T, visit_count.T, send_rows,
     )
     Q = D // N
@@ -705,7 +805,7 @@
             jax.ShapeDtypeStruct((1, C), F32),
         ),
         in_specs=[
-            pl.BlockSpec(memory_space=pl.ANY),
+            pl.BlockSpec((U, C), lambda i: (i, 0)),
             pl.BlockSpec((1, C, U), lambda i: (i, 0, 0)),
             pl.BlockSpec((1, C, Q), lambda i: (0, 0, i)),
             pl.BlockSpec((2, C, Q), lambda i: (0, 0, i)),
@@ -713,15 +813,14 @@
             whole,
         ],
         out_specs=[
-            pl.BlockSpec(memory_space=pl.ANY),
+            pl.BlockSpec((U, C), lambda i: (i, 0)),
             pl.BlockSpec((U, C), lambda i: (i, 0)),
             pl.BlockSpec((Q, C), lambda i: (i, 0)),
             pl.BlockSpec((2, Q, C), lambda i: (0, i, 0)),
             line,
             line,
         ],
-        input_output_aliases={0: 0},
-        compiler_params=pltpu.CompilerParams(vmem_limit_bytes=16 * 2**20),
+        compiler_params=pltpu.CompilerParams(vmem_limit_bytes=60 * 2**20),
         name="finish",
     )(emb, gf, gn, gc, gnb, gcb)
     return emb, grad_features, grad_neigh, gnb.reshape(C), grad_combine.reshape(2 * D, C), gcb.reshape(C)

time: 141 us -> 113 us (0.80)
  Pallas kernels: 131 us -> 112 us
  local copies, waits for them, and re-layouts: 8.97 us -> 0 us
    pallas_call x1, Pallas kernels: 128 us -> 108 us  [shards(): pl.pallas_call(functools.partial(kernel, z, names), out_shape=outs, in_sp...]
    unnamed x13 -> x0, local copies, waits for them, and re-layouts: 6.53 us -> none
    reshape x2 -> x0, local copies, waits for them, and re-layouts: 2.44 us -> none  [the longest x1 1.22 us: shards(): neigh_bias.reshape(1, C)]
    pallas_call x1, Pallas kernels: 2.72 us -> 4.74 us  [shards(): pl.pallas_call(finish, grid=(N,), out_shape=(jax.ShapeDtypeStruct((R, C),...]
where the time goes in v4:
time: 113 us
  Pallas kernels  112 us (99%)
    pallas_call x1, Pallas kernels, shards(): pl.pallas_call(functools.partial(kernel, z, names), out_shape=outs, in_sp...  108 us
    pallas_call x1, Pallas kernels, shards(): pl.pallas_call(finish, grid=(N,), out_shape=(jax.ShapeDtypeStruct((R, C),...  4.74 us

profile of v4, /device:TPU:25, one launch (start us, length us, event | category | flops | bytes accessed | tf_op | source)
XLA Modules:
  0.0 113.0 jit_solution(3268710797780387971)
XLA Ops:
  0.6 107.6 %layer.1 = (bf16[1024,256]{1,0:T(8,128)(2,1)}, bf16[4,256,256]{2,1,0:T(8,128)(2,1)}, bf16[1,256,1024]{2,1,0:T(8,128)(2,1)}, bf16[2,256,1024]{2,1,0:T(8,128)(2,1)}, f32[8,256]{1,0:T(8,128)}, /*index=5*/f32[8,256]{1,0:T(8,128)}) custom-call(bf16[1024,1024]{1,0:T(8,128)(2,1)} %refs_0_.1, bf16[1024,256]{1,0:T(8,128)(2,1)} %refs_1_.1, bf16[256]{0:T(256)(128)(2,1)} %refs_2_.1, ...), custom_call_target="tpu_custom_call" | custom-call | flops 20000000000 | bytes 20000000 | tf_op jit(solution)/shard_map/layer/pallas_call | solution.py:776
  108.3 4.7 %finish.1 = (bf16[1024,256]{1,0:T(8,128)(2,1)}, f32[1024,256]{1,0:T(8,128)}, f32[1024,256]{1,0:T(8,128)}, f32[2,1024,256]{2,1,0:T(8,128)}, f32[1,256]{1,0:T(1,128)}, /*index=5*/f32[1,256]{1,0:T(1,128)}) custom-call(bf16[1024,256]{1,0:T(8,128)(2,1)} %get-tuple-element.18.emb_in, bf16[4,256,256]{2,1,0:T(8,128)(2,1)} %get-tuple-element.19.gf, ...), custom_call_target="tpu_custom_call" | custom-call | tf_op jit(solution)/shard_map/finish/pallas_call | solution.py:796

commit v5 on v4

v5 whole, which is shorter than its diff:
```python
import functools

import jax
import jax.numpy as jnp
from jax import lax
from jax.experimental import pallas as pl
from jax.experimental.pallas import tpu as pltpu
from jax.sharding import PartitionSpec as P

EPSILON = 1e-06
PARTS = 4
SUMS = ("c", "n0", "n1")
F32 = jnp.float32
BF16 = jnp.bfloat16
I32 = jnp.int32
I16 = jnp.int16
MESH = pl.DeviceIdType.MESH


def mm(left, right):
    return jnp.dot(left, right, preferred_element_type=F32)


def mm_nt(left, right):
    return lax.dot_general(left, right, (((1,), (1,)), ((), ())), preferred_element_type=F32)


def at(index, size):
    if isinstance(index, int):
        return slice(index * size, (index + 1) * size)
    return pl.ds(pl.multiple_of(index * size, size), size)


class Sizes:
    def __init__(self, feats, neigh, send, slot, wide, narrow):
        self.rows, self.width = feats.shape
        self.cols = neigh.shape[1]
        self.cap = send.shape[1]
        self.slots = slot.shape[0]
        self.wide, self.narrow = wide, narrow
        self.chunk = min(256, self.rows)
        self.part = self.rows // narrow
        self.local = self.rows // self.cap
        self.blocks = self.local + wide
        self.pairs = wide // 2

    def red(self, rows):
        size = max(16, rows // 2 // self.pairs)
        down = rows // 2 // size
        return size, down, self.width * down // self.pairs


NAMES_IN = ["feats_in", "nw_in", "nb_in", "comb_in", "cb_in", "cot_in", "slot_in", "mask_in", "visit_in", "send_in"]
NAMES_OUT = ["emb_out", "gf_out", "gn_out", "gc_out", "gnb_out", "gcb_out"]


def scratch(z):
    R, D, C, W, N, U, CAP = z.rows, z.width, z.cols, z.wide, z.narrow, z.part, z.cap
    v = lambda *shape: pltpu.VMEM(shape[:-1], shape[-1])
    bufs = dict(
        feats=v(R, D, BF16),
        nwfull=v(N, D, C, BF16),
        nbfull=v(N, 8, C, F32),
        nb=v(C, BF16),
        cb=v(C, BF16),
        wfull=v(N, 2 * D, C, BF16),
        cot=v(R, C, BF16),
        slot=v(z.slots, R, I32),
        mask=v(z.slots, R, I32),
        visit=v(z.slots, R, I32),
        send=v(W, CAP, I32),
        send_t=v(CAP, W, I32),
        code=v(R, 128, I32),
        wts=v(R, 128, F32),
        counts=v(z.blocks, R, CAP, BF16),
        sel=v(W, CAP, R, BF16),
        msg=v(R, D, BF16),
        zacc=v(R, C, F32),
        zhi=v(R, C, BF16),
        zlo=v(R, C, BF16),
        zqa=v(R, C, BF16),
        zqb=v(R, C, BF16),
        zscale=v(8, C, F32),
        thi=v(W, CAP, C, BF16),
        tlo=v(W, CAP, C, BF16),
        zscales=v(W, 8, C, F32),
        zsend=v(W, CAP, C, I16),
        ztab=v(W, CAP, C, I16),
        acc=v(R, C, F32),
        self_t=v(C, R, F32),
        cot_t=v(C, R, F32),
        invs=v(16, R, F32),
        stat=v(2 * (R // z.chunk), z.chunk, F32),
        stats=v(N, 2 * (R // z.chunk), z.chunk, F32),
        emb=v(R, C, BF16),
        gp=v(C, R, BF16),
        gps=v(C, R, BF16),
        gprows=v(N, C, U, BF16),
        gsend=v(W, C, CAP, BF16),
        gret=v(W, C, CAP, BF16),
        yacc=v(C, R, F32),
        y=v(C, R, BF16),
        yrows=v(N, C, U, BF16),
        msg_t=v(D, U, BF16),
        gh=v(D, U, BF16),
        ghc=v(N, C, U, BF16),
        gfb=v(D, U, BF16),
        gc=v(2, C, D, BF16),
        gc_half=v(2, C // 2, D, BF16),
        gc_in=v(W // 2, 2, z.red(C)[0], z.red(C)[2], BF16),
        gc_sum=v(2, C, D, BF16),
        gn0=v(1, C // 2, D, BF16),
        gn0_half=v(1, C // 4, D, BF16),
        gn0_in=v(W // 2, 1, z.red(C // 2)[0], z.red(C // 2)[2], BF16),
        gn0_sum=v(1, C // 2, D, BF16),
        gn1=v(1, C // 2, D, BF16),
        gn1_half=v(1, C // 4, D, BF16),
        gn1_in=v(W // 2, 1, z.red(C // 2)[0], z.red(C // 2)[2], BF16),
        gn1_sum=v(1, C // 2, D, BF16),
        gcb=v(8, C, F32),
        gcb_in=v(W, 8, C, F32),
        gnb=v(8, C, F32),
        gnb_in=v(W, 8, C, F32),
    )
    kinds = dict(
        sh0=N, sh1=N, sh2=N, sp0=N, sp1=N, sp2=N, sf0=N, sf1=1, sf2=1, nb=1, st=1, gp=1, y=1, gh=2, gf=1,
        z=W, zs=1, gr=PARTS, bc=1, bn=1,
    )
    for k in SUMS:
        kinds.update({"hs" + k: 1, "rs" + k: 1, "ag" + k: 1, "fw" + k: 1})
    sems = {name + "_r": pltpu.SemaphoreType.DMA((count,)) for name, count in kinds.items()}
    sems["sent"] = pltpu.SemaphoreType.DMA((len(kinds),))
    sems["load"] = pltpu.SemaphoreType.DMA((10,))
    sems["store"] = pltpu.SemaphoreType.DMA((7,))
    return bufs, sems, list(kinds)


class Refs:
    pass


def kernel(z, names, kinds, *refs):
    g = Refs()
    for name, ref in zip(names, refs):
        setattr(g, name, ref)
    R, D, C, W, N, U, CAP = z.rows, z.width, z.cols, z.wide, z.narrow, z.part, z.cap
    CH = z.chunk
    half = D // 2
    me_w, me_n = lax.axis_index("wide"), lax.axis_index("narrow")
    core = lax.rem(me_w, 2)
    sibling = me_w + 1 - 2 * core

    def loop(count, body, start=0):
        def step(i, carry):
            body(i)
            return carry

        lax.fori_loop(start, count, step, 0)

    def sweep(count, body):
        for i in range(count):
            body(i)

    def flip(me, e, size):
        peer, bit = 0, 1
        while bit < size:
            peer = peer + bit * lax.rem(me // bit + e // bit, 2)
            bit *= 2
        return peer

    def peer_n(d):
        return flip(me_n, N - d, N)

    def peer_w(d):
        return flip(me_w, W - d, W)

    def ahead_n(d):
        return lax.rem(me_n + d, N)

    def behind_n(d):
        return lax.rem(me_n - d + N, N)

    def across(e):
        return flip(me_w, e, W)

    def remote(name, index, src, dst, axis="narrow", peer=0):
        return pltpu.make_async_remote_copy(
            src_ref=src,
            dst_ref=dst,
            send_sem=g.sent.at[kinds.index(name)],
            recv_sem=getattr(g, name + "_r").at[index],
            device_id={axis: peer},
            device_id_type=MESH,
        )

    def arrived(name, index, ref):
        remote(name, index, ref, ref, "narrow", peer_n(1)).wait_recv()

    def left(name, ref):
        remote(name, 0, ref, ref, "narrow", peer_n(1)).wait_send()

    hops = (2, 4)
    first = (None, D, 0)
    eighth = D // 8

    def rows_at(start, size):
        return pl.ds(pl.multiple_of(start, size), size)

    def hop_bit(h):
        return lax.rem(me_w // hops[h], 2)

    def quarter(k, h):
        return rows_at(first[k] + h * half + (2 * core + hop_bit(h)) * eighth, eighth)

    def quarter_copy(k, d, h):
        mine = quarter(k, h)
        return remote("sh%d" % k, d, g.comb_in.at[mine], g.wfull.at[me_n, mine], "narrow", ahead_n(d))

    def quarter_send(k):
        def body(d):
            for h in range(2):
                quarter_copy(k, d, h).start()

        loop(N, body, 1)

    def quarter_pass(k, d):
        s = behind_n(d)
        arrived("sh%d" % k, d, g.wfull.at[s, 0 : 2 * eighth])
        for h in range(2):
            part = g.wfull.at[s, quarter(k, h)]
            remote("sp%d" % k, d, part, part, "wide", me_w + hops[h] - 2 * hops[h] * hop_bit(h)).start()

    def quarter_forward(k, d):
        s = behind_n(d)
        arrived("sp%d" % k, d, g.wfull.at[s, 0 : 2 * eighth])
        for h in range(2):
            part = g.wfull.at[s, rows_at(first[k] + h * half + 2 * core * eighth, 2 * eighth)]
            remote("sf%d" % k, 0, part, part, "wide", sibling).start()

    part_w = D // W

    def share():
        return rows_at((core * (W // 2) + me_w // 2) * part_w, part_w)

    def share_send(d):
        remote("sh0", d, g.nw_in.at[share()], g.nwfull.at[me_n, share()], "narrow", ahead_n(d)).start()

    def share_pass(d):
        part = g.nwfull.at[behind_n(d), share()]
        arrived("sh0", d, part)
        loop(W // 2, lambda e: remote("sp0", d, part, part, "wide", across(2 * e)).start(), 1)

    def share_forward(d):
        s = behind_n(d)
        arrived("sp0", d, g.nwfull.at[s, 0 : (W // 2 - 1) * part_w])
        part = g.nwfull.at[s, rows_at(core * half, half)]
        remote("sf0", d, part, part, "wide", sibling).start()

    def nb_copy(d):
        return remote("nb", 0, g.nbfull.at[me_n], g.nbfull.at[me_n], "narrow", peer_n(d))

    def z_copy(d):
        peer = peer_w(d)
        return remote("z", d, g.zsend.at[peer], g.ztab.at[me_w], "wide", peer)

    def zscale_copy(d):
        return remote("zs", 0, g.zscale, g.zscales.at[me_w], "wide", peer_w(d))

    def stat_copy(d):
        return remote("st", 0, g.stat, g.stats.at[me_n], "narrow", peer_n(d))

    def gp_copy(d):
        s = peer_n(d)
        return remote("gp", 0, g.gp.at[:, at(s, U)], g.gprows.at[me_n], "narrow", s)

    def ret_copy(p, d):
        peer, rows = peer_w(d), at(p, C // PARTS)
        return remote("gr", p, g.gsend.at[peer, rows], g.gret.at[me_w, rows], "wide", peer)

    def y_copy(p, d):
        s, rows = peer_n(d), at(p, C // PARTS)
        return remote("y", 0, g.y.at[rows, at(s, U)], g.yrows.at[me_n, rows], "narrow", s)

    def gh_copy(q, d):
        s = peer_n(d)
        return remote("gh", q, g.gh.at[rows_at(s * C + q * (C // 2), C // 2)], g.ghc.at[me_n, at(q, C // 2)], "narrow", s)

    def gf_copy(d):
        s = peer_n(d)
        return remote("gf", 0, g.gfb.at[at(s, C)], g.gf_out.at[me_n], "narrow", s)

    def bias_copy(name, src, dst, d):
        return remote(name, 0, src, dst.at[me_w], "wide", peer_w(d))

    def grad(k, suffix=""):
        return getattr(g, "g" + k + suffix)

    def core_rows(k, which):
        return (slice(None), at(which, grad(k).shape[1] // 2))

    def red_block(k, w):
        rows = grad(k).shape[1]
        size, down, lanes = z.red(rows)
        q = w // 2
        row = lax.rem(w, 2) * (rows // 2) + lax.rem(q, down) * size
        return (slice(None), rows_at(row, size), at(q // down, lanes))

    def out_rows(k, which):
        rows = grad(k).shape[1]
        if k == "c":
            return g.gc_out.at[:, at(which, rows // 2)]
        return g.gn_out.at[:, rows_at(int(k[1]) * rows + which * (rows // 2), rows // 2)]

    def pair_start(k):
        remote("hs" + k, 0, grad(k).at[core_rows(k, 1 - core)], grad(k, "_half"), "wide", sibling).start()

    def reduce_pair(k):
        arrived("hs" + k, 0, grad(k, "_half"))
        own, mine = grad(k), core_rows(k, core)
        own[mine] = (own[mine].astype(F32) + grad(k, "_half")[...].astype(F32)).astype(BF16)

        def body(e):
            peer = across(2 * e)
            remote("rs" + k, 0, own.at[red_block(k, peer)], grad(k, "_in").at[me_w // 2], "wide", peer).start()

        loop(W // 2, body, 1)

    def reduce_sum(k):
        others = grad(k, "_in")
        arrived("rs" + k, 0, others.at[0 : W // 2 - 1])
        mine = red_block(k, me_w)
        total = lax.fori_loop(
            1, W // 2, lambda e, t: t + others[across(2 * e) // 2].astype(F32), grad(k)[mine].astype(F32), unroll=W <= 8
        )
        grad(k, "_sum")[mine] = total.astype(BF16)
        part = grad(k, "_sum").at[mine]
        loop(W // 2, lambda e: remote("ag" + k, 0, part, part, "wide", across(2 * e)).start(), 1)

    def gather_pass(k):
        arrived("ag" + k, 0, grad(k, "_in").at[0 : W // 2 - 1])
        part = grad(k, "_sum").at[core_rows(k, core)]
        remote("fw" + k, 0, part, out_rows(k, core), "wide", sibling).start()
        store = pltpu.make_async_copy(part, out_rows(k, core), g.store.at[SUMS.index(k)])
        store.start()
        return store

    def gather_wait(k):
        arrived("fw" + k, 0, out_rows(k, 1 - core))

    loads = [
        (g.feats_in, g.feats),
        (g.nw_in, g.nwfull.at[me_n]),
        (g.comb_in, g.wfull.at[me_n]),
        (g.slot_in, g.slot),
        (g.mask_in, g.mask),
        (g.visit_in, g.visit),
        (g.send_in, g.send),
        (g.cot_in, g.cot),
        (g.nb_in, g.nb),
        (g.cb_in, g.cb),
    ]

    def load(i):
        return pltpu.make_async_copy(loads[i][0], loads[i][1], g.load.at[i])

    barrier = pltpu.get_barrier_semaphore()
    loop(W, lambda d: pl.semaphore_signal(barrier, inc=1, device_id={"wide": peer_w(d)}, device_id_type=MESH), 1)
    loop(N, lambda d: pl.semaphore_signal(barrier, inc=1, device_id={"narrow": peer_n(d)}, device_id_type=MESH), 1)
    order = (6, 8, 3, 4, 5, 0, 1, 2, 7, 9)
    for i in order:
        load(i).start()
    load(6).wait()
    g.send_t[...] = g.send[...].T

    def select(d):
        r = peer_w(d)
        which = lax.broadcasted_iota(I32, (CAP, W), 1)
        col = jnp.sum(jnp.where(which == r, g.send_t[...], 0), axis=1, keepdims=True)
        place_u = lax.broadcasted_iota(I32, (CAP, R), 1)
        g.sel[r] = jnp.where(place_u == col, 1.0, 0.0).astype(BF16)

    loop(W, select, 1)
    pl.semaphore_wait(barrier, W - 1 + N - 1)
    loop(N, share_send, 1)
    load(8).wait()
    g.nbfull[me_n] = jnp.broadcast_to(g.nb[...].astype(F32).reshape(1, C), (8, C))
    loop(N, lambda d: nb_copy(d).start(), 1)

    for i in (3, 4, 5):
        load(i).wait()
    K = z.slots
    shift = CAP.bit_length() - 1

    def fill(i):
        rows = at(i, CH)
        g.code[rows, :] = jnp.zeros((CH, 128), I32)
        g.wts[rows, :] = jnp.zeros((CH, 128), F32)
        code = g.slot[:, rows].T
        g.code[rows, 0:K] = code
        g.code[rows, 64 : 64 + K] = code
        weight = (g.mask[:, rows] * g.visit[:, rows]).astype(F32).T
        g.wts[rows, 0:K] = weight
        g.wts[rows, 64 : 64 + K] = weight

    loop(R // CH, fill)

    lane = lax.broadcasted_iota(I32, (8, 128), 1)
    sub = lax.broadcasted_iota(I32, (8, 128), 0)
    half_lane = jnp.where(lane >= 64, 1, 0)
    place = [sub == 2 * j + half_lane for j in range(4)]
    place_b = [jnp.where(m, 1.0, 0.0) for m in place]
    place_b = [jnp.concatenate([m, m], axis=0).astype(BF16) for m in place_b]
    low_row = lax.broadcasted_iota(I32, (CAP, 128), 0).astype(F32).astype(BF16)

    def count_group(i):
        start = pl.multiple_of(i * 16, 16)
        outs = []
        for p in range(2):
            rows = pl.ds(pl.multiple_of(start + 8 * p, 8), 8)
            code, weight = g.code[rows, :], g.wts[rows, :]
            high, low = code >> shift, (code & (CAP - 1)).astype(F32)
            left = []
            for h in range(0, z.blocks, 2):
                pair = [jnp.where(high == h + q, weight, 0.0) for q in range(2)]
                pair = jnp.concatenate(pair, axis=0).astype(BF16)
                left.append(jnp.concatenate([pair * place_b[j] for j in range(4)], axis=1))
            left = jnp.concatenate(left, axis=0)
            right = []
            for j in range(4):
                row = jnp.sum(jnp.where(place[j], low, 0.0), axis=0, keepdims=True)
                row = jnp.broadcast_to(row.astype(BF16), (CAP, 128))
                right.append(jnp.where(low_row == row, jnp.ones((), BF16), jnp.zeros((), BF16)))
            outs.append(mm_nt(left, jnp.concatenate(right, axis=1)))
        for h in range(z.blocks):
            block = [out[h * 8 : h * 8 + 8] for out in outs]
            g.counts[h, pl.ds(start, 16), :] = jnp.concatenate(block, axis=0).astype(BF16)

    UNROLL = 4
    groups = R // 16 // UNROLL

    def count_groups(first, last):
        def body(i):
            for q in range(UNROLL):
                count_group(i * UNROLL + q)

        loop(last, body, first)

    def hidden(s):
        def body(i):
            rows = at(i, CH)
            value = mm(g.feats[rows, :], g.nwfull[s]) + g.nbfull[s, 0:1, :]
            value = jnp.maximum(value, 0.0)
            top = value.astype(BF16)
            rest = (value - top.astype(F32)).astype(BF16)
            g.msg[rows, at(s, C)] = top
            weight = g.wfull[me_n, pl.ds(pl.multiple_of(D + s * C, C), C), :]
            g.zacc[rows, :] += mm(top, weight) + mm(rest, weight)

        sweep(R // CH, body)

    done = [0]

    def counts_until(last):
        last = groups * last // 16
        count_groups(done[0], last)
        done[0] = last

    def zero(i):
        g.zacc[at(i, CH), :] = jnp.zeros((CH, C), F32)

    loop(R // CH, zero)
    for i in (0, 1, 2):
        load(i).wait()
    hidden(me_n)
    counts_until(4)
    loop(N, share_pass, 1)
    quarter_send(1)
    counts_until(8)
    share_forward(1)

    def take(d):
        arrived("sf0", d, g.nwfull.at[0, 0:half])
        hidden(behind_n(d))

    share_forward(2)
    arrived("nb", 0, g.nbfull.at[0 : N - 1])
    take(1)
    loop(N, share_forward, 3)
    take(2)
    quarter_send(2)
    loop(N, take, 3)

    def column_max(i, most):
        return jnp.maximum(most, jnp.max(jnp.abs(g.zacc[at(i, CH), :]), axis=0, keepdims=True))

    most = lax.fori_loop(0, R // CH, column_max, jnp.full((1, C), 1e-30, F32))
    scale = most * (1.0 / 32766.0)
    g.zscale[...] = jnp.broadcast_to(scale, (8, C))
    loop(W, lambda d: zscale_copy(d).start(), 1)
    inv_scale = 1.0 / scale

    def code_z(i):
        rows = at(i, CH)
        whole = jnp.round(g.zacc[rows, :] * inv_scale)
        high = jnp.floor(whole * (1.0 / 256.0))
        g.zqa[rows, :] = high.astype(BF16)
        g.zqb[rows, :] = (whole - high * 256.0).astype(BF16)

    loop(R // CH, code_z)

    def send_z(d):
        peer = peer_w(d)
        picked = mm(g.sel[peer], g.zqa[...]) * 256.0 + mm(g.sel[peer], g.zqb[...])
        g.zsend[peer] = picked.astype(I32).astype(I16)
        z_copy(d).start()

    near = W // 4 + 1
    loop(near, send_z, 1)
    counts_until(10)
    loop(W, send_z, near)

    def split_z(i):
        rows = at(i, CH)
        value = g.zacc[rows, :]
        top = value.astype(BF16)
        g.zhi[rows, :] = top
        g.zlo[rows, :] = (value - top.astype(F32)).astype(BF16)

    loop(R // CH, split_z)
    counts_until(16)
    load(7).wait()
    load(9).wait()

    def own_part(i):
        rows = at(i, CH)
        value = mm(g.feats[rows, :], g.wfull[me_n, 0:D, :]) + g.cb[...].astype(F32).reshape(1, C)
        g.self_t[:, rows] = value.T
        g.cot_t[:, rows] = g.cot[rows, :].astype(F32).T
        total = jnp.zeros((CH, C), F32)
        for h in range(z.local):
            part = slice(h * CAP, (h + 1) * CAP)
            block = g.counts[h, rows, :]
            total += mm(block, g.zhi[part, :]) + mm(block, g.zlo[part, :])
        g.acc[rows, :] = total

    sweep(R // CH, own_part)
    ones = jnp.ones((16, 128), BF16)
    g.invs[...] = 2.0 / mm_nt(ones, g.wts[...].astype(BF16))

    def mine_t(i):
        cols = at(i, C)
        g.msg_t[cols, :] = g.msg[at(me_n, U), cols].astype(F32).T.astype(BF16)

    loop(D // C, mine_t)

    def take_z(d):
        s = peer_w(d)
        piece = min(32, CAP)
        for i in range(CAP // piece):
            rows = at(i, piece)
            value = g.ztab[s, rows, :].astype(I32).astype(F32) * g.zscales[s, 0:1, :]
            top = value.astype(BF16)
            g.thi[s, rows, :] = top
            g.tlo[s, rows, :] = (value - top.astype(F32)).astype(BF16)

    def pool(first, last):
        loop(last, take_z, first)

        def body(i):
            rows = at(i, CH)

            def add(d, total):
                s = peer_w(d)
                block = g.counts[z.local + s, rows, :]
                return total + mm(block, g.thi[s]) + mm(block, g.tlo[s])

            g.acc[rows, :] = lax.fori_loop(first, last, add, g.acc[rows, :], unroll=W <= 8)

        sweep(R // CH, body)

    arrived("zs", 0, g.zscales.at[0 : W - 1])
    loop(near, lambda d: z_copy(d).wait_recv(), 1)
    pool(1, near)
    loop(W, lambda d: z_copy(d).wait_recv(), near)
    for k in (1, 2):
        loop(N, functools.partial(quarter_pass, k), 1)
    pool(near, W)
    def activate(i):
        rows = at(i, CH)
        pre = g.acc[rows, :].T * g.invs[0:1, rows] + g.self_t[:, rows]
        g.self_t[:, rows] = pre
        act = jnp.maximum(pre, 0.0)
        squares = jnp.sum(act * act, axis=0, keepdims=True)
        inner = jnp.sum(act * g.cot_t[:, rows], axis=0, keepdims=True)
        g.stat[2 * i : 2 * i + 2, :] = jnp.concatenate([squares, inner], axis=0)

    sweep(R // CH, activate)
    loop(N, lambda d: stat_copy(d).start(), 1)
    arrived("st", 0, g.stats.at[0 : N - 1])
    g.stats[me_n] = g.stat[...]

    def norms(i):
        total = g.stats[0, 2 * i : 2 * i + 2, :]
        for s in range(1, N):
            total += g.stats[s, 2 * i : 2 * i + 2, :]
        return lax.rsqrt(total[0:1] / D + EPSILON), total[1:2]

    def grad_act(i):
        rows = at(i, CH)
        inv, inner = norms(i)
        pre = g.self_t[:, rows]
        act = jnp.maximum(pre, 0.0)
        grad = g.cot_t[:, rows] * inv - act * (inner * (inv * inv * inv) / D)
        grad = jnp.where(pre > 0, grad, 0.0)
        g.gp[:, rows] = grad.astype(BF16)
        g.gps[:, rows] = (grad * g.invs[0:1, rows]).astype(BF16)

    sweep(R // CH, grad_act)
    loop(N, lambda d: gp_copy(d).start(), 1)

    def send_ret(d):
        peer = peer_w(d)
        g.gsend[peer] = mm(g.gps[...], g.counts[z.local + peer]).astype(BF16)
        ret_copy(0, d).start()

    loop(W, send_ret, 1)

    def more_ret(p):
        loop(W, lambda d: ret_copy(p, d).start(), 1)

    more_ret(1)
    for k in (1, 2):
        loop(N, functools.partial(quarter_forward, k), 1)
    join = max(1, 128 // CAP)
    for h in range(0, z.local, join):
        parts = [mm(g.gps[...], g.counts[h + q]) for q in range(join)]
        parts = jnp.concatenate(parts, axis=1) if join > 1 else parts[0]
        g.yacc[:, h * CAP : (h + join) * CAP] = parts

    def embed(i):
        rows = at(i, CH)
        inv, _ = norms(i)
        value = jnp.maximum(g.self_t[:, rows], 0.0) * inv
        g.emb[rows, :] = value.T.astype(BF16)

    sweep(R // CH, embed)
    emb_store = pltpu.make_async_copy(g.emb, g.emb_out, g.store.at[4])
    emb_store.start()
    more_ret(2)

    LW = min(512, D)

    def grad_self(i):
        lanes = at(i, LW)
        g.gc[0, :, lanes] = mm(g.gp[...], g.feats[:, lanes]).astype(BF16)

    sweep(D // LW, grad_self)
    ones_r = jnp.ones((8, R), BF16)
    g.gcb[...] = mm_nt(ones_r, g.gp[...])

    g.gprows[me_n] = g.gp[:, at(me_n, U)]

    def take_ret(p):
        part = at(p, C // PARTS)
        arrived("gr", p, g.gret.at[0 : W - 1, part])

        def body(i):
            lanes = at(i, CH)

            def add(d, total):
                s = peer_w(d)
                return total + mm(g.gret[s, part, :], g.sel[s, :, lanes])

            total = lax.fori_loop(1, W, add, g.yacc[part, lanes], unroll=W <= 8)
            g.y[part, lanes] = total.astype(BF16)

        sweep(R // CH, body)
        loop(N, lambda d: y_copy(p, d).start(), 1)

    for p in range(PARTS):
        take_ret(p)
        if p + 3 < PARTS:
            more_ret(p + 3)
    g.yrows[me_n] = g.y[:, at(me_n, U)]

    def grad_pool(i):
        lanes = at(i, LW)
        g.gc[1, :, lanes] = mm(g.y[...], g.msg[:, lanes]).astype(BF16)

    sweep(D // LW, grad_pool)
    loop(W, lambda d: bias_copy("bc", g.gcb, g.gcb_in, d).start(), 1)
    pair_start("c")

    reduce_pair("c")
    arrived("sf1", 0, g.wfull.at[0 : N - 1, 0:half])
    arrived("y", 0, g.yrows.at[0 : N - 1])

    def hidden_rows(i):
        rows = at(i, CH)
        wrows = slice(D + i * CH, D + (i + 1) * CH)
        total = jnp.zeros((CH, U), F32)
        for s in range(N):
            total += mm(g.wfull[s, wrows, :], g.yrows[s])
        g.gh[rows, :] = jnp.where(g.msg_t[rows, :] > 0, total, 0.0).astype(BF16)

    sweep(D // CH, hidden_rows)
    loop(N, lambda d: gh_copy(0, d).start(), 1)
    g.ghc[me_n] = g.gh[at(me_n, C), :]

    def feature_rows(i):
        rows = at(i, CH)
        total = jnp.zeros((CH, U), F32)
        for s in range(N):
            total += mm(g.wfull[s, rows, :], g.gprows[s]) + mm(g.nwfull[s, rows, :], g.gh[s * C : (s + 1) * C, :])
        g.gfb[rows, :] = total.astype(BF16)

    arrived("gp", 0, g.gprows.at[0 : N - 1])
    arrived("sf2", 0, g.wfull.at[0 : N - 1, 0:half])
    sweep(D // CH, feature_rows)
    gf_store = pltpu.make_async_copy(g.gfb.at[at(me_n, C)], g.gf_out.at[me_n], g.store.at[3])
    gf_store.start()

    reduce_sum("c")

    def grad_neigh(q):
        rows = at(q, C // 2)
        out = (g.gn0, g.gn1)[q]

        def body(i):
            lanes = at(i, LW)
            total = jnp.zeros((C // 2, LW), F32)
            for s in range(N):
                total += mm(g.ghc[s, rows, :], g.feats[s * U : (s + 1) * U, lanes])
            out[0, :, lanes] = total.astype(BF16)

        sweep(D // LW, body)

    loop(N, lambda d: gh_copy(1, d).start(), 1)
    arrived("gh", 0, g.ghc.at[0 : N - 1, 0 : C // 2])
    grad_neigh(0)
    pair_start("n0")
    arrived("gh", 1, g.ghc.at[0 : N - 1, 0 : C // 2])
    loop(N, lambda d: gf_copy(d).start(), 1)
    reduce_pair("n0")
    grad_neigh(1)
    pair_start("n1")
    total = jnp.zeros((8, C), F32)
    ones_u = jnp.ones((8, U), BF16)
    for s in range(N):
        total += mm_nt(ones_u, g.ghc[s])
    g.gnb[...] = total
    loop(W, lambda d: bias_copy("bn", g.gnb, g.gnb_in, d).start(), 1)
    gc_store = gather_pass("c")
    reduce_pair("n1")
    reduce_sum("n0")
    def bias_sum(name, own, others):
        arrived(name, 0, others.at[0 : W - 1])
        left(name, others.at[0 : W - 1])
        own[...] = lax.fori_loop(1, W, lambda d, total: total + others[peer_w(d)], own[...])

    bias_sum("bc", g.gcb, g.gcb_in)
    bias_sum("bn", g.gnb, g.gnb_in)
    gcb_store = pltpu.make_async_copy(g.gcb, g.gcb_out, g.store.at[5])
    gnb_store = pltpu.make_async_copy(g.gnb, g.gnb_out, g.store.at[6])
    gcb_store.start()
    gnb_store.start()
    reduce_sum("n1")
    gn0_store = gather_pass("n0")
    gn1_store = gather_pass("n1")
    for k in SUMS:
        gather_wait(k)
    arrived("gf", 0, g.gf_out.at[0 : N - 1])

    left("sh0", g.nwfull.at[0 : N - 1, 0:part_w])
    left("sp0", g.nwfull.at[0 : N - 1, 0 : (W // 2 - 1) * part_w])
    left("sf0", g.nwfull.at[0 : N - 1, 0:half])
    for k in (1, 2):
        left("sh%d" % k, g.wfull.at[0 : N - 1, 0 : 2 * eighth])
        left("sp%d" % k, g.wfull.at[0 : N - 1, 0 : 2 * eighth])
        left("sf%d" % k, g.wfull.at[0 : N - 1, 0:half])
    left("nb", g.nbfull.at[0 : N - 1])
    left("z", g.zsend.at[0 : W - 1])
    left("zs", g.zscales.at[0 : W - 1])
    left("st", g.stats.at[0 : N - 1])
    left("gp", g.gprows.at[0 : N - 1])
    left("gr", g.gsend.at[0 : W - 1])
    left("y", g.yrows.at[0 : N - 1])
    left("gh", g.ghc.at[0 : N - 1])
    left("gf", g.gf_out.at[0 : N - 1])
    for k in SUMS:
        left("hs" + k, grad(k, "_half"))
        left("rs" + k, grad(k, "_in").at[0 : W // 2 - 1])
        left("ag" + k, grad(k, "_in").at[0 : W // 2 - 1])
        left("fw" + k, grad(k, "_sum").at[core_rows(k, core)])
    for store in (emb_store, gf_store, gc_store, gcb_store, gnb_store, gn0_store, gn1_store):
        store.wait()


def finish(z, *refs):
    names = ["emb", "gf", "gn", "gc", "gnb", "gcb"]
    ins = dict(zip(names, refs[:6]))
    outs = dict(zip(names, refs[6:12]))
    emb, gf, gn, gc, nb, cb, gf_t, gn_t, gc_t, nb_t, cb_t, load, store = refs[12:]
    D, C, N, U = z.width, z.cols, z.narrow, z.part
    step = D // N
    emb_load = pltpu.make_async_copy(ins["emb"], emb, load.at[4 * N + 2])
    emb_load.start()
    jobs = []
    for p in range(2):
        for i in range(N):
            lanes = slice(i * step, (i + 1) * step)
            jobs.append((ins["gc"].at[p, :, lanes], gc.at[p, :, lanes], gc_t.at[p, lanes], outs["gc"].at[p, lanes]))
    for i in range(N):
        lanes = slice(i * step, (i + 1) * step)
        jobs.append((ins["gn"].at[0, :, lanes], gn.at[:, lanes], gn_t.at[lanes], outs["gn"].at[lanes]))
    for i in range(N):
        rows = slice(i * U, (i + 1) * U)
        jobs.append((ins["gf"].at[i], gf.at[i], gf_t.at[rows], outs["gf"].at[rows]))
    loads = [pltpu.make_async_copy(src, held, load.at[i]) for i, (src, held, _, _) in enumerate(jobs)]
    loads += [pltpu.make_async_copy(ins[k], v, load.at[len(jobs) + i]) for i, (k, v) in enumerate((("gnb", nb), ("gcb", cb)))]
    for copy in loads:
        copy.start()
    stores = [pltpu.make_async_copy(emb, outs["emb"], store.at[0])]
    emb_load.wait()
    stores[0].start()
    for i, (_, held, turned, out) in enumerate(jobs):
        loads[i].wait()
        turned[...] = held[...].astype(F32).T
        stores.append(pltpu.make_async_copy(turned, out, store.at[1 + i]))
        stores[-1].start()
    for i, (k, v, t) in enumerate((("gnb", nb, nb_t), ("gcb", cb, cb_t))):
        loads[len(jobs) + i].wait()
        t[...] = v[0:1, :]
        stores.append(pltpu.make_async_copy(t, outs[k], store.at[1 + len(jobs) + i]))
        stores[-1].start()
    for copy in stores:
        copy.wait()


def shards(wide, narrow, node_feats, neigh_weight, neigh_bias, combine_weight, combine_bias, cotangent,
           neighbour_slot, neighbour_mask, visit_count, send_rows):
    z = Sizes(node_feats, neigh_weight, send_rows, neighbour_slot.T, wide, narrow)
    R, D, C, W, N, U = z.rows, z.width, z.cols, z.wide, z.narrow, z.part
    bufs, sems, kinds = scratch(z)
    names = NAMES_IN + NAMES_OUT + list(bufs) + list(sems)
    outs = (
        jax.ShapeDtypeStruct((R, C), BF16),
        jax.ShapeDtypeStruct((N, C, U), BF16),
        jax.ShapeDtypeStruct((1, C, D), BF16),
        jax.ShapeDtypeStruct((2, C, D), BF16),
        jax.ShapeDtypeStruct((8, C), F32),
        jax.ShapeDtypeStruct((8, C), F32),
    )
    emb, gf, gn, gc, gnb, gcb = pl.pallas_call(
        functools.partial(kernel, z, names, kinds),
        out_shape=outs,
        in_specs=[pl.BlockSpec(memory_space=pl.ANY)] * len(NAMES_IN),
        out_specs=[pl.BlockSpec(memory_space=pl.ANY)] * len(NAMES_OUT),
        scratch_shapes=list(bufs.values()) + list(sems.values()),
        compiler_params=pltpu.CompilerParams(
            collective_id=0, has_side_effects=True, vmem_limit_bytes=60 * 2**20
        ),
        cost_estimate=pl.CostEstimate(flops=2 * 10**10, bytes_accessed=2 * 10**7, transcendentals=0),
        name="layer",
    )(
        node_feats, neigh_weight, neigh_bias, combine_weight, combine_bias, cotangent,
        neighbour_slot.T, neighbour_mask.T, visit_count.T, send_rows,
    )
    hbm = pl.BlockSpec(memory_space=pl.ANY)
    emb, grad_features, grad_neigh, grad_combine, gnb, gcb = pl.pallas_call(
        functools.partial(finish, z),
        out_shape=(
            jax.ShapeDtypeStruct((R, C), BF16),
            jax.ShapeDtypeStruct((R, C), F32),
            jax.ShapeDtypeStruct((D, C), F32),
            jax.ShapeDtypeStruct((2, D, C), F32),
            jax.ShapeDtypeStruct((1, C), F32),
            jax.ShapeDtypeStruct((1, C), F32),
        ),
        in_specs=[hbm] * 6,
        out_specs=[hbm] * 6,
        scratch_shapes=[
            pltpu.VMEM((R, C), BF16),
            pltpu.VMEM((N, C, U), BF16),
            pltpu.VMEM((C, D), BF16),
            pltpu.VMEM((2, C, D), BF16),
            pltpu.VMEM((8, C), F32),
            pltpu.VMEM((8, C), F32),
            pltpu.VMEM((R, C), F32),
            pltpu.VMEM((D, C), F32),
            pltpu.VMEM((2, D, C), F32),
            pltpu.VMEM((1, C), F32),
            pltpu.VMEM((1, C), F32),
            pltpu.SemaphoreType.DMA((4 * N + 3,)),
            pltpu.SemaphoreType.DMA((4 * N + 3,)),
        ],
        compiler_params=pltpu.CompilerParams(vmem_limit_bytes=60 * 2**20),
        name="finish",
    )(emb, gf, gn, gc, gnb, gcb)
    return emb, grad_features, grad_neigh, gnb.reshape(C), grad_combine.reshape(2 * D, C), gcb.reshape(C)


def solution(mesh):
    placed = (
        P("wide", None),
        P(None, "narrow"),
        P("narrow"),
        P(None, "narrow"),
        P("narrow"),
        P("wide", "narrow"),
        P("wide", None),
        P("wide", None),
        P("wide", None),
        P("wide", None),
    )
    return jax.shard_map(
        functools.partial(shards, mesh.shape["wide"], mesh.shape["narrow"]),
        mesh=mesh,
        in_specs=placed,
        out_specs=(
            P("wide", "narrow"),
            P("wide", "narrow"),
            P(None, "narrow"),
            P("narrow"),
            P(None, "narrow"),
            P("narrow"),
        ),
        check_vma=False,
    )
```

time: 113 us -> 101 us (0.89)
  the two profiles are of different devices: /device:TPU:25 before, /device:TPU:0 now
where the time goes in v5:
time: 101 us
  Pallas kernels  99.7 us (99%)
    pallas_call x1, Pallas kernels, shards(): pl.pallas_call(functools.partial(kernel, z, names, kinds), out_shape=outs...  95.9 us
    pallas_call x1, Pallas kernels, shards(): pl.pallas_call(functools.partial(finish, z), out_shape=(jax.ShapeDtypeStr...  3.79 us

profile of v5, /device:TPU:0, one launch (start us, length us, event | category | flops | bytes accessed | tf_op | source)
XLA Modules:
  0.0 100.5 jit_solution(616737641066874242)
XLA Ops:
  0.6 95.9 %layer.1 = (bf16[1024,256]{1,0:T(8,128)(2,1)}, bf16[4,256,256]{2,1,0:T(8,128)(2,1)}, bf16[1,256,1024]{2,1,0:T(8,128)(2,1)}, bf16[2,256,1024]{2,1,0:T(8,128)(2,1)}, f32[8,256]{1,0:T(8,128)}, /*index=5*/f32[8,256]{1,0:T(8,128)}) custom-call(bf16[1024,1024]{1,0:T(8,128)(2,1)} %refs_0_.1, bf16[1024,256]{1,0:T(8,128)(2,1)} %refs_1_.1, bf16[256]{0:T(256)(128)(2,1)} %refs_2_.1, ...), custom_call_target="tpu_custom_call" | custom-call | flops 20000000000 | bytes 20000000 | tf_op jit(solution)/shard_map/layer/pallas_call | solution.py:854
  96.6 3.8 %finish.1 = (bf16[1024,256]{1,0:T(8,128)(2,1)}, f32[1024,256]{1,0:T(8,128)}, f32[1024,256]{1,0:T(8,128)}, f32[2,1024,256]{2,1,0:T(8,128)}, f32[1,256]{1,0:T(1,128)}, /*index=5*/f32[1,256]{1,0:T(1,128)}) custom-call(bf16[1024,256]{1,0:T(8,128)(2,1)} %get-tuple-element.18.refs_0_, bf16[4,256,256]{2,1,0:T(8,128)(2,1)} %get-tuple-element.19.refs_1_, ...), custom_call_target="tpu_custom_call" | custom-call | tf_op jit(solution)/shard_map/finish/pallas_call | solution.py:870

commit v6 on v5

--- a/solution.py
+++ b/solution.py
@@ -95,6 +95,10 @@
         emb=v(R, C, BF16),
         gp=v(C, R, BF16),
         gps=v(C, R, BF16),
+        act=v(C, R, BF16),
+        actrows=v(N, C, U, BF16),
+        cotrows=v(N, U, C, BF16),
+        cotrows_t=v(N, C, U, F32),
         gprows=v(N, C, U, BF16),
         gsend=v(W, C, CAP, BF16),
         gret=v(W, C, CAP, BF16),
@@ -104,7 +108,8 @@
         msg_t=v(D, U, BF16),
         gh=v(D, U, BF16),
         ghc=v(N, C, U, BF16),
-        gfb=v(D, U, BF16),
+        gft=v(N, U, C, BF16),
+        gct=v(2, D, C, BF16),
         gc=v(2, C, D, BF16),
         gc_half=v(2, C // 2, D, BF16),
         gc_in=v(W // 2, 2, z.red(C)[0], z.red(C)[2], BF16),
@@ -123,12 +128,13 @@
         gnb_in=v(W, 8, C, F32),
     )
     kinds = dict(
-        sh0=N, sh1=N, sh2=N, sp0=N, sp1=N, sp2=N, sf0=N, sf1=1, sf2=1, nb=1, st=1, gp=1, y=1, gh=2, gf=1,
+        sh0=N, sh1=N, sh2=N, sp0=N, sp1=N, sp2=N, sf0=N, sf1=1, sf2=1, nb=1, st=1, ct=1, ac=1, y=1, gh=2, gf=1,
         z=W, zs=1, gr=PARTS, bc=1, bn=1,
     )
     for k in SUMS:
         kinds.update({"hs" + k: 1, "rs" + k: 1, "ag" + k: 1, "fw" + k: 1})
     sems = {name + "_r": pltpu.SemaphoreType.DMA((count,)) for name, count in kinds.items()}
+    sems["turn"] = pltpu.SemaphoreType.REGULAR
     sems["sent"] = pltpu.SemaphoreType.DMA((len(kinds),))
     sems["load"] = pltpu.SemaphoreType.DMA((10,))
     sems["store"] = pltpu.SemaphoreType.DMA((7,))
@@ -199,62 +205,63 @@
     def left(name, ref):
         remote(name, 0, ref, ref, "narrow", peer_n(1)).wait_send()
 
-    hops = (2, 4)
-    first = (None, D, 0)
-    eighth = D // 8
-
     def rows_at(start, size):
         return pl.ds(pl.multiple_of(start, size), size)
 
+    sources = (g.nw_in, None, g.comb_in)
+    fulls = (g.nwfull, None, g.wfull)
+    part_w = D // W
+
+    def share():
+        return rows_at((core * (W // 2) + me_w // 2) * part_w, part_w)
+
+    def share_send(k):
+        def body(d):
+            remote("sh%d" % k, d, sources[k].at[share()], fulls[k].at[me_n, share()], "narrow", ahead_n(d)).start()
+
+        loop(N, body, 1)
+
+    def share_pass(k):
+        def body(d):
+            part = fulls[k].at[behind_n(d), share()]
+            arrived("sh%d" % k, d, part)
+            loop(W // 2, lambda e: remote("sp%d" % k, d, part, part, "wide", across(2 * e)).start(), 1)
+
+        loop(N, body, 1)
+
+    def share_forward(k, d):
+        s = behind_n(d)
+        arrived("sp%d" % k, d, fulls[k].at[s, 0 : (W // 2 - 1) * part_w])
+        part = fulls[k].at[s, rows_at(core * half, half)]
+        remote("sf%d" % k, d if k == 0 else 0, part, part, "wide", sibling).start()
+
+    hops = (2, 4)
+    eighth = D // 8
+
     def hop_bit(h):
         return lax.rem(me_w // hops[h], 2)
 
-    def quarter(k, h):
-        return rows_at(first[k] + h * half + (2 * core + hop_bit(h)) * eighth, eighth)
-
-    def quarter_copy(k, d, h):
-        mine = quarter(k, h)
-        return remote("sh%d" % k, d, g.comb_in.at[mine], g.wfull.at[me_n, mine], "narrow", ahead_n(d))
-
-    def quarter_send(k):
-        def body(d):
-            for h in range(2):
-                quarter_copy(k, d, h).start()
-
-        loop(N, body, 1)
-
-    def quarter_pass(k, d):
+    def quarter(h):
+        return rows_at(D + h * half + (2 * core + hop_bit(h)) * eighth, eighth)
+
+    def quarter_send(d):
+        for h in range(2):
+            mine = quarter(h)
+            remote("sh1", d, g.comb_in.at[mine], g.wfull.at[me_n, mine], "narrow", ahead_n(d)).start()
+
+    def quarter_pass(d):
         s = behind_n(d)
-        arrived("sh%d" % k, d, g.wfull.at[s, 0 : 2 * eighth])
+        arrived("sh1", d, g.wfull.at[s, 0 : 2 * eighth])
         for h in range(2):
-            part = g.wfull.at[s, quarter(k, h)]
-            remote("sp%d" % k, d, part, part, "wide", me_w + hops[h] - 2 * hops[h] * hop_bit(h)).start()
-
-    def quarter_forward(k, d):
+            part = g.wfull.at[s, quarter(h)]
+            remote("sp1", d, part, part, "wide", me_w + hops[h] - 2 * hops[h] * hop_bit(h)).start()
+
+    def quarter_forward(d):
         s = behind_n(d)
-        arrived("sp%d" % k, d, g.wfull.at[s, 0 : 2 * eighth])
+        arrived("sp1", d, g.wfull.at[s, 0 : 2 * eighth])
         for h in range(2):
-            part = g.wfull.at[s, rows_at(first[k] + h * half + 2 * core * eighth, 2 * eighth)]
-            remote("sf%d" % k, 0, part, part, "wide", sibling).start()
-
-    part_w = D // W
-
-    def share():
-        return rows_at((core * (W // 2) + me_w // 2) * part_w, part_w)
-
-    def share_send(d):
-        remote("sh0", d, g.nw_in.at[share()], g.nwfull.at[me_n, share()], "narrow", ahead_n(d)).start()
-
-    def share_pass(d):
-        part = g.nwfull.at[behind_n(d), share()]
-        arrived("sh0", d, part)
-        loop(W // 2, lambda e: remote("sp0", d, part, part, "wide", across(2 * e)).start(), 1)
-
-    def share_forward(d):
-        s = behind_n(d)
-        arrived("sp0", d, g.nwfull.at[s, 0 : (W // 2 - 1) * part_w])
-        part = g.nwfull.at[s, rows_at(core * half, half)]
-        remote("sf0", d, part, part, "wide", sibling).start()
+            part = g.wfull.at[s, rows_at(D + h * half + 2 * core * eighth, 2 * eighth)]
+            remote("sf1", 0, part, part, "wide", sibling).start()
 
     def nb_copy(d):
         return remote("nb", 0, g.nbfull.at[me_n], g.nbfull.at[me_n], "narrow", peer_n(d))
@@ -269,9 +276,13 @@
     def stat_copy(d):
         return remote("st", 0, g.stat, g.stats.at[me_n], "narrow", peer_n(d))
 
-    def gp_copy(d):
+    def cot_copy(d):
         s = peer_n(d)
-        return remote("gp", 0, g.gp.at[:, at(s, U)], g.gprows.at[me_n], "narrow", s)
+        return remote("ct", 0, g.cot_in.at[at(s, U)], g.cotrows.at[me_n], "narrow", s)
+
+    def act_copy(d):
+        s = peer_n(d)
+        return remote("ac", 0, g.act.at[:, at(s, U)], g.actrows.at[me_n], "narrow", s)
 
     def ret_copy(p, d):
         peer, rows = peer_w(d), at(p, C // PARTS)
@@ -287,7 +298,7 @@
 
     def gf_copy(d):
         s = peer_n(d)
-        return remote("gf", 0, g.gfb.at[at(s, C)], g.gf_out.at[me_n], "narrow", s)
+        return remote("gf", 0, g.gft.at[s], g.gf_out.at[me_n], "narrow", s)
 
     def bias_copy(name, src, dst, d):
         return remote(name, 0, src, dst.at[me_w], "wide", peer_w(d))
@@ -308,7 +319,7 @@
     def out_rows(k, which):
         rows = grad(k).shape[1]
         if k == "c":
-            return g.gc_out.at[:, at(which, rows // 2)]
+            return g.gc_sum.at[:, at(which, rows // 2)]
         return g.gn_out.at[:, rows_at(int(k[1]) * rows + which * (rows // 2), rows // 2)]
 
     def pair_start(k):
@@ -340,6 +351,8 @@
         arrived("ag" + k, 0, grad(k, "_in").at[0 : W // 2 - 1])
         part = grad(k, "_sum").at[core_rows(k, core)]
         remote("fw" + k, 0, part, out_rows(k, core), "wide", sibling).start()
+        if k == "c":
+            return None
         store = pltpu.make_async_copy(part, out_rows(k, core), g.store.at[SUMS.index(k)])
         store.start()
         return store
@@ -369,19 +382,8 @@
     order = (6, 8, 3, 4, 5, 0, 1, 2, 7, 9)
     for i in order:
         load(i).start()
-    load(6).wait()
-    g.send_t[...] = g.send[...].T
-
-    def select(d):
-        r = peer_w(d)
-        which = lax.broadcasted_iota(I32, (CAP, W), 1)
-        col = jnp.sum(jnp.where(which == r, g.send_t[...], 0), axis=1, keepdims=True)
-        place_u = lax.broadcasted_iota(I32, (CAP, R), 1)
-        g.sel[r] = jnp.where(place_u == col, 1.0, 0.0).astype(BF16)
-
-    loop(W, select, 1)
     pl.semaphore_wait(barrier, W - 1 + N - 1)
-    loop(N, share_send, 1)
+    share_send(0)
     load(8).wait()
     g.nbfull[me_n] = jnp.broadcast_to(g.nb[...].astype(F32).reshape(1, C), (8, C))
     loop(N, lambda d: nb_copy(d).start(), 1)
@@ -472,22 +474,35 @@
     for i in (0, 1, 2):
         load(i).wait()
     hidden(me_n)
-    counts_until(4)
-    loop(N, share_pass, 1)
-    quarter_send(1)
+    counts_until(2)
+    load(6).wait()
+    g.send_t[...] = g.send[...].T
+
+    def select(d):
+        r = peer_w(d)
+        which = lax.broadcasted_iota(I32, (CAP, W), 1)
+        col = jnp.sum(jnp.where(which == r, g.send_t[...], 0), axis=1, keepdims=True)
+        place_u = lax.broadcasted_iota(I32, (CAP, R), 1)
+        g.sel[r] = jnp.where(place_u == col, 1.0, 0.0).astype(BF16)
+
+    loop(W, select, 1)
+    share_pass(0)
+    loop(N, quarter_send, 1)
     counts_until(8)
-    share_forward(1)
+    share_forward(0, 1)
 
     def take(d):
         arrived("sf0", d, g.nwfull.at[0, 0:half])
         hidden(behind_n(d))
 
-    share_forward(2)
+    counts_until(10)
+    share_forward(0, 2)
+    loop(N, lambda d: cot_copy(d).start(), 1)
     arrived("nb", 0, g.nbfull.at[0 : N - 1])
     take(1)
-    loop(N, share_forward, 3)
+    loop(N, functools.partial(share_forward, 0), 3)
     take(2)
-    quarter_send(2)
+    share_send(2)
     loop(N, take, 3)
 
     def column_max(i, most):
@@ -516,7 +531,7 @@
 
     near = W // 4 + 1
     loop(near, send_z, 1)
-    counts_until(10)
+    counts_until(12)
     loop(W, send_z, near)
 
     def split_z(i):
@@ -576,26 +591,33 @@
 
             g.acc[rows, :] = lax.fori_loop(first, last, add, g.acc[rows, :], unroll=W <= 8)
 
-        sweep(R // CH, body)
+        return body
 
     arrived("zs", 0, g.zscales.at[0 : W - 1])
-    loop(near, lambda d: z_copy(d).wait_recv(), 1)
-    pool(1, near)
-    loop(W, lambda d: z_copy(d).wait_recv(), near)
-    for k in (1, 2):
-        loop(N, functools.partial(quarter_pass, k), 1)
-    pool(near, W)
+    for first_d, last_d in ((1, near), (W - 1, W)):
+        loop(last_d, lambda d: z_copy(d).wait_recv(), first_d)
+        sweep(R // CH, pool(first_d, last_d))
+    loop(W - 1, lambda d: z_copy(d).wait_recv(), near)
+    loop(N, quarter_pass, 1)
+    pool_rest = pool(near, W - 1)
+
     def activate(i):
+        pool_rest(i)
         rows = at(i, CH)
         pre = g.acc[rows, :].T * g.invs[0:1, rows] + g.self_t[:, rows]
         g.self_t[:, rows] = pre
         act = jnp.maximum(pre, 0.0)
+        g.act[:, rows] = act.astype(BF16)
         squares = jnp.sum(act * act, axis=0, keepdims=True)
         inner = jnp.sum(act * g.cot_t[:, rows], axis=0, keepdims=True)
         g.stat[2 * i : 2 * i + 2, :] = jnp.concatenate([squares, inner], axis=0)
 
     sweep(R // CH, activate)
     loop(N, lambda d: stat_copy(d).start(), 1)
+    pl.semaphore_signal(g.turn, inc=1, device_id={"wide": sibling}, device_id_type=MESH)
+    g.actrows[me_n] = g.act[:, at(me_n, U)]
+    pl.semaphore_wait(g.turn, 1)
+    loop(N, lambda d: act_copy(d).start(), 1)
     arrived("st", 0, g.stats.at[0 : N - 1])
     g.stats[me_n] = g.stat[...]
 
@@ -616,7 +638,6 @@
         g.gps[:, rows] = (grad * g.invs[0:1, rows]).astype(BF16)
 
     sweep(R // CH, grad_act)
-    loop(N, lambda d: gp_copy(d).start(), 1)
 
     def send_ret(d):
         peer = peer_w(d)
@@ -629,8 +650,7 @@
         loop(W, lambda d: ret_copy(p, d).start(), 1)
 
     more_ret(1)
-    for k in (1, 2):
-        loop(N, functools.partial(quarter_forward, k), 1)
+    more_ret(2)
     join = max(1, 128 // CAP)
     for h in range(0, z.local, join):
         parts = [mm(g.gps[...], g.counts[h + q]) for q in range(join)]
@@ -646,7 +666,7 @@
     sweep(R // CH, embed)
     emb_store = pltpu.make_async_copy(g.emb, g.emb_out, g.store.at[4])
     emb_store.start()
-    more_ret(2)
+    more_ret(3)
 
     LW = min(512, D)
 
@@ -658,7 +678,6 @@
     ones_r = jnp.ones((8, R), BF16)
     g.gcb[...] = mm_nt(ones_r, g.gp[...])
 
-    g.gprows[me_n] = g.gp[:, at(me_n, U)]
 
     def take_ret(p):
         part = at(p, C // PARTS)
@@ -677,10 +696,11 @@
         sweep(R // CH, body)
         loop(N, lambda d: y_copy(p, d).start(), 1)
 
-    for p in range(PARTS):
+    take_ret(0)
+    loop(N, quarter_forward, 1)
+    share_pass(2)
+    for p in range(1, PARTS):
         take_ret(p)
-        if p + 3 < PARTS:
-            more_ret(p + 3)
     g.yrows[me_n] = g.y[:, at(me_n, U)]
 
     def grad_pool(i):
@@ -692,6 +712,10 @@
     pair_start("c")
 
     reduce_pair("c")
+    arrived("ct", 0, g.cotrows.at[0 : N - 1])
+    g.cotrows[me_n] = g.cot[at(me_n, U), :]
+    for s in range(N):
+        g.cotrows_t[s] = g.cotrows[s].astype(F32).T
     arrived("sf1", 0, g.wfull.at[0 : N - 1, 0:half])
     arrived("y", 0, g.yrows.at[0 : N - 1])
 
@@ -708,16 +732,31 @@
     g.ghc[me_n] = g.gh[at(me_n, C), :]
 
     def feature_rows(i):
-        rows = at(i, CH)
-        total = jnp.zeros((CH, U), F32)
+        rows = at(i, C)
+        total = jnp.zeros((C, U), F32)
         for s in range(N):
             total += mm(g.wfull[s, rows, :], g.gprows[s]) + mm(g.nwfull[s, rows, :], g.gh[s * C : (s + 1) * C, :])
-        g.gfb[rows, :] = total.astype(BF16)
-
-    arrived("gp", 0, g.gprows.at[0 : N - 1])
+        g.gft[i] = total.T.astype(BF16)
+
+    loop(N, functools.partial(share_forward, 2), 1)
+    arrived("ac", 0, g.actrows.at[0 : N - 1])
+    per = CH // U
+    lanes = at(lax.rem(me_n, per), U) if per > 1 else slice(None)
+    total = g.stats[0, :, lanes]
+    for s in range(1, N):
+        total += g.stats[s, :, lanes]
+    row = lax.broadcasted_iota(I32, total.shape, 0) - 2 * (me_n // per)
+    inv = lax.rsqrt(jnp.sum(jnp.where(row == 0, total, 0.0), axis=0, keepdims=True) / D + EPSILON)
+    inner = jnp.sum(jnp.where(row == 1, total, 0.0), axis=0, keepdims=True)
+    factor = inner * (inv * inv * inv) / D
+    for s in range(N):
+        act = g.actrows[s].astype(F32)
+        grad_rows = jnp.where(act > 0, g.cotrows_t[s] * inv - act * factor, 0.0)
+        g.gprows[s] = grad_rows.astype(BF16)
     arrived("sf2", 0, g.wfull.at[0 : N - 1, 0:half])
-    sweep(D // CH, feature_rows)
-    gf_store = pltpu.make_async_copy(g.gfb.at[at(me_n, C)], g.gf_out.at[me_n], g.store.at[3])
+    loop(N, lambda d: gh_copy(1, d).start(), 1)
+    sweep(N, feature_rows)
+    gf_store = pltpu.make_async_copy(g.gft.at[me_n], g.gf_out.at[me_n], g.store.at[3])
     gf_store.start()
 
     reduce_sum("c")
@@ -735,7 +774,6 @@
 
         sweep(D // LW, body)
 
-    loop(N, lambda d: gh_copy(1, d).start(), 1)
     arrived("gh", 0, g.ghc.at[0 : N - 1, 0 : C // 2])
     grad_neigh(0)
     pair_start("n0")
@@ -750,7 +788,6 @@
         total += mm_nt(ones_u, g.ghc[s])
     g.gnb[...] = total
     loop(W, lambda d: bias_copy("bn", g.gnb, g.gnb_in, d).start(), 1)
-    gc_store = gather_pass("c")
     reduce_pair("n1")
     reduce_sum("n0")
     def bias_sum(name, own, others):
@@ -764,25 +801,33 @@
     gnb_store = pltpu.make_async_copy(g.gnb, g.gnb_out, g.store.at[6])
     gcb_store.start()
     gnb_store.start()
+    gather_pass("c")
     reduce_sum("n1")
     gn0_store = gather_pass("n0")
     gn1_store = gather_pass("n1")
-    for k in SUMS:
+    gather_wait("c")
+    for p in range(2):
+        for i in range(D // CH):
+            g.gct[p, at(i, CH), :] = g.gc_sum[p, :, at(i, CH)].astype(F32).T.astype(BF16)
+    gc_store = pltpu.make_async_copy(g.gct, g.gc_out, g.store.at[0])
+    gc_store.start()
+    for k in SUMS[1:]:
         gather_wait(k)
     arrived("gf", 0, g.gf_out.at[0 : N - 1])
 
-    left("sh0", g.nwfull.at[0 : N - 1, 0:part_w])
-    left("sp0", g.nwfull.at[0 : N - 1, 0 : (W // 2 - 1) * part_w])
-    left("sf0", g.nwfull.at[0 : N - 1, 0:half])
-    for k in (1, 2):
-        left("sh%d" % k, g.wfull.at[0 : N - 1, 0 : 2 * eighth])
-        left("sp%d" % k, g.wfull.at[0 : N - 1, 0 : 2 * eighth])
-        left("sf%d" % k, g.wfull.at[0 : N - 1, 0:half])
+    for k in (0, 2):
+        left("sh%d" % k, fulls[k].at[0 : N - 1, 0:part_w])
+        left("sp%d" % k, fulls[k].at[0 : N - 1, 0 : (W // 2 - 1) * part_w])
+        left("sf%d" % k, fulls[k].at[0 : N - 1, 0:half])
+    left("sh1", g.wfull.at[0 : N - 1, 0 : 2 * eighth])
+    left("sp1", g.wfull.at[0 : N - 1, 0 : 2 * eighth])
+    left("sf1", g.wfull.at[0 : N - 1, 0:half])
     left("nb", g.nbfull.at[0 : N - 1])
     left("z", g.zsend.at[0 : W - 1])
     left("zs", g.zscales.at[0 : W - 1])
     left("st", g.stats.at[0 : N - 1])
-    left("gp", g.gprows.at[0 : N - 1])
+    left("ct", g.cotrows.at[0 : N - 1])
+    left("ac", g.actrows.at[0 : N - 1])
     left("gr", g.gsend.at[0 : W - 1])
     left("y", g.yrows.at[0 : N - 1])
     left("gh", g.ghc.at[0 : N - 1])
@@ -803,36 +848,38 @@
     emb, gf, gn, gc, nb, cb, gf_t, gn_t, gc_t, nb_t, cb_t, load, store = refs[12:]
     D, C, N, U = z.width, z.cols, z.narrow, z.part
     step = D // N
-    emb_load = pltpu.make_async_copy(ins["emb"], emb, load.at[4 * N + 2])
+    emb_load = pltpu.make_async_copy(ins["emb"], emb, load.at[6])
     emb_load.start()
-    jobs = []
+    jobs = [
+        (ins["gn"].at[0], gn, [(gn.at[:, at(i, step)], gn_t.at[at(i, step)], outs["gn"].at[at(i, step)]) for i in range(N)]),
+        (ins["gf"], gf, [(gf.at[i], gf_t.at[at(i, U)], outs["gf"].at[at(i, U)]) for i in range(N)]),
+    ]
     for p in range(2):
-        for i in range(N):
-            lanes = slice(i * step, (i + 1) * step)
-            jobs.append((ins["gc"].at[p, :, lanes], gc.at[p, :, lanes], gc_t.at[p, lanes], outs["gc"].at[p, lanes]))
-    for i in range(N):
-        lanes = slice(i * step, (i + 1) * step)
-        jobs.append((ins["gn"].at[0, :, lanes], gn.at[:, lanes], gn_t.at[lanes], outs["gn"].at[lanes]))
-    for i in range(N):
-        rows = slice(i * U, (i + 1) * U)
-        jobs.append((ins["gf"].at[i], gf.at[i], gf_t.at[rows], outs["gf"].at[rows]))
-    loads = [pltpu.make_async_copy(src, held, load.at[i]) for i, (src, held, _, _) in enumerate(jobs)]
-    loads += [pltpu.make_async_copy(ins[k], v, load.at[len(jobs) + i]) for i, (k, v) in enumerate((("gnb", nb), ("gcb", cb)))]
+        parts = [(gc.at[p, at(i, step)], gc_t.at[p, at(i, step)], outs["gc"].at[p, at(i, step)]) for i in range(N)]
+        jobs.append((ins["gc"].at[p], gc.at[p], parts))
+    loads = [pltpu.make_async_copy(src, held, load.at[i]) for i, (src, held, _) in enumerate(jobs)]
+    small = (("gnb", nb, nb_t), ("gcb", cb, cb_t))
+    loads += [pltpu.make_async_copy(ins[k], held, load.at[4 + i]) for i, (k, held, _) in enumerate(small)]
     for copy in loads:
         copy.start()
     stores = [pltpu.make_async_copy(emb, outs["emb"], store.at[0])]
-    emb_load.wait()
-    stores[0].start()
-    for i, (_, held, turned, out) in enumerate(jobs):
+
+    def keep(src, dst):
+        stores.append(pltpu.make_async_copy(src, dst, store.at[len(stores)]))
+        stores[-1].start()
+
+    for i, (_, _, parts) in enumerate(jobs):
         loads[i].wait()
-        turned[...] = held[...].astype(F32).T
-        stores.append(pltpu.make_async_copy(turned, out, store.at[1 + i]))
-        stores[-1].start()
-    for i, (k, v, t) in enumerate((("gnb", nb, nb_t), ("gcb", cb, cb_t))):
-        loads[len(jobs) + i].wait()
-        t[...] = v[0:1, :]
-        stores.append(pltpu.make_async_copy(t, outs[k], store.at[1 + len(jobs) + i]))
-        stores[-1].start()
+        for k, (part, turned, out) in enumerate(parts):
+            turned[...] = part[...].astype(F32).T if i == 0 else part[...].astype(F32)
+            keep(turned, out)
+        if i == 0:
+            emb_load.wait()
+            stores[0].start()
+    for i, (k, held, turned) in enumerate(small):
+        loads[4 + i].wait()
+        turned[...] = held[0:1, :]
+        keep(turned, outs[k])
     for copy in stores:
         copy.wait()
 
@@ -845,9 +892,9 @@
     names = NAMES_IN + NAMES_OUT + list(bufs) + list(sems)
     outs = (
         jax.ShapeDtypeStruct((R, C), BF16),
-        jax.ShapeDtypeStruct((N, C, U), BF16),
+        jax.ShapeDtypeStruct((N, U, C), BF16),
         jax.ShapeDtypeStruct((1, C, D), BF16),
-        jax.ShapeDtypeStruct((2, C, D), BF16),
+        jax.ShapeDtypeStruct((2, D, C), BF16),
         jax.ShapeDtypeStruct((8, C), F32),
         jax.ShapeDtypeStruct((8, C), F32),
     )
@@ -881,9 +928,9 @@
         out_specs=[hbm] * 6,
         scratch_shapes=[
             pltpu.VMEM((R, C), BF16),
-            pltpu.VMEM((N, C, U), BF16),
+            pltpu.VMEM((N, U, C), BF16),
             pltpu.VMEM((C, D), BF16),
-            pltpu.VMEM((2, C, D), BF16),
+            pltpu.VMEM((2, D, C), BF16),
             pltpu.VMEM((8, C), F32),
             pltpu.VMEM((8, C), F32),
             pltpu.VMEM((R, C), F32),
@@ -891,7 +938,7 @@
             pltpu.VMEM((2, D, C), F32),
             pltpu.VMEM((1, C), F32),
             pltpu.VMEM((1, C), F32),
-            pltpu.SemaphoreType.DMA((4 * N + 3,)),
+            pltpu.SemaphoreType.DMA((7,)),
             pltpu.SemaphoreType.DMA((4 * N + 3,)),
         ],
         compiler_params=pltpu.CompilerParams(vmem_limit_bytes=60 * 2**20),

time: 101 us -> 98 us (0.970)
  Pallas kernels: 99.7 us -> 97 us
    pallas_call x1, Pallas kernels: 95.9 us -> 93.3 us  [shards(): pl.pallas_call(functools.partial(kernel, z, names, kinds), out_shape=outs...]
where the time goes in v6:
time: 98 us; the launch traced here: 97.8 us
  Pallas kernels  97 us (99%)
    pallas_call x1, Pallas kernels, shards(): pl.pallas_call(functools.partial(kernel, z, names, kinds), out_shape=outs...  93.3 us
    pallas_call x1, Pallas kernels, shards(): pl.pallas_call(functools.partial(finish, z), out_shape=(jax.ShapeDtypeStr...  3.69 us

profile of v6, /device:TPU:0, one launch (start us, length us, event | category | flops | bytes accessed | tf_op | source)
XLA Modules:
  0.0 97.8 jit_solution(1606551939192008489)
XLA Ops:
  0.6 93.3 %layer.1 = (bf16[1024,256]{1,0:T(8,128)(2,1)}, bf16[4,256,256]{2,1,0:T(8,128)(2,1)}, bf16[1,256,1024]{2,1,0:T(8,128)(2,1)}, bf16[2,1024,256]{2,1,0:T(8,128)(2,1)}, f32[8,256]{1,0:T(8,128)}, /*index=5*/f32[8,256]{1,0:T(8,128)}) custom-call(bf16[1024,1024]{1,0:T(8,128)(2,1)} %refs_0_.1, bf16[1024,256]{1,0:T(8,128)(2,1)} %refs_1_.1, bf16[256]{0:T(256)(128)(2,1)} %refs_2_.1, ...), custom_call_target="tpu_custom_call" | custom-call | flops 20000000000 | bytes 20000000 | tf_op jit(solution)/shard_map/layer/pallas_call | solution.py:901
  94.0 3.7 %finish.1 = (bf16[1024,256]{1,0:T(8,128)(2,1)}, f32[1024,256]{1,0:T(8,128)}, f32[1024,256]{1,0:T(8,128)}, f32[2,1024,256]{2,1,0:T(8,128)}, f32[1,256]{1,0:T(1,128)}, /*index=5*/f32[1,256]{1,0:T(1,128)}) custom-call(bf16[1024,256]{1,0:T(8,128)(2,1)} %get-tuple-element.18.refs_0_, bf16[4,256,256]{2,1,0:T(8,128)(2,1)} %get-tuple-element.19.refs_1_, ...), custom_call_target="tpu_custom_call" | custom-call | tf_op jit(solution)/shard_map/finish/pallas_call | solution.py:917

commit v7 on v6

--- a/solution.py
+++ b/solution.py
@@ -73,6 +73,7 @@
         code=v(R, 128, I32),
         wts=v(R, 128, F32),
         counts=v(z.blocks, R, CAP, BF16),
+        counts_lo=v(z.blocks, R, CAP, BF16),
         sel=v(W, CAP, R, BF16),
         msg=v(R, D, BF16),
         zacc=v(R, C, F32),
@@ -434,8 +435,10 @@
                 right.append(jnp.where(low_row == row, jnp.ones((), BF16), jnp.zeros((), BF16)))
             outs.append(mm_nt(left, jnp.concatenate(right, axis=1)))
         for h in range(z.blocks):
-            block = [out[h * 8 : h * 8 + 8] for out in outs]
-            g.counts[h, pl.ds(start, 16), :] = jnp.concatenate(block, axis=0).astype(BF16)
+            block = jnp.concatenate([out[h * 8 : h * 8 + 8] for out in outs], axis=0)
+            top = block.astype(BF16)
+            g.counts[h, pl.ds(start, 16), :] = top
+            g.counts_lo[h, pl.ds(start, 16), :] = (block - top.astype(F32)).astype(BF16)
 
     UNROLL = 4
     groups = R // 16 // UNROLL
@@ -555,7 +558,7 @@
         for h in range(z.local):
             part = slice(h * CAP, (h + 1) * CAP)
             block = g.counts[h, rows, :]
-            total += mm(block, g.zhi[part, :]) + mm(block, g.zlo[part, :])
+            total += mm(block, g.zhi[part, :]) + mm(block, g.zlo[part, :]) + mm(g.counts_lo[h, rows, :], g.zhi[part, :])
         g.acc[rows, :] = total
 
     sweep(R // CH, own_part)
@@ -587,7 +590,8 @@
             def add(d, total):
                 s = peer_w(d)
                 block = g.counts[z.local + s, rows, :]
-                return total + mm(block, g.thi[s]) + mm(block, g.tlo[s])
+                rest = g.counts_lo[z.local + s, rows, :]
+                return total + mm(block, g.thi[s]) + mm(block, g.tlo[s]) + mm(rest, g.thi[s])
 
             g.acc[rows, :] = lax.fori_loop(first, last, add, g.acc[rows, :], unroll=W <= 8)
 

time: 98 us -> 98.7 us (level)
  no operation moved by 1% of the time
where the time goes in v7:
time: 98.7 us; the launch traced here: 98.6 us
  Pallas kernels  97.8 us (99%)
    pallas_call x1, Pallas kernels, shards(): pl.pallas_call(functools.partial(kernel, z, names, kinds), out_shape=outs...  94.1 us
    pallas_call x1, Pallas kernels, shards(): pl.pallas_call(functools.partial(finish, z), out_shape=(jax.ShapeDtypeStr...  3.69 us

profile of v7, /device:TPU:0, one launch (start us, length us, event | category | flops | bytes accessed | tf_op | source)
XLA Modules:
  0.0 98.6 jit_solution(5311458976582638428)
XLA Ops:
  0.6 94.1 %layer.1 = (bf16[1024,256]{1,0:T(8,128)(2,1)}, bf16[4,256,256]{2,1,0:T(8,128)(2,1)}, bf16[1,256,1024]{2,1,0:T(8,128)(2,1)}, bf16[2,1024,256]{2,1,0:T(8,128)(2,1)}, f32[8,256]{1,0:T(8,128)}, /*index=5*/f32[8,256]{1,0:T(8,128)}) custom-call(bf16[1024,1024]{1,0:T(8,128)(2,1)} %refs_0_.1, bf16[1024,256]{1,0:T(8,128)(2,1)} %refs_1_.1, bf16[256]{0:T(256)(128)(2,1)} %refs_2_.1, ...), custom_call_target="tpu_custom_call" | custom-call | flops 20000000000 | bytes 20000000 | tf_op jit(solution)/shard_map/layer/pallas_call | solution.py:905
  94.7 3.7 %finish.1 = (bf16[1024,256]{1,0:T(8,128)(2,1)}, f32[1024,256]{1,0:T(8,128)}, f32[1024,256]{1,0:T(8,128)}, f32[2,1024,256]{2,1,0:T(8,128)}, f32[1,256]{1,0:T(1,128)}, /*index=5*/f32[1,256]{1,0:T(1,128)}) custom-call(bf16[1024,256]{1,0:T(8,128)(2,1)} %get-tuple-element.18.refs_0_, bf16[4,256,256]{2,1,0:T(8,128)(2,1)} %get-tuple-element.19.refs_1_, ...), custom_call_target="tpu_custom_call" | custom-call | tf_op jit(solution)/shard_map/finish/pallas_call | solution.py:921

commit v8 on v7

--- a/solution.py
+++ b/solution.py
@@ -845,45 +845,30 @@
         store.wait()
 
 
-def finish(z, *refs):
-    names = ["emb", "gf", "gn", "gc", "gnb", "gcb"]
-    ins = dict(zip(names, refs[:6]))
-    outs = dict(zip(names, refs[6:12]))
-    emb, gf, gn, gc, nb, cb, gf_t, gn_t, gc_t, nb_t, cb_t, load, store = refs[12:]
-    D, C, N, U = z.width, z.cols, z.narrow, z.part
+def finish(z, emb, gf, gn, gc, gnb, gcb, *refs):
+    emb_out, gf_out, gn_out, gc_out, gnb_out, gcb_out, gf_t, gn_t, gc_t, gnb_t, gcb_t, store = refs
+    D, N, U = z.width, z.narrow, z.part
     step = D // N
-    emb_load = pltpu.make_async_copy(ins["emb"], emb, load.at[6])
-    emb_load.start()
-    jobs = [
-        (ins["gn"].at[0], gn, [(gn.at[:, at(i, step)], gn_t.at[at(i, step)], outs["gn"].at[at(i, step)]) for i in range(N)]),
-        (ins["gf"], gf, [(gf.at[i], gf_t.at[at(i, U)], outs["gf"].at[at(i, U)]) for i in range(N)]),
-    ]
-    for p in range(2):
-        parts = [(gc.at[p, at(i, step)], gc_t.at[p, at(i, step)], outs["gc"].at[p, at(i, step)]) for i in range(N)]
-        jobs.append((ins["gc"].at[p], gc.at[p], parts))
-    loads = [pltpu.make_async_copy(src, held, load.at[i]) for i, (src, held, _) in enumerate(jobs)]
-    small = (("gnb", nb, nb_t), ("gcb", cb, cb_t))
-    loads += [pltpu.make_async_copy(ins[k], held, load.at[4 + i]) for i, (k, held, _) in enumerate(small)]
-    for copy in loads:
-        copy.start()
-    stores = [pltpu.make_async_copy(emb, outs["emb"], store.at[0])]
+    stores = []
 
     def keep(src, dst):
         stores.append(pltpu.make_async_copy(src, dst, store.at[len(stores)]))
         stores[-1].start()
 
-    for i, (_, _, parts) in enumerate(jobs):
-        loads[i].wait()
-        for k, (part, turned, out) in enumerate(parts):
-            turned[...] = part[...].astype(F32).T if i == 0 else part[...].astype(F32)
-            keep(turned, out)
-        if i == 0:
-            emb_load.wait()
-            stores[0].start()
-    for i, (k, held, turned) in enumerate(small):
-        loads[4 + i].wait()
-        turned[...] = held[0:1, :]
-        keep(turned, outs[k])
+    keep(emb, emb_out)
+    for i in range(N):
+        rows = at(i, step)
+        for p in range(2):
+            gc_t[p, rows, :] = gc[p, rows, :].astype(F32)
+            keep(gc_t.at[p, rows], gc_out.at[p, rows])
+        gn_t[rows, :] = gn[0, :, rows].astype(F32).T
+        keep(gn_t.at[rows], gn_out.at[rows])
+        gf_t[at(i, U), :] = gf[i].astype(F32)
+        keep(gf_t.at[at(i, U)], gf_out.at[at(i, U)])
+    gnb_t[...] = gnb[0:1, :]
+    gcb_t[...] = gcb[0:1, :]
+    keep(gnb_t, gnb_out)
+    keep(gcb_t, gcb_out)
     for copy in stores:
         copy.wait()
 
@@ -895,12 +880,12 @@
     bufs, sems, kinds = scratch(z)
     names = NAMES_IN + NAMES_OUT + list(bufs) + list(sems)
     outs = (
-        jax.ShapeDtypeStruct((R, C), BF16),
-        jax.ShapeDtypeStruct((N, U, C), BF16),
-        jax.ShapeDtypeStruct((1, C, D), BF16),
-        jax.ShapeDtypeStruct((2, D, C), BF16),
-        jax.ShapeDtypeStruct((8, C), F32),
-        jax.ShapeDtypeStruct((8, C), F32),
+        pltpu.VMEM((R, C), BF16),
+        pltpu.VMEM((N, U, C), BF16),
+        pltpu.VMEM((1, C, D), BF16),
+        pltpu.VMEM((2, D, C), BF16),
+        pltpu.VMEM((8, C), F32),
+        pltpu.VMEM((8, C), F32),
     )
     emb, gf, gn, gc, gnb, gcb = pl.pallas_call(
         functools.partial(kernel, z, names, kinds),
@@ -909,7 +894,7 @@
         out_specs=[pl.BlockSpec(memory_space=pl.ANY)] * len(NAMES_OUT),
         scratch_shapes=list(bufs.values()) + list(sems.values()),
         compiler_params=pltpu.CompilerParams(
-            collective_id=0, has_side_effects=True, vmem_limit_bytes=60 * 2**20
+            collective_id=0, has_side_effects=True, vmem_limit_bytes=56 * 2**20
         ),
         cost_estimate=pl.CostEstimate(flops=2 * 10**10, bytes_accessed=2 * 10**7, transcendentals=0),
         name="layer",
@@ -928,24 +913,17 @@
             jax.ShapeDtypeStruct((1, C), F32),
             jax.ShapeDtypeStruct((1, C), F32),
         ),
-        in_specs=[hbm] * 6,
+        in_specs=[pl.BlockSpec(memory_space=pltpu.VMEM)] * 6,
         out_specs=[hbm] * 6,
         scratch_shapes=[
-            pltpu.VMEM((R, C), BF16),
-            pltpu.VMEM((N, U, C), BF16),
-            pltpu.VMEM((C, D), BF16),
-            pltpu.VMEM((2, D, C), BF16),
-            pltpu.VMEM((8, C), F32),
-            pltpu.VMEM((8, C), F32),
             pltpu.VMEM((R, C), F32),
             pltpu.VMEM((D, C), F32),
             pltpu.VMEM((2, D, C), F32),
             pltpu.VMEM((1, C), F32),
             pltpu.VMEM((1, C), F32),
-            pltpu.SemaphoreType.DMA((7,)),
             pltpu.SemaphoreType.DMA((4 * N + 3,)),
         ],
-        compiler_params=pltpu.CompilerParams(vmem_limit_bytes=60 * 2**20),
+        compiler_params=pltpu.CompilerParams(vmem_limit_bytes=32 * 2**20),
         name="finish",
     )(emb, gf, gn, gc, gnb, gcb)
     return emb, grad_features, grad_neigh, gnb.reshape(C), grad_combine.reshape(2 * D, C), gcb.reshape(C)

time: 98.7 us -> 97.2 us (0.985)
  Pallas kernels: 97.8 us -> 96.3 us
    pallas_call x1, Pallas kernels: 3.69 us -> 2.33 us  [shards(): pl.pallas_call(functools.partial(finish, z), out_shape=(jax.ShapeDtypeStr...]
where the time goes in v8:
time: 97.2 us; the launch traced here: 97.1 us
  Pallas kernels  96.3 us (99%)
    pallas_call x1, Pallas kernels, shards(): pl.pallas_call(functools.partial(kernel, z, names, kinds), out_shape=outs...  94 us
    pallas_call x1, Pallas kernels, shards(): pl.pallas_call(functools.partial(finish, z), out_shape=(jax.ShapeDtypeStr...  2.33 us

profile of v8, /device:TPU:0, one launch (start us, length us, event | category | flops | bytes accessed | tf_op | source)
XLA Modules:
  0.0 97.1 jit_solution(12434699834270102735)
XLA Ops:
  0.6 94.0 %layer.1 = (bf16[1024,256]{1,0:T(8,128)(2,1)S(1)}, bf16[4,256,256]{2,1,0:T(8,128)(2,1)S(1)}, bf16[1,256,1024]{2,1,0:T(8,128)(2,1)S(1)}, bf16[2,1024,256]{2,1,0:T...) custom-call(bf16[1024,1024]{1,0:T(8,128)(2,1)} %refs_0_.1, bf16[1024,256]{1,0:T(8,128)(2,1)} %refs_1_.1, ...), custom_call_target="tpu_custom_call" | custom-call | flops 20000000000 | bytes 20000000 | tf_op jit(solution)/shard_map/layer/pallas_call | solution.py:890
  94.6 2.3 %finish.1 = (bf16[1024,256]{1,0:T(8,128)(2,1)}, f32[1024,256]{1,0:T(8,128)}, f32[1024,256]{1,0:T(8,128)}, f32[2,1024,256]{2,1,0:T(8,128)}, f32[1,256]{1,0:T(1,128)}, /*index=5*/f32[1,256]{1,0:T(1,128)}) custom-call(bf16[1024,256]{1,0:T(8,128)(2,1)S(1)} %get-tuple-element.18.emb, bf16[4,256,256]{2,1,0:T(8,128)(2,1)S(1)} %get-tuple-element.19.gf, ...), custom_call_target="tpu_custom_call" | custom-call | tf_op jit(solution)/shard_map/finish/pallas_call | solution.py:906

commit v9 on v8

--- a/solution.py
+++ b/solution.py
@@ -894,7 +894,7 @@
         out_specs=[pl.BlockSpec(memory_space=pl.ANY)] * len(NAMES_OUT),
         scratch_shapes=list(bufs.values()) + list(sems.values()),
         compiler_params=pltpu.CompilerParams(
-            collective_id=0, has_side_effects=True, vmem_limit_bytes=56 * 2**20
+            collective_id=0, has_side_effects=True, vmem_limit_bytes=58 * 2**20
         ),
         cost_estimate=pl.CostEstimate(flops=2 * 10**10, bytes_accessed=2 * 10**7, transcendentals=0),
         name="layer",

time: 97.2 us -> 97.2 us (level)
  no operation moved by 1% of the time
where the time goes in v9:
time: 97.2 us; the launch traced here: 97.1 us
  Pallas kernels  96.3 us (99%)
    pallas_call x1, Pallas kernels, shards(): pl.pallas_call(functools.partial(kernel, z, names, kinds), out_shape=outs...  94 us
    pallas_call x1, Pallas kernels, shards(): pl.pallas_call(functools.partial(finish, z), out_shape=(jax.ShapeDtypeStr...  2.33 us

profile of v9, /device:TPU:0, one launch (start us, length us, event | category | flops | bytes accessed | tf_op | source)
XLA Modules:
  0.0 97.1 jit_solution(8054668340145443736)
XLA Ops:
  0.6 94.0 %layer.1 = (bf16[1024,256]{1,0:T(8,128)(2,1)S(1)}, bf16[4,256,256]{2,1,0:T(8,128)(2,1)S(1)}, bf16[1,256,1024]{2,1,0:T(8,128)(2,1)S(1)}, bf16[2,1024,256]{2,1,0:T...) custom-call(bf16[1024,1024]{1,0:T(8,128)(2,1)} %refs_0_.1, bf16[1024,256]{1,0:T(8,128)(2,1)} %refs_1_.1, ...), custom_call_target="tpu_custom_call" | custom-call | flops 20000000000 | bytes 20000000 | tf_op jit(solution)/shard_map/layer/pallas_call | solution.py:890
  94.6 2.3 %finish.1 = (bf16[1024,256]{1,0:T(8,128)(2,1)}, f32[1024,256]{1,0:T(8,128)}, f32[1024,256]{1,0:T(8,128)}, f32[2,1024,256]{2,1,0:T(8,128)}, f32[1,256]{1,0:T(1,128)}, /*index=5*/f32[1,256]{1,0:T(1,128)}) custom-call(bf16[1024,256]{1,0:T(8,128)(2,1)S(1)} %get-tuple-element.18.emb, bf16[4,256,256]{2,1,0:T(8,128)(2,1)S(1)} %get-tuple-element.19.gf, ...), custom_call_target="tpu_custom_call" | custom-call | tf_op jit(solution)/shard_map/finish/pallas_call | solution.py:906

commit v10 on v9

--- a/solution.py
+++ b/solution.py
@@ -129,7 +129,7 @@
         gnb_in=v(W, 8, C, F32),
     )
     kinds = dict(
-        sh0=N, sh1=N, sh2=N, sp0=N, sp1=N, sp2=N, sf0=N, sf1=1, sf2=1, nb=1, st=1, ct=1, ac=1, y=1, gh=2, gf=1,
+        sh0=N, sh1=1, sh2=N, sp0=N, sp1=1, sp2=N, sf0=N, sf1=1, sf2=1, nb=1, st=1, ct=1, ac=1, y=1, gh=2, gf=1,
         z=W, zs=1, gr=PARTS, bc=1, bn=1,
     )
     for k in SUMS:
@@ -248,18 +248,16 @@
     def quarter_send(d):
         for h in range(2):
             mine = quarter(h)
-            remote("sh1", d, g.comb_in.at[mine], g.wfull.at[me_n, mine], "narrow", ahead_n(d)).start()
+            remote("sh1", 0, g.comb_in.at[mine], g.wfull.at[me_n, mine], "narrow", ahead_n(d)).start()
 
     def quarter_pass(d):
         s = behind_n(d)
-        arrived("sh1", d, g.wfull.at[s, 0 : 2 * eighth])
         for h in range(2):
             part = g.wfull.at[s, quarter(h)]
-            remote("sp1", d, part, part, "wide", me_w + hops[h] - 2 * hops[h] * hop_bit(h)).start()
+            remote("sp1", 0, part, part, "wide", me_w + hops[h] - 2 * hops[h] * hop_bit(h)).start()
 
     def quarter_forward(d):
         s = behind_n(d)
-        arrived("sp1", d, g.wfull.at[s, 0 : 2 * eighth])
         for h in range(2):
             part = g.wfull.at[s, rows_at(D + h * half + 2 * core * eighth, 2 * eighth)]
             remote("sf1", 0, part, part, "wide", sibling).start()
@@ -602,6 +600,7 @@
         loop(last_d, lambda d: z_copy(d).wait_recv(), first_d)
         sweep(R // CH, pool(first_d, last_d))
     loop(W - 1, lambda d: z_copy(d).wait_recv(), near)
+    arrived("sh1", 0, g.wfull.at[0 : N - 1, 0 : 2 * eighth])
     loop(N, quarter_pass, 1)
     pool_rest = pool(near, W - 1)
 
@@ -701,6 +700,7 @@
         loop(N, lambda d: y_copy(p, d).start(), 1)
 
     take_ret(0)
+    arrived("sp1", 0, g.wfull.at[0 : N - 1, 0 : 2 * eighth])
     loop(N, quarter_forward, 1)
     share_pass(2)
     for p in range(1, PARTS):

time: 97.2 us -> 97.2 us (level)
  no operation moved by 1% of the time
where the time goes in v10:
time: 97.2 us; the launch traced here: 97 us
  Pallas kernels  96.2 us (99%)
    pallas_call x1, Pallas kernels, shards(): pl.pallas_call(functools.partial(kernel, z, names, kinds), out_shape=outs...  93.9 us
    pallas_call x1, Pallas kernels, shards(): pl.pallas_call(functools.partial(finish, z), out_shape=(jax.ShapeDtypeStr...  2.33 us

profile of v10, /device:TPU:0, one launch (start us, length us, event | category | flops | bytes accessed | tf_op | source)
XLA Modules:
  0.0 97.0 jit_solution(17532215355663078191)
XLA Ops:
  0.6 93.9 %layer.1 = (bf16[1024,256]{1,0:T(8,128)(2,1)S(1)}, bf16[4,256,256]{2,1,0:T(8,128)(2,1)S(1)}, bf16[1,256,1024]{2,1,0:T(8,128)(2,1)S(1)}, bf16[2,1024,256]{2,1,0:T...) custom-call(bf16[1024,1024]{1,0:T(8,128)(2,1)} %refs_0_.1, bf16[1024,256]{1,0:T(8,128)(2,1)} %refs_1_.1, ...), custom_call_target="tpu_custom_call" | custom-call | flops 20000000000 | bytes 20000000 | tf_op jit(solution)/shard_map/layer/pallas_call | solution.py:890
  94.5 2.3 %finish.1 = (bf16[1024,256]{1,0:T(8,128)(2,1)}, f32[1024,256]{1,0:T(8,128)}, f32[1024,256]{1,0:T(8,128)}, f32[2,1024,256]{2,1,0:T(8,128)}, f32[1,256]{1,0:T(1,128)}, /*index=5*/f32[1,256]{1,0:T(1,128)}) custom-call(bf16[1024,256]{1,0:T(8,128)(2,1)S(1)} %get-tuple-element.18.emb, bf16[4,256,256]{2,1,0:T(8,128)(2,1)S(1)} %get-tuple-element.19.gf, ...), custom_call_target="tpu_custom_call" | custom-call | tf_op jit(solution)/shard_map/finish/pallas_call | solution.py:906
